TPU v7x, 256 devices: a whole 4x4x8 slice. The times are simulated.
256 devices in a mesh: dp: 32 (over y_hi, z, core), ctx: 8 (over x, y_lo).
Axes of the slice: x: 4, y: 4 (y_hi: 2, y_lo: 2; y = y_hi * 2 + y_lo), z: 8, core: 2. Of those that a mesh axis runs over, the one named last changes fastest.
Arguments:
- query_heads: bfloat16 [32, 1024, 4096], P('dp', 'ctx'), may hold values from -160 to 160
- key_heads: bfloat16 [32, 1024, 512], P('dp', 'ctx'), may hold values from -6 to 6
- value_heads: bfloat16 [32, 1024, 512], P('dp', 'ctx'), may hold values from -6 to 6
- out_grad: bfloat16 [32, 1024, 4096], P('dp', 'ctx'), may hold values from -6 to 6
- layer_inputs: bfloat16 [32, 1024, 8192], P('dp', 'ctx'), may hold values from -6 to 6
- doc_lengths: int32 [32, 8], P('dp'), may hold values from 1 to 512, 1024 in all within a row
Outputs:
- query_grad: bfloat16 [32, 1024, 4096], P('dp', 'ctx')
- key_grad: bfloat16 [32, 1024, 512], P('dp', 'ctx')
- value_grad: bfloat16 [32, 1024, 512], P('dp', 'ctx')
- weight_grad: float32 [8192, 512], P(('dp', 'ctx'))
All inputs are finite; a program needn't handle non-finite values.
Results may differ from a plain program's by a relative error of at most 0.0053.
Values may be sent and summed in bfloat16 or wider, within the bound.
No kernel may reach another device: no remote copies, remote signals or barrier semaphores. Data moves between devices by JAX's collectives and lax.ppermute only.
A program may use at most 128 MiB of HBM per device.

v0:
```python
import jax
import jax.numpy as jnp
from jax import lax
from jax.sharding import PartitionSpec as P

HD = 128
HEADS = 32
KVH = 4


NEG_FILL = -1e30


def document_ids(lengths_row, length):
    endings = jnp.cumsum(lengths_row)
    positions = jnp.arange(length, dtype=jnp.int32)
    return jnp.sum((positions[:, None] >= endings[None, :]).astype(jnp.int32), axis=1)


def shards(query_heads, key_heads, value_heads, out_grad, layer_inputs, doc_lengths):
    queries_here = query_heads[0]
    rows_here = queries_here.shape[0]
    shard_count = lax.axis_size("ctx")
    data_count = lax.axis_size("dp")
    length = rows_here * shard_count
    group_size = HEADS // KVH
    softmax_scale = HD ** (-0.5)
    key_width = key_heads.shape[2]
    key_all, value_all = (
        lax.all_gather(key_heads[0], "ctx", axis=0, tiled=True),
        lax.all_gather(value_heads[0], "ctx", axis=0, tiled=True),
    )
    documents = document_ids(doc_lengths[0], length)
    first_row = lax.axis_index("ctx") * rows_here
    positions = jnp.arange(length, dtype=jnp.int32)
    query_pos = first_row + jnp.arange(rows_here, dtype=jnp.int32)
    query_docs = lax.dynamic_slice_in_dim(documents, first_row, rows_here)
    allowed = (query_docs[:, None] == documents[None, :]) & (
        positions[None, :] <= query_pos[:, None]
    )
    query_split = queries_here.reshape(rows_here, KVH, group_size, HD)
    key_split = key_all.reshape(length, KVH, HD)
    value_split = value_all.reshape(length, KVH, HD)
    grad_split = out_grad[0].reshape(rows_here, KVH, group_size, HD)
    scores = (
        jnp.einsum("igsd,jgd->gsij", query_split, key_split, preferred_element_type=jnp.float32)
        * softmax_scale
    )
    scores = jnp.where(allowed[None, None], scores, NEG_FILL)
    row_top = jnp.max(scores, axis=-1, keepdims=True)
    row_total = jnp.sum(jnp.exp(scores - row_top), axis=-1, keepdims=True)
    probability = jnp.exp(scores - (row_top + jnp.log(row_total)))
    prob_low = probability.astype(jnp.bfloat16)
    attended = jnp.einsum(
        "gsij,jgd->igsd", prob_low, value_split, preferred_element_type=jnp.float32
    )
    delta = jnp.transpose(jnp.sum(grad_split.astype(jnp.float32) * attended, axis=-1), (1, 2, 0))
    dprob = jnp.einsum(
        "igsd,jgd->gsij", grad_split, value_split, preferred_element_type=jnp.float32
    )
    dscore_low = (probability * (dprob - delta[..., None])).astype(jnp.bfloat16)
    query_grad = (
        jnp.einsum("gsij,jgd->igsd", dscore_low, key_split, preferred_element_type=jnp.float32)
        * softmax_scale
    )
    query_grad = query_grad.reshape(rows_here, HEADS * HD).astype(jnp.bfloat16)
    key_term = (
        jnp.einsum("gsij,igsd->jgd", dscore_low, query_split, preferred_element_type=jnp.float32)
        * softmax_scale
    )
    value_term = jnp.einsum(
        "gsij,igsd->jgd", prob_low, grad_split, preferred_element_type=jnp.float32
    )
    summed_grads = lax.psum_scatter(
        jnp.concatenate(
            [
                key_term.reshape(lax.axis_size("ctx") * rows_here, key_width),
                value_term.reshape(lax.axis_size("ctx") * rows_here, key_width),
            ],
            axis=1,
        ),
        "ctx",
        scatter_dimension=0,
        tiled=True,
    )
    key_grad = summed_grads[:, :key_width].astype(jnp.bfloat16)
    value_grad = summed_grads[:, key_width:].astype(jnp.bfloat16)
    inputs_here = layer_inputs[0]
    weight_grad = lax.psum_scatter(
        jnp.einsum("te,tc->ec", inputs_here, value_grad, preferred_element_type=jnp.float32),
        ("dp", "ctx"),
        scatter_dimension=0,
        tiled=True,
    )
    weight_grad = weight_grad * (data_count * length) ** (-0.5)
    return (query_grad[None], key_grad[None], value_grad[None], weight_grad)


def solution(mesh):
    placed = (
        P("dp", "ctx", None),
        P("dp", "ctx", None),
        P("dp", "ctx", None),
        P("dp", "ctx", None),
        P("dp", "ctx", None),
        P("dp", None),
    )
    return jax.shard_map(
        shards,
        mesh=mesh,
        in_specs=placed,
        out_specs=(
            P("dp", "ctx", None),
            P("dp", "ctx", None),
            P("dp", "ctx", None),
            P(("dp", "ctx"), None),
        ),
        check_vma=False,
    )
```

profile of v0, /device:TPU:8, one launch (start us, length us, event | category | flops | bytes accessed | tf_op | source)
XLA Modules:
  0.0 1569.1 jit_solution(6129489574129275259)
XLA Ops:
  7.2 1.8 copy.56
  9.1 0.0 all-gather.7.cloned.1.call-start
  9.1 1.7 copy.59
  10.8 0.0 reduce-scatter.5.cloned.1.call-start
  10.9 0.8 reduce-window.8
  11.7 0.1 convert_reduce_fusion
  11.8 1.6 copy.89
  13.4 2.3 copy.60
  15.7 0.1 dynamic_slice.3
  15.7 0.2 fusion.6
  16.0 40.4 %all-gather.5.cloned.1.call-done = bf16[1,1024,512]{1,2,0:T(8,128)(2,1)} async-done(((bf16[1,128,512]{1,2,0:T(8,128)(2,1)}), bf16[1,1024,512]{1,2,0:T(8,128)(2,1)}) %all-gather.5.cloned.1.call-update) | async-done | bytes 1048592 | tf_op jit(solution)/shard_map/all_gather | solution.py:30
  56.3 8.3 fusion.3
  64.7 9.3 exponential_reduce_fusion
  74.0 11.4 fusion.7
  85.4 20.1 %all-gather.7.cloned.1.call-done = bf16[1,1024,512]{1,2,0:T(8,128)(2,1)} async-done(((bf16[1,128,512]{1,2,0:T(8,128)(2,1)}), bf16[1,1024,512]{1,2,0:T(8,128)(2,1)}) %all-gather.7.cloned.1.call-update) | async-done | bytes 1048592 | tf_op jit(solution)/shard_map/all_gather | solution.py:31
  105.6 10.5 fusion.5
  116.1 9.1 fusion.1
  125.2 3.2 copy-done.1
  128.4 4.2 bitcast_multiply_fusion
  132.6 2.9 copy.68
  135.5 2.9 copy.69
  138.4 4.7 pad_maximum_fusion
  143.2 95.6 %reduce-scatter.5.cloned.1.call-done = f32[128,1024]{1,0:T(8,128)} async-done(((f32[1024,1024]{1,0:T(8,128)}), f32[128,1024]{1,0:T(8,128)}) %reduce-scatter.5.cloned.1.call-update) | async-done | bytes 524304 | tf_op jit(solution)/shard_map/reduce_scatter | solution.py:74
  238.7 1.1 convert.4
  239.8 8.1 convolution_bitcast_fusion
  247.9 17.5 %copy.87 = f32[8192,512]{1,0:T(8,128)} copy(f32[8192,512]{0,1:T(8,128)} %convolution_bitcast_fusion) | data formatting | bytes 33554432
  265.4 5.0 multiply_convert_fusion
  270.4 1.3 copy.70
  271.7 0.7 slice_bitcast_fusion.1
  272.5 1288.4 %reduce-scatter.7.cloned.1.call-done = f32[32,512]{1,0:T(8,128)} async-done(((f32[8192,512]{1,0:T(8,128)}), f32[32,512]{1,0:T(8,128)}) %reduce-scatter.7.cloned.1.call-update) | async-done | bytes 65552
  1560.9 1.0 copy.88
  1561.9 0.7 copy.71
  (16 shorter events, 0.2 us)
Async XLA Ops:
  7.2 232.7 %copy-start = (bf16[1,128,8192]{2,1,0:T(8,128)(2,1)S(1)}, bf16[1,128,8192]{2,1,0:T(8,128)(2,1)}, u32[]{:S(2)}) copy-start(bf16[1,128,8192]{2,1,0:T(8,128)(2,1)} %param.10) | copy-start | bytes 6291460
  7.2 49.2 %all-gather.5.cloned.1.call-start = ((), (), s32[]{:S(2)}) async-start(), calls=%async_computation.3 | async-start | bytes 1179648 | tf_op jit(solution)/shard_map/all_gather | solution.py:30
  9.1 96.5 %all-gather.7.cloned.1.call-start = ((), (), s32[]{:S(2)}) async-start(), calls=%async_computation.4 | async-start | bytes 1179648 | tf_op jit(solution)/shard_map/all_gather | solution.py:31
  10.8 227.9 %reduce-scatter.5.cloned.1.call-start = ((), (), s32[]{:S(2)}) async-start(), calls=%async_computation.2 | async-start | bytes 4718592 | tf_op jit(solution)/shard_map/reduce_scatter | solution.py:74
  105.6 10.5 copy-start.2
  105.6 10.5 copy-start.3
  125.2 3.2 copy-start.1
  143.1 1417.7 %reduce-scatter.7.cloned.1.call-start = ((), (), s32[]{:S(2)}) async-start(), calls=%async_computation.5 | async-start | bytes 16842752
Sparse Core Ops, SparseCore 0:
  10.3 45.9 all-gather.4
  58.6 46.8 all-gather.6
  143.3 95.4 reduce-scatter.4
  265.5 1295.2 reduce-scatter.6
where the time goes:
time: 1570 us
  waiting for transfers between devices  1440 us (92%)
  matrix products  56.7 us (4%)
  local copies, waits for them, and re-layouts  37.7 us (2%)
  other arithmetic  16.2 us (1%)
    unnamed x5, waiting for transfers between devices  1290 us
    reduce_scatter x1, waiting for transfers between devices, shards(): lax.psum_scatter(jnp.concatenate([key_term.reshape(lax.axis_size('ctx') *...  95.6 us
    all_gather x1, waiting for transfers between devices, shards(): lax.all_gather(key_heads[0], 'ctx', axis=0, tiled=True)  40.4 us
  transfers between devices with their start and end apart: 4, of which 4 were waited for; matrix products, arithmetic and copies ran while one was open for 3% of the time, Pallas kernels for 0%

commit v1 on v0

v1 whole, which is shorter than its diff:
```python
import math

import jax
import jax.numpy as jnp
from jax import lax
from jax.experimental import pallas as pl
from jax.experimental.pallas import tpu as pltpu
from jax.sharding import PartitionSpec as P

HD = 128
GROUPS = 4
GROUP = 8
ROWS = 128
NEAR = 4
SCALE = HD**-0.5
SCALE_LOG2 = SCALE * math.log2(math.e)
NEG_FILL = -1e30
F32 = jnp.float32
BF16 = jnp.bfloat16


def params(mib):
    return pltpu.CompilerParams(vmem_limit_bytes=mib * 2**20)


def dot(a, b, contract):
    return lax.dot_general(a, b, ((contract[:1], contract[1:]), ((), ())), preferred_element_type=F32)


def fill_bias(lengths, bias):
    first = lax.axis_index("ctx") * ROWS
    query = lax.broadcasted_iota(jnp.int32, (ROWS, 2 * ROWS), 1) % ROWS
    key = lax.broadcasted_iota(jnp.int32, (ROWS, 2 * ROWS), 0)
    start = jnp.zeros_like(query)
    ending = jnp.int32(0)
    for n in range(lengths.shape[1]):
        ending = ending + lengths[0, n]
        start = jnp.where(ending <= query + first, ending, start)
    for block in range(NEAR):
        place = key + (first - block * ROWS)
        if block == 0:
            place = jnp.where(key <= query, place, place - NEAR * ROWS)
        bias[block * ROWS : (block + 1) * ROWS, :] = jnp.where(place >= start, 0.0, NEG_FILL)


def lower():
    query = lax.broadcasted_iota(jnp.int32, (ROWS, 2 * ROWS), 1) % ROWS
    key = lax.broadcasted_iota(jnp.int32, (ROWS, 2 * ROWS), 0)
    return key <= query


def fold(tile, mask):
    return jnp.concatenate(
        [jnp.where(mask, tile[:ROWS], tile[NEAR * ROWS :]), tile[ROWS : NEAR * ROWS]], axis=0
    )


def unfold(tile, mask):
    return jnp.concatenate(
        [
            jnp.where(mask, tile[:ROWS], 0.0).astype(BF16),
            tile[ROWS:].astype(BF16),
            jnp.where(mask, 0.0, tile[:ROWS]).astype(BF16),
        ],
        axis=0,
    )


def heads(ref, first, count):
    return jnp.concatenate([ref[:, (first + n) * HD : (first + n + 1) * HD] for n in range(count)], axis=0)


def value_kernel(lengths, q, do, k0, k1, k2, k3, k4, own, s1, s2, s3, s4, stats, bias, prob):
    @pl.when(pl.program_id(0) == 0)
    def _():
        fill_bias(lengths, bias)

    mask = lower()
    keys = jnp.concatenate([ref[...] for ref in (k0, k1, k2, k3, k4)], axis=0)
    for pair in range(GROUP // 2):
        lanes = slice(pair * 256, (pair + 1) * 256)
        scores = fold(dot(keys, heads(q, 2 * pair, 2), (1, 1)), mask) + bias[...]
        top = jnp.max(scores, axis=0, keepdims=True)
        weight = jnp.exp2((scores - top) * SCALE_LOG2)
        inverse = 1.0 / jnp.sum(weight, axis=0, keepdims=True)
        prob[:, lanes] = unfold(weight * inverse, mask)
        stats[0, 0:1, lanes] = top
        stats[0, 1:2, lanes] = inverse
    grad = dot(prob[...], heads(do, 0, GROUP), (1, 0))
    own[...] = grad[:ROWS]
    for n, ref in enumerate((s1, s2, s3, s4)):
        ref[...] = grad[(n + 1) * ROWS : (n + 2) * ROWS].astype(BF16)


def score_kernel(
    lengths, q, do, k0, k1, k2, k3, k4, v0, v1, v2, v3, v4, stats, dq, own, s1, s2, s3, s4, bias, dsc
):
    @pl.when(pl.program_id(0) == 0)
    def _():
        fill_bias(lengths, bias)

    mask = lower()
    keys = jnp.concatenate([ref[...] for ref in (k0, k1, k2, k3, k4)], axis=0)
    values = jnp.concatenate([ref[...] for ref in (v0, v1, v2, v3, v4)], axis=0)
    keys_t = jnp.concatenate([ref[...].T for ref in (k0, k1, k2, k3, k4)], axis=1)
    for pair in range(GROUP // 2):
        lanes = slice(pair * 256, (pair + 1) * 256)
        top, inverse = stats[0, 0:1, lanes], stats[0, 1:2, lanes]
        scores = fold(dot(keys, heads(q, 2 * pair, 2), (1, 1)), mask) + bias[...]
        probability = jnp.exp2((scores - top) * SCALE_LOG2) * inverse
        dprob = fold(dot(values, heads(do, 2 * pair, 2), (1, 1)), mask)
        delta = jnp.sum(probability.astype(BF16).astype(F32) * dprob, axis=0, keepdims=True)
        low = unfold(probability * (dprob - delta), mask)
        dsc[:, lanes] = low
        dq_t = dot(keys_t, low, (1, 0)) * SCALE
        for n in range(2):
            cols = slice((2 * pair + n) * HD, (2 * pair + n + 1) * HD)
            dq[:, cols] = dq_t[:, n * HD : (n + 1) * HD].T.astype(BF16)
    grad = dot(dsc[...], heads(q, 0, GROUP), (1, 0)) * SCALE
    own[...] = grad[:ROWS]
    for n, ref in enumerate((s1, s2, s3, s4)):
        ref[...] = grad[(n + 1) * ROWS : (n + 2) * ROWS].astype(BF16)


def group_spec(width):
    return pl.BlockSpec((ROWS, width), lambda g: (0, g))


def whole_spec(shape):
    return pl.BlockSpec(shape, lambda *_: (0,) * len(shape))


STATS_SPEC = pl.BlockSpec((1, 8, GROUP * ROWS), lambda g: (g, 0, 0))
SMEM = pl.BlockSpec(memory_space=pltpu.SMEM)


def sds(shape, dtype):
    return jax.ShapeDtypeStruct(shape, dtype)


def value_call(lengths, q, do, keys):
    key_spec = group_spec(HD)
    width = GROUPS * HD
    return pl.pallas_call(
        value_kernel,
        grid=(GROUPS,),
        in_specs=[SMEM, group_spec(GROUP * HD), group_spec(GROUP * HD)] + [key_spec] * 5,
        out_specs=[key_spec] * 5 + [STATS_SPEC],
        out_shape=[sds((ROWS, width), F32)]
        + [sds((ROWS, width), BF16)] * NEAR
        + [sds((GROUPS, 8, GROUP * ROWS), F32)],
        scratch_shapes=[
            pltpu.VMEM((NEAR * ROWS, 2 * ROWS), F32),
            pltpu.VMEM((5 * ROWS, GROUP * ROWS), BF16),
        ],
        compiler_params=params(32),
        cost_estimate=pl.CostEstimate(flops=10**10, bytes_accessed=4 * 10**6, transcendentals=2 * 10**6),
        name="value_grad",
    )(lengths, q, do, *keys)


def score_call(lengths, q, do, keys, values, stats):
    key_spec = group_spec(HD)
    width = GROUPS * HD
    return pl.pallas_call(
        score_kernel,
        grid=(GROUPS,),
        in_specs=[SMEM, group_spec(GROUP * HD), group_spec(GROUP * HD)] + [key_spec] * 10 + [STATS_SPEC],
        out_specs=[group_spec(GROUP * HD)] + [key_spec] * 5,
        out_shape=[sds((ROWS, GROUPS * GROUP * HD), BF16), sds((ROWS, width), F32)]
        + [sds((ROWS, width), BF16)] * NEAR,
        scratch_shapes=[
            pltpu.VMEM((NEAR * ROWS, 2 * ROWS), F32),
            pltpu.VMEM((5 * ROWS, GROUP * ROWS), BF16),
        ],
        compiler_params=params(32),
        cost_estimate=pl.CostEstimate(flops=10**10, bytes_accessed=4 * 10**6, transcendentals=2 * 10**6),
        name="score_grad",
    )(lengths, q, do, *keys, *values, stats)


def deal_kernel(x, *refs):
    outs, pick = refs[:8], refs[8]
    dp, ctx = lax.axis_index("dp"), lax.axis_index("ctx")
    core, high = dp % 2, dp // 16

    @pl.when(pl.program_id(0) == 0)
    def _():
        row = lax.broadcasted_iota(jnp.int32, (1024, 1024), 0)
        col = lax.broadcasted_iota(jnp.int32, (1024, 1024), 1)
        to, far, pair, n = row // 128, (row // 64) % 2, (row // 32) % 2, row % 32
        source = (pair * 2 + (far ^ core)) * 256 + ((to + ctx) % 8) * 32 + n
        pick[...] = jnp.where(col == source, 1.0, 0.0).astype(BF16)

    step = pl.program_id(0)
    dealt = dot(pick[...], x[...], (1, 1)).astype(BF16)
    for to in range(8):
        outs[to][0] = dealt[to * 128 : to * 128 + 64]
        outs[to][1] = dealt[to * 128 + 64 : to * 128 + 128]


def deal_call(x):
    def source(step):
        return (0, step ^ (4 * (lax.axis_index("dp") // 16)))

    return pl.pallas_call(
        deal_kernel,
        grid=(8,),
        in_specs=[pl.BlockSpec((ROWS, 1024), source)],
        out_specs=[pl.BlockSpec((2, 64, ROWS), lambda step: (0, step, 0))] * 8,
        out_shape=[sds((2, 512, ROWS), BF16)] * 8,
        scratch_shapes=[pltpu.VMEM((1024, 1024), BF16)],
        compiler_params=params(24),
        cost_estimate=pl.CostEstimate(flops=2 * 10**9, bytes_accessed=4 * 10**6, transcendentals=0),
        name="deal_inputs",
    )(x)


def weight_kernel(*refs):
    inputs, grads, out = refs[:8], refs[8:16], refs[16]
    left = jnp.concatenate([ref[0] for ref in inputs], axis=1)
    right = jnp.concatenate([ref[...] for ref in grads], axis=0)
    out[...] = dot(left, right, (1, 0)).astype(out.dtype)


def weight_call(half, inputs, grads, dtype):
    width = grads[0].shape[1]
    return pl.pallas_call(
        weight_kernel,
        grid=(2,),
        in_specs=[pl.BlockSpec((1, 256, ROWS), lambda n: (half, n, 0))] * 8 + [whole_spec((ROWS, width))] * 8,
        out_specs=pl.BlockSpec((256, width), lambda n: (n, 0)),
        out_shape=sds((512, width), dtype),
        compiler_params=params(24),
        cost_estimate=pl.CostEstimate(flops=6 * 10**8, bytes_accessed=3 * 10**6, transcendentals=0),
        name="weight_grad",
    )(*inputs, *grads)


def send(array, axis, target, count):
    return lax.ppermute(array, axis, [(n, target(n)) for n in range(count)])


def ring(array, distance):
    return send(array, "ctx", lambda n: (n + distance) % 8, 8)


def after(array, *others):
    return lax.optimization_barrier((array, *others))[0]


def shards(query_heads, key_heads, value_heads, out_grad, layer_inputs, doc_lengths):
    q, do = query_heads[0], out_grad[0]
    key, value = key_heads[0], value_heads[0]
    tokens = lax.axis_size("dp") * lax.axis_size("ctx") * q.shape[0]
    keys = [key] + [ring(key, d) for d in range(1, 5)]
    dealt = deal_call(layer_inputs[0])
    values = [value] + [ring(value, d) for d in range(1, 5)]
    inputs = [dealt[0]] + [ring(dealt[d], d) for d in range(1, 8)]

    *value_terms, stats = value_call(doc_lengths, q, do, keys)
    arrived = [ring(term, -d) for d, term in enumerate(value_terms[1:], 1)]
    value_grad = (value_terms[0] + sum(term.astype(F32) for term in arrived)).astype(BF16)
    query_grad, *key_terms = score_call(doc_lengths, q, do, keys, values, stats)

    grads = [value_grad] + [ring(value_grad, d) for d in range(1, 8)]
    away = weight_call(1, inputs, grads, BF16)
    other_core = send(away, "dp", lambda n: n ^ 1, 32)
    here = weight_call(0, inputs, grads, F32)
    total = here + other_core.astype(F32)
    other_high = send(total[256:].astype(BF16), "dp", lambda n: n ^ 16, 32)
    total = total[:256] + other_high.astype(F32)
    rings = [[high * 16 + 2 * z + core for z in range(8)] for high in range(2) for core in range(2)]
    parts = lax.all_to_all(total.astype(BF16).reshape(8, 32, -1), "dp", 0, 0, axis_index_groups=rings)
    weight_grad = jnp.sum(parts.astype(F32), axis=0) * tokens**-0.5

    arrived = [ring(term, -d) for d, term in enumerate(key_terms[1:], 1)]
    key_grad = (key_terms[0] + sum(term.astype(F32) for term in arrived)).astype(BF16)
    return query_grad[None], key_grad[None], value_grad[None], weight_grad


def solution(mesh):
    split = P("dp", "ctx", None)
    return jax.shard_map(
        shards,
        mesh=mesh,
        in_specs=(split,) * 5 + (P("dp", None),),
        out_specs=(split, split, split, P(("dp", "ctx"), None)),
        check_vma=False,
    )
```

time: 1570 us -> 147 us (0.09)
  waiting for transfers between devices: 1440 us -> 58.3 us
  matrix products: 56.7 us -> 0 us
  starting transfers between devices: 0.16 us -> 50.6 us
  local copies, waits for them, and re-layouts: 37.7 us -> 4.08 us
  Pallas kernels: 0 us -> 28 us
    unnamed x5 -> x0, waiting for transfers between devices: 1290 us -> none
    reduce_scatter x1 -> x0, waiting for transfers between devices: 95.6 us -> none  [shards(): lax.psum_scatter(jnp.concatenate([key_term.reshape(lax.axis_size('ctx') *...]
    all_gather x2 -> x0, waiting for transfers between devices: 60.5 us -> none  [the longest x1 40.4 us: shards(): lax.all_gather(key_heads[0], 'ctx', axis=0, tiled=True)]
    ppermute x0 -> x32, waiting for transfers between devices: none -> 58.3 us  [send(): return lax.ppermute(array, axis, [(n, target(n)) for n in range(count)])]
    dot_general x7 -> x0, matrix products: 56.7 us -> none  [the longest x1 11.4 us: shards(): jnp.einsum('gsij,igsd->jgd', prob_low, grad_split, preferred_element_type...]
    ppermute x0 -> x32, starting transfers between devices: none -> 41.3 us  [send(): return lax.ppermute(array, axis, [(n, target(n)) for n in range(count)])]
    pallas_call x0 -> x5, Pallas kernels: none -> 28 us  [the longest x1 12.6 us: score_call(): pl.pallas_call(score_kernel, grid=(GROUPS,), in_specs=[SMEM, group_spec(G...]
    unnamed x15 -> x22, local copies, waits for them, and re-layouts: 29.4 us -> 4.05 us
  transfers between devices with their start and end apart: 4 -> 33, of which waited for: 4 -> 15; matrix products, arithmetic and copies ran while one was open for 3% -> 1% of each run, Pallas kernels for 0% -> 14%
where the time goes in v1:
time: 147 us; the launch traced here: 145 us
  waiting for transfers between devices  58.3 us (40%)
  starting transfers between devices  50.6 us (34%)
  Pallas kernels  28 us (19%)
  local copies, waits for them, and re-layouts  4.08 us (3%)
  other arithmetic  3.39 us (2%)
    ppermute x32, waiting for transfers between devices, send(): return lax.ppermute(array, axis, [(n, target(n)) for n in range(count)])  58.3 us
    ppermute x32, starting transfers between devices, send(): return lax.ppermute(array, axis, [(n, target(n)) for n in range(count)])  41.3 us
    pallas_call x1, Pallas kernels, score_call(): pl.pallas_call(score_kernel, grid=(GROUPS,), in_specs=[SMEM, group_spec(G...  12.6 us
    all_to_all x1, starting transfers between devices, shards(): lax.all_to_all(total.astype(BF16).reshape(8, 32, -1), 'dp', 0, 0, axis_in...  9.3 us
    pallas_call x1, Pallas kernels, deal_call(): pl.pallas_call(deal_kernel, grid=(8,), in_specs=[pl.BlockSpec((ROWS, 1024...  7.37 us
    pallas_call x1, Pallas kernels, value_call(): pl.pallas_call(value_kernel, grid=(GROUPS,), in_specs=[SMEM, group_spec(G...  6.3 us
    unnamed x22, local copies, waits for them, and re-layouts  4.05 us
  transfers between devices with their start and end apart: 33, of which 15 were waited for; matrix products, arithmetic and copies ran while one was open for 1% of the time, Pallas kernels for 14%

profile of v1, /device:TPU:8, one launch (start us, length us, event | category | flops | bytes accessed | tf_op | source)
XLA Modules:
  0.0 145.3 jit_solution(10690491967729029091)
XLA Ops:
  0.6 1.5 %collective-permute-start = (bf16[128,512]{1,0:T(8,128)(2,1)}, bf16[128,512]{1,0:T(8,128)(2,1)S(1)}, u32[]{:S(2)}, u32[]{:S(2)}) collective-permute-start(bf16[128,512]{1,0:T(8,128)(2,1)} %bitcast.16), channel_id=1, source_target_pairs={{0,1},{1,2},{2,3},{3,4},{4,5},{5,6},{6,7},{7,0},{8,9},{9,10},{10,1... | collective-permute-start | bytes 393224 | tf_op jit(solution)/shard_map/ppermute | solution.py:241
  2.1 1.5 %collective-permute-start.1 = (bf16[128,512]{1,0:T(8,128)(2,1)}, bf16[128,512]{1,0:T(8,128)(2,1)S(1)}, u32[]{:S(2)}, u32[]{:S(2)}) collective-permute-start(bf16[128,512]{1,0:T(8,128)(2,1)} %bitcast.17), channel_id=1, source_target_pairs={{0,2},{1,3},{2,4},{3,5},{4,6},{5,7},{6,0},{7,1},{8,10},{9,11},{10,... | collective-permute-start | bytes 393224 | tf_op jit(solution)/shard_map/ppermute | solution.py:241
  3.6 2.8 %collective-permute-start.2 = (bf16[128,512]{1,0:T(8,128)(2,1)}, bf16[128,512]{1,0:T(8,128)(2,1)S(1)}, u32[]{:S(2)}, u32[]{:S(2)}) collective-permute-start(bf16[128,512]{1,0:T(8,128)(2,1)} %bitcast.18), channel_id=1, source_target_pairs={{0,3},{1,4},{2,5},{3,6},{4,7},{5,0},{6,1},{7,2},{8,11},{9,12},{10,... | collective-permute-start | bytes 393224 | tf_op jit(solution)/shard_map/ppermute | solution.py:241
  7.2 3.1 %collective-permute-done.1.k2 = bf16[128,512]{1,0:T(8,128)(2,1)S(1)} collective-permute-done((bf16[128,512]{1,0:T(8,128)(2,1)}, bf16[128,512]{1,0:T(8,128)(2,1)S(1)}, u32[]{:S(2)}, u32[]{:S(2)}) %collective-permute-start.1) | collective-permute-done | bytes 131104 | tf_op jit(solution)/shard_map/ppermute | solution.py:241
  10.3 2.0 %collective-permute-done.2.k3 = bf16[128,512]{1,0:T(8,128)(2,1)S(1)} collective-permute-done((bf16[128,512]{1,0:T(8,128)(2,1)}, bf16[128,512]{1,0:T(8,128)(2,1)S(1)}, u32[]{:S(2)}, u32[]{:S(2)}) %collective-permute-start.2) | collective-permute-done | bytes 131104 | tf_op jit(solution)/shard_map/ppermute | solution.py:241
  12.4 4.3 %collective-permute-done.3.k4 = bf16[128,512]{1,0:T(8,128)(2,1)S(1)} collective-permute-done((bf16[128,512]{1,0:T(8,128)(2,1)}, bf16[128,512]{1,0:T(8,128)(2,1)S(1)}, u32[]{:S(2)}, u32[]{:S(2)}) %collective-permute-start.3) | collective-permute-done | bytes 131104 | tf_op jit(solution)/shard_map/ppermute | solution.py:241
  20.7 6.3 %value_grad.1 = (f32[128,512]{1,0:T(8,128)S(1)}, bf16[128,512]{1,0:T(8,128)(2,1)S(1)}, bf16[128,512]{1,0:T(8,128)(2,1)S(1)}, bf16[128,512]{1,0:T(8,128)(2,1)S(1)...) custom-call(s32[1,8]{1,0:T(1,128)S(1)} %copy-done.9, bf16[128,4096]{1,0:T(8,128)(2,1)S(1)} %bitcast.12, ...), custom_call_target="tpu_custom_call" | custom-call | flops 10000000000 | bytes 4000000 | tf_op jit(solution)/shard_map/value_grad/pallas_call | solution.py:144
  27.1 7.4 %deal_inputs.1 = (bf16[2,512,128]{2,1,0:T(8,128)(2,1)S(1)}, bf16[2,512,128]{2,1,0:T(8,128)(2,1)S(1)}, bf16[2,512,128]{2,1,0:T(8,128)(2,1)S(1)}, bf16[2,512,128]{...) custom-call(bf16[128,8192]{1,0:T(8,128)(2,1)S(1)} %bitcast.11), custom_call_target="tpu_custom_call" | custom-call | flops 2000000000 | bytes 4000000 | tf_op jit(solution)/shard_map/deal_inputs/pallas_call | solution.py:206
  34.5 2.9 %collective-permute-start.16 = (bf16[2,512,128]{2,1,0:T(8,128)(2,1)S(1)}, bf16[2,512,128]{2,1,0:T(8,128)(2,1)S(1)}, u32[]{:S(2)}, u32[]{:S(2)}) collective-permute-start(bf16[2,512,128]{2,1,0:T(8,128)(2,1)S(1)} %get-tuple-element.37), channel_id=1, source_target_pairs={{0,1},{1,2},{2,3},{3,4},{4,5},{5,6},{6,7},{7,0},{8,9},{9,10},{10,1... | collective-permute-start | bytes 786440 | tf_op jit(solution)/shard_map/ppermute | solution.py:241
  37.4 3.2 %collective-permute-start.13 = (bf16[128,512]{1,0:T(8,128)(2,1)S(1)}, bf16[128,512]{1,0:T(8,128)(2,1)S(1)}, u32[]{:S(2)}, u32[]{:S(2)}) collective-permute-start(bf16[128,512]{1,0:T(8,128)(2,1)S(1)} %get-tuple-element.33), channel_id=1, source_target_pairs={{0,6},{1,7},{2,0},{3,1},{4,2},{5,3},{6,4},{7,5},{8,14},{9,15},{10,... | collective-permute-start | bytes 393224 | tf_op jit(solution)/shard_map/ppermute | solution.py:241
  41.6 3.6 %collective-permute-done.13 = bf16[128,512]{1,0:T(8,128)(2,1)S(1)} collective-permute-done((bf16[128,512]{1,0:T(8,128)(2,1)S(1)}, bf16[128,512]{1,0:T(8,128)(2,1)S(1)}, u32[]{:S(2)}, u32[]{:S(2)}) %collective-permute-start.13) | collective-permute-done | bytes 131104 | tf_op jit(solution)/shard_map/ppermute | solution.py:241
  45.2 10.1 %collective-permute-done.14 = bf16[128,512]{1,0:T(8,128)(2,1)S(1)} collective-permute-done((bf16[128,512]{1,0:T(8,128)(2,1)S(1)}, bf16[128,512]{1,0:T(8,128)(2,1)S(1)}, u32[]{:S(2)}, u32[]{:S(2)}) %collective-permute-start.14) | collective-permute-done | bytes 131104 | tf_op jit(solution)/shard_map/ppermute | solution.py:241
  55.2 5.1 %collective-permute-start.20 = (bf16[2,512,128]{2,1,0:T(8,128)(2,1)S(1)}, bf16[2,512,128]{2,1,0:T(8,128)(2,1)S(1)}, u32[]{:S(2)}, u32[]{:S(2)}) collective-permute-start(bf16[2,512,128]{2,1,0:T(8,128)(2,1)S(1)} %get-tuple-element.41), channel_id=1, source_target_pairs={{0,5},{1,6},{2,7},{3,0},{4,1},{5,2},{6,3},{7,4},{8,13},{9,14},{10,... | collective-permute-start | bytes 786440 | tf_op jit(solution)/shard_map/ppermute | solution.py:241
  61.3 2.2 %collective-permute-start.23 = (bf16[128,512]{1,0:T(8,128)(2,1)S(1)}, bf16[128,512]{1,0:T(8,128)(2,1)S(1)}, u32[]{:S(2)}, u32[]{:S(2)}) collective-permute-start(bf16[128,512]{1,0:T(8,128)(2,1)S(1)} %add_convert_fusion.refs_8_), channel_id=1, source_target_pairs={{0,1},{1,2},{2,3},{3,4},{4,5},{5,6},{6,7},{7,0},{8,9},{9,10},{10,1... | collective-permute-start | bytes 393224 | tf_op jit(solution)/shard_map/ppermute | solution.py:241
  65.5 4.7 %collective-permute-done.20.refs_5_ = bf16[2,512,128]{2,1,0:T(8,128)(2,1)S(1)} collective-permute-done((bf16[2,512,128]{2,1,0:T(8,128)(2,1)S(1)}, bf16[2,512,128]{2,1,0:T(8,128)(2,1)S(1)}, u32[]{:S(2)}, u32[]{:S(2)}) %collective-permute-start.20) | collective-permute-done | bytes 262176 | tf_op jit(solution)/shard_map/ppermute | solution.py:241
  70.2 3.5 %collective-permute-done.21.refs_6_ = bf16[2,512,128]{2,1,0:T(8,128)(2,1)S(1)} collective-permute-done((bf16[2,512,128]{2,1,0:T(8,128)(2,1)S(1)}, bf16[2,512,128]{2,1,0:T(8,128)(2,1)S(1)}, u32[]{:S(2)}, u32[]{:S(2)}) %collective-permute-start.21) | collective-permute-done | bytes 262176 | tf_op jit(solution)/shard_map/ppermute | solution.py:241
  74.2 5.1 %collective-permute-done.22.refs_7_ = bf16[2,512,128]{2,1,0:T(8,128)(2,1)S(1)} collective-permute-done((bf16[2,512,128]{2,1,0:T(8,128)(2,1)S(1)}, bf16[2,512,128]{2,1,0:T(8,128)(2,1)S(1)}, u32[]{:S(2)}, u32[]{:S(2)}) %collective-permute-start.22) | collective-permute-done | bytes 262176 | tf_op jit(solution)/shard_map/ppermute | solution.py:241
  79.3 1.6 %collective-permute-start.28 = (bf16[128,512]{1,0:T(8,128)(2,1)S(1)}, bf16[128,512]{1,0:T(8,128)(2,1)S(1)}, u32[]{:S(2)}, u32[]{:S(2)}) collective-permute-start(bf16[128,512]{1,0:T(8,128)(2,1)S(1)} %add_convert_fusion.refs_8_), channel_id=1, source_target_pairs={{0,6},{1,7},{2,0},{3,1},{4,2},{5,3},{6,4},{7,5},{8,14},{9,15},{10,... | collective-permute-start | bytes 393224 | tf_op jit(solution)/shard_map/ppermute | solution.py:241
  80.9 1.5 %collective-permute-start.29 = (bf16[128,512]{1,0:T(8,128)(2,1)S(1)}, bf16[128,512]{1,0:T(8,128)(2,1)S(1)}, u32[]{:S(2)}, u32[]{:S(2)}) collective-permute-start(bf16[128,512]{1,0:T(8,128)(2,1)S(1)} %add_convert_fusion.refs_8_), channel_id=1, source_target_pairs={{0,7},{1,0},{2,1},{3,2},{4,3},{5,4},{6,5},{7,6},{8,15},{9,8},{10,9... | collective-permute-start | bytes 393224 | tf_op jit(solution)/shard_map/ppermute | solution.py:241
  82.4 4.2 %collective-permute-done.27.refs_13_ = bf16[128,512]{1,0:T(8,128)(2,1)S(1)} collective-permute-done((bf16[128,512]{1,0:T(8,128)(2,1)S(1)}, bf16[128,512]{1,0:T(8,128)(2,1)S(1)}, u32[]{:S(2)}, u32[]{:S(2)}) %collective-permute-start.27) | collective-permute-done | bytes 131104 | tf_op jit(solution)/shard_map/ppermute | solution.py:241
  86.7 1.8 %collective-permute-done.29.refs_15_ = bf16[128,512]{1,0:T(8,128)(2,1)S(1)} collective-permute-done((bf16[128,512]{1,0:T(8,128)(2,1)S(1)}, bf16[128,512]{1,0:T(8,128)(2,1)S(1)}, u32[]{:S(2)}, u32[]{:S(2)}) %collective-permute-start.29) | collective-permute-done | bytes 131104 | tf_op jit(solution)/shard_map/ppermute | solution.py:241
  91.5 2.7 %collective-permute-start.31 = (bf16[256,512]{1,0:T(8,128)(2,1)S(1)}, bf16[256,512]{1,0:T(8,128)(2,1)S(1)}, u32[]{:S(2)}, u32[]{:S(2)}) collective-permute-start(bf16[256,512]{1,0:T(8,128)(2,1)S(1)} %slice.15), channel_id=1, source_target_pairs={{0,128},{8,136},{16,144},{24,152},{32,160},{40,168},{48,176},{56,1... | collective-permute-start | bytes 786440 | tf_op jit(solution)/shard_map/ppermute | solution.py:241
  94.4 1.7 %collective-permute-start.5 = (bf16[128,512]{1,0:T(8,128)(2,1)S(1)}, bf16[128,512]{1,0:T(8,128)(2,1)S(1)}, u32[]{:S(2)}, u32[]{:S(2)}) collective-permute-start(bf16[128,512]{1,0:T(8,128)(2,1)S(1)} %bitcast.23), channel_id=1, source_target_pairs={{0,2},{1,3},{2,4},{3,5},{4,6},{5,7},{6,0},{7,1},{8,10},{9,11},{10,... | collective-permute-start | bytes 393224 | tf_op jit(solution)/shard_map/ppermute | solution.py:241
  96.0 3.5 %collective-permute-start.6 = (bf16[128,512]{1,0:T(8,128)(2,1)S(1)}, bf16[128,512]{1,0:T(8,128)(2,1)S(1)}, u32[]{:S(2)}, u32[]{:S(2)}) collective-permute-start(bf16[128,512]{1,0:T(8,128)(2,1)S(1)} %bitcast.24), channel_id=1, source_target_pairs={{0,3},{1,4},{2,5},{3,6},{4,7},{5,0},{6,1},{7,2},{8,11},{9,12},{10,... | collective-permute-start | bytes 393224 | tf_op jit(solution)/shard_map/ppermute | solution.py:241
  99.8 7.3 %collective-permute-done.31 = bf16[256,512]{1,0:T(8,128)(2,1)S(1)} collective-permute-done((bf16[256,512]{1,0:T(8,128)(2,1)S(1)}, bf16[256,512]{1,0:T(8,128)(2,1)S(1)}, u32[]{:S(2)}, u32[]{:S(2)}) %collective-permute-start.31) | collective-permute-done | bytes 262176 | tf_op jit(solution)/shard_map/ppermute | solution.py:241
  107.9 9.3 %all-to-all-start = ((bf16[8,32,512]{2,1,0:T(8,128)(2,1)}), bf16[8,32,512]{2,1,0:T(8,128)(2,1)}, u32[]{:S(2)}, u32[]{:S(2)}) async-start(bf16[8,32,512]{2,1,0:T(8,128)(2,1)} %bitcast.27), calls=%async_computation | async-start | bytes 524288 | tf_op jit(solution)/shard_map/all_to_all | solution.py:274
  117.3 12.6 %score_grad.1 = (bf16[128,4096]{1,0:T(8,128)(2,1)}, f32[128,512]{1,0:T(8,128)S(1)}, bf16[128,512]{1,0:T(8,128)(2,1)S(1)}, bf16[128,512]{1,0:T(8,128)(2,1)S(1)}, ...) custom-call(s32[1,8]{1,0:T(1,128)S(1)} %copy-done.10, bf16[128,4096]{1,0:T(8,128)(2,1)S(1)} %bitcast.13, ...), custom_call_target="tpu_custom_call" | custom-call | flops 10000000000 | bytes 4000000 | tf_op jit(solution)/shard_map/score_grad/pallas_call | solution.py:165
  129.8 1.3 collective-permute-start.11
  131.2 3.7 %collective-permute-start.8 = (bf16[128,512]{1,0:T(8,128)(2,1)S(1)}, bf16[128,512]{1,0:T(8,128)(2,1)S(1)}, u32[]{:S(2)}, u32[]{:S(2)}) collective-permute-start(bf16[128,512]{1,0:T(8,128)(2,1)S(1)} %get-tuple-element.27), channel_id=1, source_target_pairs={{0,7},{1,0},{2,1},{3,2},{4,3},{5,4},{6,5},{7,6},{8,15},{9,8},{10,9... | collective-permute-start | bytes 393224 | tf_op jit(solution)/shard_map/ppermute | solution.py:241
  134.8 1.3 collective-permute-start.9
  136.2 2.1 %collective-permute-done.10 = bf16[128,512]{1,0:T(8,128)(2,1)S(1)} collective-permute-done((bf16[128,512]{1,0:T(8,128)(2,1)S(1)}, bf16[128,512]{1,0:T(8,128)(2,1)S(1)}, u32[]{:S(2)}, u32[]{:S(2)}) %collective-permute-start.10) | collective-permute-done | bytes 131104 | tf_op jit(solution)/shard_map/ppermute | solution.py:241
  138.3 4.7 %collective-permute-done.8 = bf16[128,512]{1,0:T(8,128)(2,1)S(1)} collective-permute-done((bf16[128,512]{1,0:T(8,128)(2,1)S(1)}, bf16[128,512]{1,0:T(8,128)(2,1)S(1)}, u32[]{:S(2)}, u32[]{:S(2)}) %collective-permute-start.8) | collective-permute-done | bytes 131104 | tf_op jit(solution)/shard_map/ppermute | solution.py:241
  (68 shorter events, 15.8 us)
Async XLA Ops:
  0.6 6.6 %collective-permute-start = (bf16[128,512]{1,0:T(8,128)(2,1)}, bf16[128,512]{1,0:T(8,128)(2,1)S(1)}, u32[]{:S(2)}, u32[]{:S(2)}) collective-permute-start(bf16[128,512]{1,0:T(8,128)(2,1)} %bitcast.16), channel_id=1, source_target_pairs={{0,1},{1,2},{2,3},{3,4},{4,5},{5,6},{6,7},{7,0},{8,9},{9,10},{10,1... | collective-permute-start | bytes 393224 | tf_op jit(solution)/shard_map/ppermute | solution.py:241
  2.1 8.3 %collective-permute-start.1 = (bf16[128,512]{1,0:T(8,128)(2,1)}, bf16[128,512]{1,0:T(8,128)(2,1)S(1)}, u32[]{:S(2)}, u32[]{:S(2)}) collective-permute-start(bf16[128,512]{1,0:T(8,128)(2,1)} %bitcast.17), channel_id=1, source_target_pairs={{0,2},{1,3},{2,4},{3,5},{4,6},{5,7},{6,0},{7,1},{8,10},{9,11},{10,... | collective-permute-start | bytes 393224 | tf_op jit(solution)/shard_map/ppermute | solution.py:241
  3.6 8.8 %collective-permute-start.2 = (bf16[128,512]{1,0:T(8,128)(2,1)}, bf16[128,512]{1,0:T(8,128)(2,1)S(1)}, u32[]{:S(2)}, u32[]{:S(2)}) collective-permute-start(bf16[128,512]{1,0:T(8,128)(2,1)} %bitcast.18), channel_id=1, source_target_pairs={{0,3},{1,4},{2,5},{3,6},{4,7},{5,0},{6,1},{7,2},{8,11},{9,12},{10,... | collective-permute-start | bytes 393224 | tf_op jit(solution)/shard_map/ppermute | solution.py:241
  6.4 10.3 %collective-permute-start.3 = (bf16[128,512]{1,0:T(8,128)(2,1)}, bf16[128,512]{1,0:T(8,128)(2,1)S(1)}, u32[]{:S(2)}, u32[]{:S(2)}) collective-permute-start(bf16[128,512]{1,0:T(8,128)(2,1)} %bitcast.19), channel_id=1, source_target_pairs={{0,4},{1,5},{2,6},{3,7},{4,0},{5,1},{6,2},{7,3},{8,12},{9,13},{10,... | collective-permute-start | bytes 393224 | tf_op jit(solution)/shard_map/ppermute | solution.py:241
  27.0 13.7 %collective-permute-start.12 = (bf16[128,512]{1,0:T(8,128)(2,1)S(1)}, bf16[128,512]{1,0:T(8,128)(2,1)S(1)}, u32[]{:S(2)}, u32[]{:S(2)}) collective-permute-start(bf16[128,512]{1,0:T(8,128)(2,1)S(1)} %get-tuple-element.32), channel_id=1, source_target_pairs={{0,7},{1,0},{2,1},{3,2},{4,3},{5,4},{6,5},{7,6},{8,15},{9,8},{10,9... | collective-permute-start | bytes 393224 | tf_op jit(solution)/shard_map/ppermute | solution.py:241
  34.5 25.9 %collective-permute-start.16 = (bf16[2,512,128]{2,1,0:T(8,128)(2,1)S(1)}, bf16[2,512,128]{2,1,0:T(8,128)(2,1)S(1)}, u32[]{:S(2)}, u32[]{:S(2)}) collective-permute-start(bf16[2,512,128]{2,1,0:T(8,128)(2,1)S(1)} %get-tuple-element.37), channel_id=1, source_target_pairs={{0,1},{1,2},{2,3},{3,4},{4,5},{5,6},{6,7},{7,0},{8,9},{9,10},{10,1... | collective-permute-start | bytes 786440 | tf_op jit(solution)/shard_map/ppermute | solution.py:241
  37.4 23.0 %collective-permute-start.17 = (bf16[2,512,128]{2,1,0:T(8,128)(2,1)S(1)}, bf16[2,512,128]{2,1,0:T(8,128)(2,1)S(1)}, u32[]{:S(2)}, u32[]{:S(2)}) collective-permute-start(bf16[2,512,128]{2,1,0:T(8,128)(2,1)S(1)} %get-tuple-element.38), channel_id=1, source_target_pairs={{0,2},{1,3},{2,4},{3,5},{4,6},{5,7},{6,0},{7,1},{8,10},{9,11},{10,... | collective-permute-start | bytes 786440 | tf_op jit(solution)/shard_map/ppermute | solution.py:241
  37.4 7.8 %collective-permute-start.13 = (bf16[128,512]{1,0:T(8,128)(2,1)S(1)}, bf16[128,512]{1,0:T(8,128)(2,1)S(1)}, u32[]{:S(2)}, u32[]{:S(2)}) collective-permute-start(bf16[128,512]{1,0:T(8,128)(2,1)S(1)} %get-tuple-element.33), channel_id=1, source_target_pairs={{0,6},{1,7},{2,0},{3,1},{4,2},{5,3},{6,4},{7,5},{8,14},{9,15},{10,... | collective-permute-start | bytes 393224 | tf_op jit(solution)/shard_map/ppermute | solution.py:241
  40.6 14.6 %collective-permute-start.14 = (bf16[128,512]{1,0:T(8,128)(2,1)S(1)}, bf16[128,512]{1,0:T(8,128)(2,1)S(1)}, u32[]{:S(2)}, u32[]{:S(2)}) collective-permute-start(bf16[128,512]{1,0:T(8,128)(2,1)S(1)} %get-tuple-element.34), channel_id=1, source_target_pairs={{0,5},{1,6},{2,7},{3,0},{4,1},{5,2},{6,3},{7,4},{8,13},{9,14},{10,... | collective-permute-start | bytes 393224 | tf_op jit(solution)/shard_map/ppermute | solution.py:241
  40.6 14.6 %collective-permute-start.15 = (bf16[128,512]{1,0:T(8,128)(2,1)S(1)}, bf16[128,512]{1,0:T(8,128)(2,1)S(1)}, u32[]{:S(2)}, u32[]{:S(2)}) collective-permute-start(bf16[128,512]{1,0:T(8,128)(2,1)S(1)} %get-tuple-element.35), channel_id=1, source_target_pairs={{0,4},{1,5},{2,6},{3,7},{4,0},{5,1},{6,2},{7,3},{8,12},{9,13},{10,... | collective-permute-start | bytes 393224 | tf_op jit(solution)/shard_map/ppermute | solution.py:241
  45.2 16.1 %collective-permute-start.18 = (bf16[2,512,128]{2,1,0:T(8,128)(2,1)S(1)}, bf16[2,512,128]{2,1,0:T(8,128)(2,1)S(1)}, u32[]{:S(2)}, u32[]{:S(2)}) collective-permute-start(bf16[2,512,128]{2,1,0:T(8,128)(2,1)S(1)} %get-tuple-element.39), channel_id=1, source_target_pairs={{0,3},{1,4},{2,5},{3,6},{4,7},{5,0},{6,1},{7,2},{8,11},{9,12},{10,... | collective-permute-start | bytes 786440 | tf_op jit(solution)/shard_map/ppermute | solution.py:241
  55.2 9.2 %collective-permute-start.19 = (bf16[2,512,128]{2,1,0:T(8,128)(2,1)S(1)}, bf16[2,512,128]{2,1,0:T(8,128)(2,1)S(1)}, u32[]{:S(2)}, u32[]{:S(2)}) collective-permute-start(bf16[2,512,128]{2,1,0:T(8,128)(2,1)S(1)} %get-tuple-element.40), channel_id=1, source_target_pairs={{0,4},{1,5},{2,6},{3,7},{4,0},{5,1},{6,2},{7,3},{8,12},{9,13},{10,... | collective-permute-start | bytes 786440 | tf_op jit(solution)/shard_map/ppermute | solution.py:241
  55.2 15.0 %collective-permute-start.20 = (bf16[2,512,128]{2,1,0:T(8,128)(2,1)S(1)}, bf16[2,512,128]{2,1,0:T(8,128)(2,1)S(1)}, u32[]{:S(2)}, u32[]{:S(2)}) collective-permute-start(bf16[2,512,128]{2,1,0:T(8,128)(2,1)S(1)} %get-tuple-element.41), channel_id=1, source_target_pairs={{0,5},{1,6},{2,7},{3,0},{4,1},{5,2},{6,3},{7,4},{8,13},{9,14},{10,... | collective-permute-start | bytes 786440 | tf_op jit(solution)/shard_map/ppermute | solution.py:241
  60.4 13.3 %collective-permute-start.21 = (bf16[2,512,128]{2,1,0:T(8,128)(2,1)S(1)}, bf16[2,512,128]{2,1,0:T(8,128)(2,1)S(1)}, u32[]{:S(2)}, u32[]{:S(2)}) collective-permute-start(bf16[2,512,128]{2,1,0:T(8,128)(2,1)S(1)} %get-tuple-element.42), channel_id=1, source_target_pairs={{0,6},{1,7},{2,0},{3,1},{4,2},{5,3},{6,4},{7,5},{8,14},{9,15},{10,... | collective-permute-start | bytes 786440 | tf_op jit(solution)/shard_map/ppermute | solution.py:241
  60.4 18.9 %collective-permute-start.22 = (bf16[2,512,128]{2,1,0:T(8,128)(2,1)S(1)}, bf16[2,512,128]{2,1,0:T(8,128)(2,1)S(1)}, u32[]{:S(2)}, u32[]{:S(2)}) collective-permute-start(bf16[2,512,128]{2,1,0:T(8,128)(2,1)S(1)} %get-tuple-element.43), channel_id=1, source_target_pairs={{0,7},{1,0},{2,1},{3,2},{4,3},{5,4},{6,5},{7,6},{8,15},{9,8},{10,9... | collective-permute-start | bytes 786440 | tf_op jit(solution)/shard_map/ppermute | solution.py:241
  61.3 18.0 %collective-permute-start.23 = (bf16[128,512]{1,0:T(8,128)(2,1)S(1)}, bf16[128,512]{1,0:T(8,128)(2,1)S(1)}, u32[]{:S(2)}, u32[]{:S(2)}) collective-permute-start(bf16[128,512]{1,0:T(8,128)(2,1)S(1)} %add_convert_fusion.refs_8_), channel_id=1, source_target_pairs={{0,1},{1,2},{2,3},{3,4},{4,5},{5,6},{6,7},{7,0},{8,9},{9,10},{10,1... | collective-permute-start | bytes 393224 | tf_op jit(solution)/shard_map/ppermute | solution.py:241
  64.5 16.4 %collective-permute-start.24 = (bf16[128,512]{1,0:T(8,128)(2,1)S(1)}, bf16[128,512]{1,0:T(8,128)(2,1)S(1)}, u32[]{:S(2)}, u32[]{:S(2)}) collective-permute-start(bf16[128,512]{1,0:T(8,128)(2,1)S(1)} %add_convert_fusion.refs_8_), channel_id=1, source_target_pairs={{0,2},{1,3},{2,4},{3,5},{4,6},{5,7},{6,0},{7,1},{8,10},{9,11},{10,... | collective-permute-start | bytes 393224 | tf_op jit(solution)/shard_map/ppermute | solution.py:241
  70.2 12.2 %collective-permute-start.25 = (bf16[128,512]{1,0:T(8,128)(2,1)S(1)}, bf16[128,512]{1,0:T(8,128)(2,1)S(1)}, u32[]{:S(2)}, u32[]{:S(2)}) collective-permute-start(bf16[128,512]{1,0:T(8,128)(2,1)S(1)} %add_convert_fusion.refs_8_), channel_id=1, source_target_pairs={{0,3},{1,4},{2,5},{3,6},{4,7},{5,0},{6,1},{7,2},{8,11},{9,12},{10,... | collective-permute-start | bytes 393224 | tf_op jit(solution)/shard_map/ppermute | solution.py:241
  73.7 8.7 %collective-permute-start.26 = (bf16[128,512]{1,0:T(8,128)(2,1)S(1)}, bf16[128,512]{1,0:T(8,128)(2,1)S(1)}, u32[]{:S(2)}, u32[]{:S(2)}) collective-permute-start(bf16[128,512]{1,0:T(8,128)(2,1)S(1)} %add_convert_fusion.refs_8_), channel_id=1, source_target_pairs={{0,4},{1,5},{2,6},{3,7},{4,0},{5,1},{6,2},{7,3},{8,12},{9,13},{10,... | collective-permute-start | bytes 393224 | tf_op jit(solution)/shard_map/ppermute | solution.py:241
  79.3 7.4 %collective-permute-start.27 = (bf16[128,512]{1,0:T(8,128)(2,1)S(1)}, bf16[128,512]{1,0:T(8,128)(2,1)S(1)}, u32[]{:S(2)}, u32[]{:S(2)}) collective-permute-start(bf16[128,512]{1,0:T(8,128)(2,1)S(1)} %add_convert_fusion.refs_8_), channel_id=1, source_target_pairs={{0,5},{1,6},{2,7},{3,0},{4,1},{5,2},{6,3},{7,4},{8,13},{9,14},{10,... | collective-permute-start | bytes 393224 | tf_op jit(solution)/shard_map/ppermute | solution.py:241
  79.3 7.4 %collective-permute-start.28 = (bf16[128,512]{1,0:T(8,128)(2,1)S(1)}, bf16[128,512]{1,0:T(8,128)(2,1)S(1)}, u32[]{:S(2)}, u32[]{:S(2)}) collective-permute-start(bf16[128,512]{1,0:T(8,128)(2,1)S(1)} %add_convert_fusion.refs_8_), channel_id=1, source_target_pairs={{0,6},{1,7},{2,0},{3,1},{4,2},{5,3},{6,4},{7,5},{8,14},{9,15},{10,... | collective-permute-start | bytes 393224 | tf_op jit(solution)/shard_map/ppermute | solution.py:241
  80.9 7.5 %collective-permute-start.29 = (bf16[128,512]{1,0:T(8,128)(2,1)S(1)}, bf16[128,512]{1,0:T(8,128)(2,1)S(1)}, u32[]{:S(2)}, u32[]{:S(2)}) collective-permute-start(bf16[128,512]{1,0:T(8,128)(2,1)S(1)} %add_convert_fusion.refs_8_), channel_id=1, source_target_pairs={{0,7},{1,0},{2,1},{3,2},{4,3},{5,4},{6,5},{7,6},{8,15},{9,8},{10,9... | collective-permute-start | bytes 393224 | tf_op jit(solution)/shard_map/ppermute | solution.py:241
  91.5 15.6 %collective-permute-start.31 = (bf16[256,512]{1,0:T(8,128)(2,1)S(1)}, bf16[256,512]{1,0:T(8,128)(2,1)S(1)}, u32[]{:S(2)}, u32[]{:S(2)}) collective-permute-start(bf16[256,512]{1,0:T(8,128)(2,1)S(1)} %slice.15), channel_id=1, source_target_pairs={{0,128},{8,136},{16,144},{24,152},{32,160},{40,168},{48,176},{56,1... | collective-permute-start | bytes 786440 | tf_op jit(solution)/shard_map/ppermute | solution.py:241
  94.2 23.0 %collective-permute-start.4 = (bf16[128,512]{1,0:T(8,128)(2,1)S(1)}, bf16[128,512]{1,0:T(8,128)(2,1)S(1)}, u32[]{:S(2)}, u32[]{:S(2)}) collective-permute-start(bf16[128,512]{1,0:T(8,128)(2,1)S(1)} %bitcast.22), channel_id=1, source_target_pairs={{0,1},{1,2},{2,3},{3,4},{4,5},{5,6},{6,7},{7,0},{8,9},{9,10},{10,1... | collective-permute-start | bytes 393224 | tf_op jit(solution)/shard_map/ppermute | solution.py:241
  94.4 22.8 %collective-permute-start.5 = (bf16[128,512]{1,0:T(8,128)(2,1)S(1)}, bf16[128,512]{1,0:T(8,128)(2,1)S(1)}, u32[]{:S(2)}, u32[]{:S(2)}) collective-permute-start(bf16[128,512]{1,0:T(8,128)(2,1)S(1)} %bitcast.23), channel_id=1, source_target_pairs={{0,2},{1,3},{2,4},{3,5},{4,6},{5,7},{6,0},{7,1},{8,10},{9,11},{10,... | collective-permute-start | bytes 393224 | tf_op jit(solution)/shard_map/ppermute | solution.py:241
  96.0 21.2 %collective-permute-start.6 = (bf16[128,512]{1,0:T(8,128)(2,1)S(1)}, bf16[128,512]{1,0:T(8,128)(2,1)S(1)}, u32[]{:S(2)}, u32[]{:S(2)}) collective-permute-start(bf16[128,512]{1,0:T(8,128)(2,1)S(1)} %bitcast.24), channel_id=1, source_target_pairs={{0,3},{1,4},{2,5},{3,6},{4,7},{5,0},{6,1},{7,2},{8,11},{9,12},{10,... | collective-permute-start | bytes 393224 | tf_op jit(solution)/shard_map/ppermute | solution.py:241
  99.5 17.7 %collective-permute-start.7 = (bf16[128,512]{1,0:T(8,128)(2,1)S(1)}, bf16[128,512]{1,0:T(8,128)(2,1)S(1)}, u32[]{:S(2)}, u32[]{:S(2)}) collective-permute-start(bf16[128,512]{1,0:T(8,128)(2,1)S(1)} %bitcast.25), channel_id=1, source_target_pairs={{0,4},{1,5},{2,6},{3,7},{4,0},{5,1},{6,2},{7,3},{8,12},{9,13},{10,... | collective-permute-start | bytes 393224 | tf_op jit(solution)/shard_map/ppermute | solution.py:241
  107.9 35.8 %all-to-all-start = ((bf16[8,32,512]{2,1,0:T(8,128)(2,1)}), bf16[8,32,512]{2,1,0:T(8,128)(2,1)}, u32[]{:S(2)}, u32[]{:S(2)}) async-start(bf16[8,32,512]{2,1,0:T(8,128)(2,1)} %bitcast.27), calls=%async_computation | async-start | bytes 524288 | tf_op jit(solution)/shard_map/all_to_all | solution.py:274
  129.8 8.4 %collective-permute-start.10 = (bf16[128,512]{1,0:T(8,128)(2,1)S(1)}, bf16[128,512]{1,0:T(8,128)(2,1)S(1)}, u32[]{:S(2)}, u32[]{:S(2)}) collective-permute-start(bf16[128,512]{1,0:T(8,128)(2,1)S(1)} %get-tuple-element.29), channel_id=1, source_target_pairs={{0,5},{1,6},{2,7},{3,0},{4,1},{5,2},{6,3},{7,4},{8,13},{9,14},{10,... | collective-permute-start | bytes 393224 | tf_op jit(solution)/shard_map/ppermute | solution.py:241
  129.8 8.4 %collective-permute-start.11 = (bf16[128,512]{1,0:T(8,128)(2,1)S(1)}, bf16[128,512]{1,0:T(8,128)(2,1)S(1)}, u32[]{:S(2)}, u32[]{:S(2)}) collective-permute-start(bf16[128,512]{1,0:T(8,128)(2,1)S(1)} %get-tuple-element.30), channel_id=1, source_target_pairs={{0,4},{1,5},{2,6},{3,7},{4,0},{5,1},{6,2},{7,3},{8,12},{9,13},{10,... | collective-permute-start | bytes 393224 | tf_op jit(solution)/shard_map/ppermute | solution.py:241
  131.2 11.8 %collective-permute-start.8 = (bf16[128,512]{1,0:T(8,128)(2,1)S(1)}, bf16[128,512]{1,0:T(8,128)(2,1)S(1)}, u32[]{:S(2)}, u32[]{:S(2)}) collective-permute-start(bf16[128,512]{1,0:T(8,128)(2,1)S(1)} %get-tuple-element.27), channel_id=1, source_target_pairs={{0,7},{1,0},{2,1},{3,2},{4,3},{5,4},{6,5},{7,6},{8,15},{9,8},{10,9... | collective-permute-start | bytes 393224 | tf_op jit(solution)/shard_map/ppermute | solution.py:241
  134.8 8.1 %collective-permute-start.9 = (bf16[128,512]{1,0:T(8,128)(2,1)S(1)}, bf16[128,512]{1,0:T(8,128)(2,1)S(1)}, u32[]{:S(2)}, u32[]{:S(2)}) collective-permute-start(bf16[128,512]{1,0:T(8,128)(2,1)S(1)} %get-tuple-element.28), channel_id=1, source_target_pairs={{0,6},{1,7},{2,0},{3,1},{4,2},{5,3},{6,4},{7,5},{8,14},{9,15},{10,... | collective-permute-start | bytes 393224 | tf_op jit(solution)/shard_map/ppermute | solution.py:241
  (12 other events, 152.7 us)

commit v2 on v1

v2 whole, which is shorter than its diff:
```python
import functools
import math

import jax
import jax.numpy as jnp
from jax import lax
from jax.experimental import pallas as pl
from jax.experimental.pallas import tpu as pltpu
from jax.sharding import PartitionSpec as P

HD = 128
GROUPS = 4
GROUP = 8
ROWS = 128
NEAR = 4
SCALE = HD**-0.5
SCALE_LOG2 = SCALE * math.log2(math.e)
NEG_FILL = -1e30
F32 = jnp.float32
BF16 = jnp.bfloat16


def params(mib):
    return pltpu.CompilerParams(vmem_limit_bytes=mib * 2**20)


def dot(a, b, contract):
    return lax.dot_general(a, b, ((contract[:1], contract[1:]), ((), ())), preferred_element_type=F32)


def fill_bias(lengths, bias):
    first = lax.axis_index("ctx") * ROWS
    query = lax.broadcasted_iota(jnp.int32, (ROWS, 2 * ROWS), 1) % ROWS
    key = lax.broadcasted_iota(jnp.int32, (ROWS, 2 * ROWS), 0)
    start = jnp.zeros_like(query)
    ending = jnp.int32(0)
    for n in range(lengths.shape[1]):
        ending = ending + lengths[0, n]
        start = jnp.where(ending <= query + first, ending, start)
    for block in range(NEAR):
        place = key + (first - block * ROWS)
        if block == 0:
            place = jnp.where(key <= query, place, place - NEAR * ROWS)
        bias[block * ROWS : (block + 1) * ROWS, :] = jnp.where(place >= start, 0.0, NEG_FILL)


def lower():
    query = lax.broadcasted_iota(jnp.int32, (ROWS, 2 * ROWS), 1) % ROWS
    key = lax.broadcasted_iota(jnp.int32, (ROWS, 2 * ROWS), 0)
    return key <= query


def fold(tile, mask):
    return jnp.concatenate(
        [jnp.where(mask, tile[:ROWS], tile[NEAR * ROWS :]), tile[ROWS : NEAR * ROWS]], axis=0
    )


def unfold(tile, mask):
    return jnp.concatenate(
        [
            jnp.where(mask, tile[:ROWS], 0.0).astype(BF16),
            tile[ROWS:].astype(BF16),
            jnp.where(mask, 0.0, tile[:ROWS]).astype(BF16),
        ],
        axis=0,
    )


def heads(ref, first, count):
    return jnp.concatenate([ref[:, (first + n) * HD : (first + n + 1) * HD] for n in range(count)], axis=0)


def blocks(refs, column):
    return jnp.concatenate([ref[:, column * HD : (column + 1) * HD] for ref in refs], axis=0)


def hand_out(grad, group, outs):
    cols = slice(group * HD, (group + 1) * HD)
    for n, ref in enumerate(outs):
        ref[:, cols] = grad[n * ROWS : (n + 1) * ROWS].astype(ref.dtype)


def value_kernel(lengths, q, do, k0, k1, k2, k3, k4, own, s1, s2, s3, s4, stats, bias, prob):
    fill_bias(lengths, bias)
    mask = lower()
    for group in range(GROUPS):
        keys = blocks((k0, k1, k2, k3, k4), group)
        for pair in range(GROUP // 2):
            lanes = slice(pair * 256, (pair + 1) * 256)
            scores = fold(dot(keys, heads(q, group * GROUP + 2 * pair, 2), (1, 1)), mask) + bias[...]
            top = jnp.max(scores, axis=0, keepdims=True)
            weight = jnp.exp2((scores - top) * SCALE_LOG2)
            inverse = 1.0 / jnp.sum(weight, axis=0, keepdims=True)
            prob[group % 2, :, lanes] = unfold(weight * inverse, mask)
            stats[group, 0:1, lanes] = top
            stats[group, 1:2, lanes] = inverse
        grad = dot(prob[group % 2], heads(do, group * GROUP, GROUP), (1, 0))
        hand_out(grad, group, (own, s1, s2, s3, s4))


def score_kernel(
    lengths, q, do, k0, k1, k2, k3, k4, v0, v1, v2, v3, v4, stats, dq, own, s1, s2, s3, s4, bias, dsc
):
    fill_bias(lengths, bias)
    mask = lower()
    for group in range(GROUPS):
        keys, values = blocks((k0, k1, k2, k3, k4), group), blocks((v0, v1, v2, v3, v4), group)
        for pair in range(GROUP // 2):
            lanes = slice(pair * 256, (pair + 1) * 256)
            first = group * GROUP + 2 * pair
            top, inverse = stats[group, 0:1, lanes], stats[group, 1:2, lanes]
            scores = fold(dot(keys, heads(q, first, 2), (1, 1)), mask) + bias[...]
            probability = jnp.exp2((scores - top) * SCALE_LOG2) * inverse
            dprob = fold(dot(values, heads(do, first, 2), (1, 1)), mask)
            delta = jnp.sum(probability.astype(BF16).astype(F32) * dprob, axis=0, keepdims=True)
            dsc[group % 2, :, lanes] = unfold(probability * (dprob - delta), mask)
        rows = (dot(dsc[group % 2], keys, (0, 0)) * SCALE).astype(BF16)
        for n in range(GROUP):
            head = group * GROUP + n
            dq[:, head * HD : (head + 1) * HD] = rows[n * HD : (n + 1) * HD]
        grad = dot(dsc[group % 2], heads(q, group * GROUP, GROUP), (1, 0)) * SCALE
        hand_out(grad, group, (own, s1, s2, s3, s4))


def sds(shape, dtype):
    return jax.ShapeDtypeStruct(shape, dtype)


VMEM = pl.BlockSpec(memory_space=pltpu.VMEM)
SMEM = pl.BlockSpec(memory_space=pltpu.SMEM)
TERMS = [sds((ROWS, GROUPS * HD), F32)] + [sds((ROWS, GROUPS * HD), BF16)] * NEAR
STATS = sds((GROUPS, 8, GROUP * ROWS), F32)
SCRATCH = [pltpu.VMEM((NEAR * ROWS, 2 * ROWS), F32), pltpu.VMEM((2, 5 * ROWS, GROUP * ROWS), BF16)]


def value_call(lengths, q, do, keys):
    return pl.pallas_call(
        value_kernel,
        in_specs=[SMEM] + [VMEM] * 7,
        out_specs=[VMEM] * 6,
        out_shape=TERMS + [STATS],
        scratch_shapes=SCRATCH,
        compiler_params=params(58),
        cost_estimate=pl.CostEstimate(flops=3 * 10**10, bytes_accessed=4 * 10**6, transcendentals=2 * 10**6),
        name="value_grad",
    )(lengths, q, do, *keys)


def score_call(lengths, q, do, keys, values, stats):
    return pl.pallas_call(
        score_kernel,
        in_specs=[SMEM] + [VMEM] * 13,
        out_specs=[VMEM] * 6,
        out_shape=[sds((ROWS, GROUPS * GROUP * HD), BF16)] + TERMS,
        scratch_shapes=SCRATCH,
        compiler_params=params(58),
        cost_estimate=pl.CostEstimate(flops=4 * 10**10, bytes_accessed=4 * 10**6, transcendentals=2 * 10**6),
        name="score_grad",
    )(lengths, q, do, *keys, *values, stats)


def deal_kernel(x, out, pick):
    step = pl.program_id(0)

    @pl.when(step == 0)
    def _():
        row = lax.broadcasted_iota(jnp.int32, (256, 256), 0)
        col = lax.broadcasted_iota(jnp.int32, (256, 256), 1)
        pick[...] = jnp.where(row == col, 1.0, 0.0).astype(BF16)

    for n in range(4):
        dealt = dot(pick[...], x[:, n * 256 : (n + 1) * 256], (1, 1)).astype(BF16)
        member = (n % 2) * 4 + (step // 4) * 2 + n // 2
        for ctx in range(8):
            first = pl.multiple_of((ctx % 2) * 128 + (step % 4) * 32, 32)
            out[member, ctx // 2, pl.ds(first, 32)] = dealt[ctx * 32 : (ctx + 1) * 32]


def deal_call(x):
    return pl.pallas_call(
        deal_kernel,
        grid=(8,),
        in_specs=[pl.BlockSpec((ROWS, 1024), lambda step: (0, step))],
        out_specs=pl.BlockSpec((8, 4, 256, ROWS), lambda step: (0, 0, 0, 0)),
        out_shape=sds((8, 4, 256, ROWS), BF16),
        scratch_shapes=[pltpu.VMEM((256, 256), BF16)],
        compiler_params=params(24),
        cost_estimate=pl.CostEstimate(flops=2 * 10**9, bytes_accessed=4 * 10**6, transcendentals=0),
        name="deal_inputs",
    )(x)


def weight_kernel(first, inputs, *refs):
    grads, outs = refs[:8], refs[8:]
    dp, ctx = lax.axis_index("dp"), lax.axis_index("ctx")
    core, high, low, x = dp % 2, dp // 16, dp // 2 % 2, ctx // 2
    members = [(core ^ c) * 4 + (high ^ h) * 2 + (low ^ n) for c in range(2) for n in range(2) for h in range(2)]
    right = jnp.concatenate([ref[...] for ref in grads], axis=0)
    for n, out in enumerate(outs):
        left = jnp.concatenate([inputs[member, (x + first + n) % 4] for member in members], axis=1)
        out[...] = dot(left, right, (1, 0)).astype(out.dtype)


def weight_call(first, count, inputs, grads, dtype):
    width = grads[0].shape[1]
    return pl.pallas_call(
        functools.partial(weight_kernel, first),
        in_specs=[VMEM] * 9,
        out_specs=[VMEM] * count,
        out_shape=[sds((256, width), dtype)] * count,
        compiler_params=params(24),
        cost_estimate=pl.CostEstimate(flops=3 * 10**8 * count, bytes_accessed=10**6 * count, transcendentals=0),
        name="weight_grad",
    )(inputs, *grads)


def place(device):
    dp, ctx = divmod(device, 8)
    return ctx // 2, dp // 16 * 2 + ctx % 2, dp // 2 % 8, dp % 2


def device(x, y, z, core):
    return ((y // 2 * 8 + z) * 2 + core) * 8 + x * 2 + y % 2


def move(array, dx=0, flip_y=False, flip_z=False, flip_core=False):
    pairs = []
    for source in range(256):
        x, y, z, core = place(source)
        target = device((x + dx) % 4, 3 - y if flip_y else y, z ^ flip_z, core ^ flip_core)
        pairs.append((source, target))
    return lax.ppermute(array, ("dp", "ctx"), pairs)


def ring(array, distance):
    return lax.ppermute(array, "ctx", [(n, (n + distance) % 8) for n in range(8)])


def after(array, *others):
    return lax.optimization_barrier((array, *others))[0]


def shards(query_heads, key_heads, value_heads, out_grad, layer_inputs, doc_lengths):
    q, do = query_heads[0], out_grad[0]
    key, value = key_heads[0], value_heads[0]
    tokens = lax.axis_size("dp") * lax.axis_size("ctx") * q.shape[0]
    keys = [key] + [ring(key, d) for d in range(1, 5)]
    values = [value] + [ring(value, d) for d in range(1, 5)]
    dealt = deal_call(layer_inputs[0])
    members = [
        [device(x, y, z, core) for core in range(2) for y in ys for z in (z0, z0 + 1)]
        for x in range(4)
        for ys in ((1, 2), (0, 3))
        for z0 in range(0, 8, 2)
    ]
    inputs = lax.all_to_all(dealt, ("dp", "ctx"), 0, 0, axis_index_groups=members)

    *value_terms, stats = value_call(doc_lengths, q, do, keys)
    arrived = [ring(term, -d) for d, term in enumerate(value_terms[1:], 1)]
    value_grad = (after(value_terms[0], *values) + sum(term.astype(F32) for term in arrived)).astype(BF16)

    flips = ((True, False), (False, True), (True, True))
    grads = [value_grad] + [move(value_grad, flip_y=y, flip_z=z) for y, z in flips]
    grads += [move(grad, flip_core=True) for grad in grads]
    away = weight_call(1, 3, inputs, grads, BF16)
    across = [move(term, dx=d) for d, term in enumerate(away, 1)]
    (total,) = weight_call(0, 1, inputs, grads, F32)

    query_grad, *key_terms = score_call(doc_lengths, q, do, keys, values, after(stats, total))
    arrived = [ring(term, -d) for d, term in enumerate(key_terms[1:], 1)]
    key_grad = (key_terms[0] + sum(term.astype(F32) for term in arrived)).astype(BF16)
    total = (after(total, query_grad) + sum(term.astype(F32) for term in across)).astype(BF16)
    owners = [
        [device(x, 2 * high + y, 2 * z + low, core) for y in range(2) for z in range(4)]
        for x in range(4)
        for high in range(2)
        for low in range(2)
        for core in range(2)
    ]
    parts = lax.all_to_all(total.reshape(8, 32, -1), ("dp", "ctx"), 0, 0, axis_index_groups=owners)
    weight_grad = jnp.sum(parts.astype(F32), axis=0) * tokens**-0.5

    return query_grad[None], key_grad[None], value_grad[None], weight_grad


def solution(mesh):
    split = P("dp", "ctx", None)
    return jax.shard_map(
        shards,
        mesh=mesh,
        in_specs=(split,) * 5 + (P("dp", None),),
        out_specs=(split, split, split, P(("dp", "ctx"), None)),
        check_vma=False,
    )
```

time: 147 us -> 105 us (0.71)
  the two profiles are of different devices: /device:TPU:8 before, /device:TPU:6 now
where the time goes in v2:
time: 105 us
  starting transfers between devices  46.8 us (45%)
  waiting for transfers between devices  29.2 us (28%)
  Pallas kernels  20.8 us (20%)
  local copies, waits for them, and re-layouts  3.62 us (3%)
  other arithmetic  3.29 us (3%)
    ppermute x16, starting transfers between devices, ring(): lax.ppermute(array, 'ctx', [(n, (n + distance) % 8) for n in range(8)])  23.6 us
    ppermute x16, waiting for transfers between devices, ring(): lax.ppermute(array, 'ctx', [(n, (n + distance) % 8) for n in range(8)])  22.9 us
    pallas_call x1, Pallas kernels, score_call(): pl.pallas_call(score_kernel, in_specs=[SMEM] + [VMEM] * 13, out_specs=[VM...  10.7 us
    ppermute x10, starting transfers between devices, move(): return lax.ppermute(array, ('dp', 'ctx'), pairs)  8.9 us
    all_to_all x1, starting transfers between devices, shards(): lax.all_to_all(total.reshape(8, 32, -1), ('dp', 'ctx'), 0, 0, axis_index_...  8.5 us
    ppermute x10, waiting for transfers between devices, move(): return lax.ppermute(array, ('dp', 'ctx'), pairs)  6.3 us
    pallas_call x1, Pallas kernels, value_call(): pl.pallas_call(value_kernel, in_specs=[SMEM] + [VMEM] * 7, out_specs=[VME...  6.03 us
    all_to_all x1, starting transfers between devices, shards(): lax.all_to_all(dealt, ('dp', 'ctx'), 0, 0, axis_index_groups=members)  5.78 us
  transfers between devices with their start and end apart: 28, of which 10 were waited for; matrix products, arithmetic and copies ran while one was open for 2% of the time, Pallas kernels for 16%

profile of v2, /device:TPU:6, one launch (start us, length us, event | category | flops | bytes accessed | tf_op | source)
XLA Modules:
  0.0 104.5 jit_solution(10074863870477948660)
XLA Ops:
  0.6 1.6 %copy-done.2 = bf16[1,128,8192]{2,1,0:T(8,128)(2,1)S(1)} copy-done((bf16[1,128,8192]{2,1,0:T(8,128)(2,1)S(1)}, bf16[1,128,8192]{2,1,0:T(8,128)(2,1)}, u32[]{:S(2)}) %copy-start.2) | copy-done | bytes 2097176
  2.2 2.7 %deal_inputs.1 = bf16[8,4,256,128]{3,2,1,0:T(8,128)(2,1)S(1)} custom-call(bf16[128,8192]{1,0:T(8,128)(2,1)S(1)} %bitcast.11), custom_call_target="tpu_custom_call" | custom-call | flops 2000000000 | bytes 4000000 | tf_op jit(solution)/shard_map/deal_inputs/pallas_call | solution.py:181
  4.9 1.3 %copy-done = bf16[8,4,256,128]{3,2,1,0:T(8,128)(2,1)} copy-done((bf16[8,4,256,128]{3,2,1,0:T(8,128)(2,1)}, bf16[8,4,256,128]{3,2,1,0:T(8,128)(2,1)S(1)}, u32[]{:S(2)}) %copy-start) | copy-done | bytes 2097176
  6.2 5.8 %all-to-all-start = ((bf16[8,4,256,128]{3,2,1,0:T(8,128)(2,1)}), bf16[8,4,256,128]{3,2,1,0:T(8,128)(2,1)S(1)}, u32[]{:S(2)}, u32[]{:S(2)}) async-start(bf16[8,4,256,128]{3,2,1,0:T(8,128)(2,1)} %copy-done), calls=%async_computation | async-start | bytes 4194304 | tf_op jit(solution)/shard_map/all_to_all | solution.py:257
  12.0 1.5 %collective-permute-start.3 = (bf16[128,512]{1,0:T(8,128)(2,1)S(1)}, bf16[128,512]{1,0:T(8,128)(2,1)S(1)}, u32[]{:S(2)}, u32[]{:S(2)}) collective-permute-start(bf16[128,512]{1,0:T(8,128)(2,1)S(1)} %bitcast.18), channel_id=1, source_target_pairs={{0,4},{1,5},{2,6},{3,7},{4,0},{5,1},{6,2},{7,3},{8,12},{9,13},{10,... | collective-permute-start | bytes 393224 | tf_op jit(solution)/shard_map/ppermute | solution.py:237
  13.5 1.7 %collective-permute-start.2 = (bf16[128,512]{1,0:T(8,128)(2,1)S(1)}, bf16[128,512]{1,0:T(8,128)(2,1)S(1)}, u32[]{:S(2)}, u32[]{:S(2)}) collective-permute-start(bf16[128,512]{1,0:T(8,128)(2,1)S(1)} %bitcast.19), channel_id=1, source_target_pairs={{0,3},{1,4},{2,5},{3,6},{4,7},{5,0},{6,1},{7,2},{8,11},{9,12},{10,... | collective-permute-start | bytes 393224 | tf_op jit(solution)/shard_map/ppermute | solution.py:237
  15.8 1.8 %collective-permute-start = (bf16[128,512]{1,0:T(8,128)(2,1)S(1)}, bf16[128,512]{1,0:T(8,128)(2,1)S(1)}, u32[]{:S(2)}, u32[]{:S(2)}) collective-permute-start(bf16[128,512]{1,0:T(8,128)(2,1)S(1)} %bitcast.21), channel_id=1, source_target_pairs={{0,1},{1,2},{2,3},{3,4},{4,5},{5,6},{6,7},{7,0},{8,9},{9,10},{10,1... | collective-permute-start | bytes 393224 | tf_op jit(solution)/shard_map/ppermute | solution.py:237
  17.6 2.4 %collective-permute-start.7 = (bf16[128,512]{1,0:T(8,128)(2,1)S(1)}, bf16[128,512]{1,0:T(8,128)(2,1)S(1)}, u32[]{:S(2)}, u32[]{:S(2)}) collective-permute-start(bf16[128,512]{1,0:T(8,128)(2,1)S(1)} %bitcast.23), channel_id=1, source_target_pairs={{0,4},{1,5},{2,6},{3,7},{4,0},{5,1},{6,2},{7,3},{8,12},{9,13},{10,... | collective-permute-start | bytes 393224 | tf_op jit(solution)/shard_map/ppermute | solution.py:237
  20.0 1.4 %collective-permute-start.6 = (bf16[128,512]{1,0:T(8,128)(2,1)S(1)}, bf16[128,512]{1,0:T(8,128)(2,1)S(1)}, u32[]{:S(2)}, u32[]{:S(2)}) collective-permute-start(bf16[128,512]{1,0:T(8,128)(2,1)S(1)} %bitcast.24), channel_id=1, source_target_pairs={{0,3},{1,4},{2,5},{3,6},{4,7},{5,0},{6,1},{7,2},{8,11},{9,12},{10,... | collective-permute-start | bytes 393224 | tf_op jit(solution)/shard_map/ppermute | solution.py:237
  22.3 2.1 %collective-permute-start.5 = (bf16[128,512]{1,0:T(8,128)(2,1)S(1)}, bf16[128,512]{1,0:T(8,128)(2,1)S(1)}, u32[]{:S(2)}, u32[]{:S(2)}) collective-permute-start(bf16[128,512]{1,0:T(8,128)(2,1)S(1)} %bitcast.25), channel_id=1, source_target_pairs={{0,2},{1,3},{2,4},{3,5},{4,6},{5,7},{6,0},{7,1},{8,10},{9,11},{10,... | collective-permute-start | bytes 393224 | tf_op jit(solution)/shard_map/ppermute | solution.py:237
  25.1 3.9 %collective-permute-done.k1 = bf16[128,512]{1,0:T(8,128)(2,1)S(1)} collective-permute-done((bf16[128,512]{1,0:T(8,128)(2,1)S(1)}, bf16[128,512]{1,0:T(8,128)(2,1)S(1)}, u32[]{:S(2)}, u32[]{:S(2)}) %collective-permute-start) | collective-permute-done | bytes 131104 | tf_op jit(solution)/shard_map/ppermute | solution.py:237
  29.7 6.0 %value_grad.1 = (f32[128,512]{1,0:T(8,128)}, bf16[128,512]{1,0:T(8,128)(2,1)}, bf16[128,512]{1,0:T(8,128)(2,1)}, bf16[128,512]{1,0:T(8,128)(2,1)}, bf16[128,512]{1,0:T(8,128)(2,1)}, /*index=5*/f32[4,8,1024]{2,1,0:T(8,128)}) custom-call(s32[1,8]{1,0:T(1,128)} %lengths.3, bf16[128,4096]{1,0:T(8,128)(2,1)} %bitcast.12, bf16[128,4096]{1,0:T(8,128)(2,1)} %bitcast.14, ...), custom_call_target="tpu_custom_call" | custom-call | flops 30000001024 | bytes 4000000 | tf_op jit(solution)/shard_map/value_grad/pallas_call | solution.py:138
  35.9 3.8 %collective-permute-start.10 = (bf16[128,512]{1,0:T(8,128)(2,1)}, bf16[128,512]{1,0:T(8,128)(2,1)S(1)}, u32[]{:S(2)}, u32[]{:S(2)}) collective-permute-start(bf16[128,512]{1,0:T(8,128)(2,1)} %get-tuple-element.27), channel_id=1, source_target_pairs={{0,5},{1,6},{2,7},{3,0},{4,1},{5,2},{6,3},{7,4},{8,13},{9,14},{10,... | collective-permute-start | bytes 393224 | tf_op jit(solution)/shard_map/ppermute | solution.py:237
  39.7 1.3 %collective-permute-start.11 = (bf16[128,512]{1,0:T(8,128)(2,1)}, bf16[128,512]{1,0:T(8,128)(2,1)S(1)}, u32[]{:S(2)}, u32[]{:S(2)}) collective-permute-start(bf16[128,512]{1,0:T(8,128)(2,1)} %get-tuple-element.28), channel_id=1, source_target_pairs={{0,4},{1,5},{2,6},{3,7},{4,0},{5,1},{6,2},{7,3},{8,12},{9,13},{10,... | collective-permute-start | bytes 393224 | tf_op jit(solution)/shard_map/ppermute | solution.py:237
  40.9 1.4 %collective-permute-done.8 = bf16[128,512]{1,0:T(8,128)(2,1)S(1)} collective-permute-done((bf16[128,512]{1,0:T(8,128)(2,1)}, bf16[128,512]{1,0:T(8,128)(2,1)S(1)}, u32[]{:S(2)}, u32[]{:S(2)}) %collective-permute-start.8) | collective-permute-done | bytes 131104 | tf_op jit(solution)/shard_map/ppermute | solution.py:237
  42.3 7.0 %collective-permute-done.9 = bf16[128,512]{1,0:T(8,128)(2,1)S(1)} collective-permute-done((bf16[128,512]{1,0:T(8,128)(2,1)}, bf16[128,512]{1,0:T(8,128)(2,1)S(1)}, u32[]{:S(2)}, u32[]{:S(2)}) %collective-permute-start.9) | collective-permute-done | bytes 131104 | tf_op jit(solution)/shard_map/ppermute | solution.py:237
  49.4 1.0 add_convert_fusion.2.refs_0_
  50.4 2.2 %collective-permute-start.14 = (bf16[128,512]{1,0:T(8,128)(2,1)S(1)}, bf16[128,512]{1,0:T(8,128)(2,1)S(1)}, u32[]{:S(2)}, u32[]{:S(2)}) collective-permute-start(bf16[128,512]{1,0:T(8,128)(2,1)S(1)} %add_convert_fusion.2.refs_0_), channel_id=1, source_target_pairs={{0,145},{1,144},{2,147},{3,146},{4,149},{5,148},{6,151},{7,150},{8... | collective-permute-start | bytes 393224 | tf_op jit(solution)/shard_map/ppermute | solution.py:233
  53.2 2.0 %collective-permute-start.12 = (bf16[128,512]{1,0:T(8,128)(2,1)S(1)}, bf16[128,512]{1,0:T(8,128)(2,1)S(1)}, u32[]{:S(2)}, u32[]{:S(2)}) collective-permute-start(bf16[128,512]{1,0:T(8,128)(2,1)S(1)} %add_convert_fusion.2.refs_0_), channel_id=1, source_target_pairs={{0,129},{1,128},{2,131},{3,130},{4,133},{5,132},{6,135},{7,134},{8... | collective-permute-start | bytes 393224 | tf_op jit(solution)/shard_map/ppermute | solution.py:233
  55.2 2.4 %collective-permute-done.14.refs_3_ = bf16[128,512]{1,0:T(8,128)(2,1)S(1)} collective-permute-done((bf16[128,512]{1,0:T(8,128)(2,1)S(1)}, bf16[128,512]{1,0:T(8,128)(2,1)S(1)}, u32[]{:S(2)}, u32[]{:S(2)}) %collective-permute-start.14) | collective-permute-done | bytes 131104 | tf_op jit(solution)/shard_map/ppermute | solution.py:233
  58.1 1.3 %collective-permute-done.12.refs_1_ = bf16[128,512]{1,0:T(8,128)(2,1)S(1)} collective-permute-done((bf16[128,512]{1,0:T(8,128)(2,1)S(1)}, bf16[128,512]{1,0:T(8,128)(2,1)S(1)}, u32[]{:S(2)}, u32[]{:S(2)}) %collective-permute-start.12) | collective-permute-done | bytes 131104 | tf_op jit(solution)/shard_map/ppermute | solution.py:233
  59.4 1.3 %collective-permute-done.16.refs_5_ = bf16[128,512]{1,0:T(8,128)(2,1)S(1)} collective-permute-done((bf16[128,512]{1,0:T(8,128)(2,1)S(1)}, bf16[128,512]{1,0:T(8,128)(2,1)S(1)}, u32[]{:S(2)}, u32[]{:S(2)}) %collective-permute-start.16) | collective-permute-done | bytes 131104 | tf_op jit(solution)/shard_map/ppermute | solution.py:233
  61.2 1.0 weight_grad.3
  62.5 2.9 %collective-permute-start.24 = (bf16[256,512]{1,0:T(8,128)(2,1)S(1)}, bf16[256,512]{1,0:T(8,128)(2,1)S(1)}, u32[]{:S(2)}, u32[]{:S(2)}) collective-permute-start(bf16[256,512]{1,0:T(8,128)(2,1)S(1)} %get-tuple-element.38), channel_id=1, source_target_pairs={{0,4},{1,5},{2,6},{3,7},{4,0},{5,1},{6,2},{7,3},{8,12},{9,13},{10,... | collective-permute-start | bytes 786440 | tf_op jit(solution)/shard_map/ppermute | solution.py:233
  65.8 10.7 %score_grad.1 = (bf16[128,4096]{1,0:T(8,128)(2,1)}, f32[128,512]{1,0:T(8,128)}, bf16[128,512]{1,0:T(8,128)(2,1)}, bf16[128,512]{1,0:T(8,128)(2,1)}, bf16[128,512]{1,0:T(8,128)(2,1)}, /*index=5*/bf16[128,512]{1,0:T(8,128)(2,1)}) custom-call(s32[1,8]{1,0:T(1,128)} %lengths.3, bf16[128,4096]{1,0:T(8,128)(2,1)} %bitcast.13, bf16[128,4096]{1,0:T(8,128)(2,1)} %bitcast.15, ...), custom_call_target="tpu_custom_call" | custom-call | flops 40000000000 | bytes 4000000 | tf_op jit(solution)/shard_map/score_grad/pallas_call | solution.py:151
  76.5 1.3 %collective-permute-done.25 = bf16[256,512]{1,0:T(8,128)(2,1)S(1)} collective-permute-done((bf16[256,512]{1,0:T(8,128)(2,1)S(1)}, bf16[256,512]{1,0:T(8,128)(2,1)S(1)}, u32[]{:S(2)}, u32[]{:S(2)}) %collective-permute-start.25) | collective-permute-done | bytes 262176 | tf_op jit(solution)/shard_map/ppermute | solution.py:233
  78.7 8.5 %all-to-all-start.1 = ((bf16[8,32,512]{2,1,0:T(8,128)(2,1)}), bf16[8,32,512]{2,1,0:T(8,128)(2,1)S(1)}, u32[]{:S(2)}, u32[]{:S(2)}) async-start(bf16[8,32,512]{2,1,0:T(8,128)(2,1)} %bitcast.8), calls=%async_computation.1 | async-start | bytes 524288 | tf_op jit(solution)/shard_map/all_to_all | solution.py:281
  87.2 1.9 %collective-permute-start.19 = (bf16[128,512]{1,0:T(8,128)(2,1)S(1)}, bf16[128,512]{1,0:T(8,128)(2,1)S(1)}, u32[]{:S(2)}, u32[]{:S(2)}) collective-permute-start(bf16[128,512]{1,0:T(8,128)(2,1)S(1)} %copy-done.17), channel_id=1, source_target_pairs={{0,7},{1,0},{2,1},{3,2},{4,3},{5,4},{6,5},{7,6},{8,15},{9,8},{10,9... | collective-permute-start | bytes 393224 | tf_op jit(solution)/shard_map/ppermute | solution.py:237
  89.9 1.4 %collective-permute-start.21 = (bf16[128,512]{1,0:T(8,128)(2,1)S(1)}, bf16[128,512]{1,0:T(8,128)(2,1)S(1)}, u32[]{:S(2)}, u32[]{:S(2)}) collective-permute-start(bf16[128,512]{1,0:T(8,128)(2,1)S(1)} %copy-done.15), channel_id=1, source_target_pairs={{0,5},{1,6},{2,7},{3,0},{4,1},{5,2},{6,3},{7,4},{8,13},{9,14},{10,... | collective-permute-start | bytes 393224 | tf_op jit(solution)/shard_map/ppermute | solution.py:237
  91.3 2.2 %collective-permute-start.22 = (bf16[128,512]{1,0:T(8,128)(2,1)S(1)}, bf16[128,512]{1,0:T(8,128)(2,1)S(1)}, u32[]{:S(2)}, u32[]{:S(2)}) collective-permute-start(bf16[128,512]{1,0:T(8,128)(2,1)S(1)} %copy-done.14), channel_id=1, source_target_pairs={{0,4},{1,5},{2,6},{3,7},{4,0},{5,1},{6,2},{7,3},{8,12},{9,13},{10,... | collective-permute-start | bytes 393224 | tf_op jit(solution)/shard_map/ppermute | solution.py:237
  93.4 1.2 %collective-permute-done.19 = bf16[128,512]{1,0:T(8,128)(2,1)S(1)} collective-permute-done((bf16[128,512]{1,0:T(8,128)(2,1)S(1)}, bf16[128,512]{1,0:T(8,128)(2,1)S(1)}, u32[]{:S(2)}, u32[]{:S(2)}) %collective-permute-start.19) | collective-permute-done | bytes 131104 | tf_op jit(solution)/shard_map/ppermute | solution.py:237
  94.6 8.5 %collective-permute-done.20 = bf16[128,512]{1,0:T(8,128)(2,1)S(1)} collective-permute-done((bf16[128,512]{1,0:T(8,128)(2,1)S(1)}, bf16[128,512]{1,0:T(8,128)(2,1)S(1)}, u32[]{:S(2)}, u32[]{:S(2)}) %collective-permute-start.20) | collective-permute-done | bytes 131104 | tf_op jit(solution)/shard_map/ppermute | solution.py:237
  (70 shorter events, 8.3 us)
Async XLA Ops:
  6.2 54.5 %all-to-all-start = ((bf16[8,4,256,128]{3,2,1,0:T(8,128)(2,1)}), bf16[8,4,256,128]{3,2,1,0:T(8,128)(2,1)S(1)}, u32[]{:S(2)}, u32[]{:S(2)}) async-start(bf16[8,4,256,128]{3,2,1,0:T(8,128)(2,1)} %copy-done), calls=%async_computation | async-start | bytes 4194304 | tf_op jit(solution)/shard_map/all_to_all | solution.py:257
  12.0 8.0 %collective-permute-start.3 = (bf16[128,512]{1,0:T(8,128)(2,1)S(1)}, bf16[128,512]{1,0:T(8,128)(2,1)S(1)}, u32[]{:S(2)}, u32[]{:S(2)}) collective-permute-start(bf16[128,512]{1,0:T(8,128)(2,1)S(1)} %bitcast.18), channel_id=1, source_target_pairs={{0,4},{1,5},{2,6},{3,7},{4,0},{5,1},{6,2},{7,3},{8,12},{9,13},{10,... | collective-permute-start | bytes 393224 | tf_op jit(solution)/shard_map/ppermute | solution.py:237
  13.5 8.7 %collective-permute-start.2 = (bf16[128,512]{1,0:T(8,128)(2,1)S(1)}, bf16[128,512]{1,0:T(8,128)(2,1)S(1)}, u32[]{:S(2)}, u32[]{:S(2)}) collective-permute-start(bf16[128,512]{1,0:T(8,128)(2,1)S(1)} %bitcast.19), channel_id=1, source_target_pairs={{0,3},{1,4},{2,5},{3,6},{4,7},{5,0},{6,1},{7,2},{8,11},{9,12},{10,... | collective-permute-start | bytes 393224 | tf_op jit(solution)/shard_map/ppermute | solution.py:237
  15.2 9.2 %collective-permute-start.1 = (bf16[128,512]{1,0:T(8,128)(2,1)S(1)}, bf16[128,512]{1,0:T(8,128)(2,1)S(1)}, u32[]{:S(2)}, u32[]{:S(2)}) collective-permute-start(bf16[128,512]{1,0:T(8,128)(2,1)S(1)} %bitcast.20), channel_id=1, source_target_pairs={{0,2},{1,3},{2,4},{3,5},{4,6},{5,7},{6,0},{7,1},{8,10},{9,11},{10,... | collective-permute-start | bytes 393224 | tf_op jit(solution)/shard_map/ppermute | solution.py:237
  15.8 13.3 %collective-permute-start = (bf16[128,512]{1,0:T(8,128)(2,1)S(1)}, bf16[128,512]{1,0:T(8,128)(2,1)S(1)}, u32[]{:S(2)}, u32[]{:S(2)}) collective-permute-start(bf16[128,512]{1,0:T(8,128)(2,1)S(1)} %bitcast.21), channel_id=1, source_target_pairs={{0,1},{1,2},{2,3},{3,4},{4,5},{5,6},{6,7},{7,0},{8,9},{9,10},{10,1... | collective-permute-start | bytes 393224 | tf_op jit(solution)/shard_map/ppermute | solution.py:237
  17.6 18.1 %collective-permute-start.7 = (bf16[128,512]{1,0:T(8,128)(2,1)S(1)}, bf16[128,512]{1,0:T(8,128)(2,1)S(1)}, u32[]{:S(2)}, u32[]{:S(2)}) collective-permute-start(bf16[128,512]{1,0:T(8,128)(2,1)S(1)} %bitcast.23), channel_id=1, source_target_pairs={{0,4},{1,5},{2,6},{3,7},{4,0},{5,1},{6,2},{7,3},{8,12},{9,13},{10,... | collective-permute-start | bytes 393224 | tf_op jit(solution)/shard_map/ppermute | solution.py:237
  20.0 15.8 %collective-permute-start.6 = (bf16[128,512]{1,0:T(8,128)(2,1)S(1)}, bf16[128,512]{1,0:T(8,128)(2,1)S(1)}, u32[]{:S(2)}, u32[]{:S(2)}) collective-permute-start(bf16[128,512]{1,0:T(8,128)(2,1)S(1)} %bitcast.24), channel_id=1, source_target_pairs={{0,3},{1,4},{2,5},{3,6},{4,7},{5,0},{6,1},{7,2},{8,11},{9,12},{10,... | collective-permute-start | bytes 393224 | tf_op jit(solution)/shard_map/ppermute | solution.py:237
  22.3 17.4 %collective-permute-start.5 = (bf16[128,512]{1,0:T(8,128)(2,1)S(1)}, bf16[128,512]{1,0:T(8,128)(2,1)S(1)}, u32[]{:S(2)}, u32[]{:S(2)}) collective-permute-start(bf16[128,512]{1,0:T(8,128)(2,1)S(1)} %bitcast.25), channel_id=1, source_target_pairs={{0,2},{1,3},{2,4},{3,5},{4,6},{5,7},{6,0},{7,1},{8,10},{9,11},{10,... | collective-permute-start | bytes 393224 | tf_op jit(solution)/shard_map/ppermute | solution.py:237
  24.4 16.5 %collective-permute-start.4 = (bf16[128,512]{1,0:T(8,128)(2,1)S(1)}, bf16[128,512]{1,0:T(8,128)(2,1)S(1)}, u32[]{:S(2)}, u32[]{:S(2)}) collective-permute-start(bf16[128,512]{1,0:T(8,128)(2,1)S(1)} %bitcast.26), channel_id=1, source_target_pairs={{0,1},{1,2},{2,3},{3,4},{4,5},{5,6},{6,7},{7,0},{8,9},{9,10},{10,1... | collective-permute-start | bytes 393224 | tf_op jit(solution)/shard_map/ppermute | solution.py:237
  35.7 6.6 %collective-permute-start.8 = (bf16[128,512]{1,0:T(8,128)(2,1)}, bf16[128,512]{1,0:T(8,128)(2,1)S(1)}, u32[]{:S(2)}, u32[]{:S(2)}) collective-permute-start(bf16[128,512]{1,0:T(8,128)(2,1)} %get-tuple-element.25), channel_id=1, source_target_pairs={{0,7},{1,0},{2,1},{3,2},{4,3},{5,4},{6,5},{7,6},{8,15},{9,8},{10,9... | collective-permute-start | bytes 393224 | tf_op jit(solution)/shard_map/ppermute | solution.py:237
  35.8 23.6 %copy-start.10 = (bf16[128,512]{1,0:T(8,128)(2,1)}, bf16[128,512]{1,0:T(8,128)(2,1)S(1)}, u32[]{:S(2)}) copy-start(bf16[128,512]{1,0:T(8,128)(2,1)S(1)} %collective-permute-done.7.v4) | copy-start | bytes 393220
  35.8 13.6 %collective-permute-start.9 = (bf16[128,512]{1,0:T(8,128)(2,1)}, bf16[128,512]{1,0:T(8,128)(2,1)S(1)}, u32[]{:S(2)}, u32[]{:S(2)}) collective-permute-start(bf16[128,512]{1,0:T(8,128)(2,1)} %get-tuple-element.26), channel_id=1, source_target_pairs={{0,6},{1,7},{2,0},{3,1},{4,2},{5,3},{6,4},{7,5},{8,14},{9,15},{10,... | collective-permute-start | bytes 393224 | tf_op jit(solution)/shard_map/ppermute | solution.py:237
  35.9 23.5 %copy-start.11 = (bf16[128,512]{1,0:T(8,128)(2,1)}, bf16[128,512]{1,0:T(8,128)(2,1)S(1)}, u32[]{:S(2)}) copy-start(bf16[128,512]{1,0:T(8,128)(2,1)S(1)} %collective-permute-done.6.v3) | copy-start | bytes 393220
  35.9 13.5 %collective-permute-start.10 = (bf16[128,512]{1,0:T(8,128)(2,1)}, bf16[128,512]{1,0:T(8,128)(2,1)S(1)}, u32[]{:S(2)}, u32[]{:S(2)}) collective-permute-start(bf16[128,512]{1,0:T(8,128)(2,1)} %get-tuple-element.27), channel_id=1, source_target_pairs={{0,5},{1,6},{2,7},{3,0},{4,1},{5,2},{6,3},{7,4},{8,13},{9,14},{10,... | collective-permute-start | bytes 393224 | tf_op jit(solution)/shard_map/ppermute | solution.py:237
  39.7 19.7 %copy-start.12 = (bf16[128,512]{1,0:T(8,128)(2,1)}, bf16[128,512]{1,0:T(8,128)(2,1)S(1)}, u32[]{:S(2)}) copy-start(bf16[128,512]{1,0:T(8,128)(2,1)S(1)} %collective-permute-done.5.v2) | copy-start | bytes 393220
  39.7 9.7 %collective-permute-start.11 = (bf16[128,512]{1,0:T(8,128)(2,1)}, bf16[128,512]{1,0:T(8,128)(2,1)S(1)}, u32[]{:S(2)}, u32[]{:S(2)}) collective-permute-start(bf16[128,512]{1,0:T(8,128)(2,1)} %get-tuple-element.28), channel_id=1, source_target_pairs={{0,4},{1,5},{2,6},{3,7},{4,0},{5,1},{6,2},{7,3},{8,12},{9,13},{10,... | collective-permute-start | bytes 393224 | tf_op jit(solution)/shard_map/ppermute | solution.py:237
  50.4 7.2 %collective-permute-start.14 = (bf16[128,512]{1,0:T(8,128)(2,1)S(1)}, bf16[128,512]{1,0:T(8,128)(2,1)S(1)}, u32[]{:S(2)}, u32[]{:S(2)}) collective-permute-start(bf16[128,512]{1,0:T(8,128)(2,1)S(1)} %add_convert_fusion.2.refs_0_), channel_id=1, source_target_pairs={{0,145},{1,144},{2,147},{3,146},{4,149},{5,148},{6,151},{7,150},{8... | collective-permute-start | bytes 393224 | tf_op jit(solution)/shard_map/ppermute | solution.py:233
  52.6 5.0 %collective-permute-start.13 = (bf16[128,512]{1,0:T(8,128)(2,1)S(1)}, bf16[128,512]{1,0:T(8,128)(2,1)S(1)}, u32[]{:S(2)}, u32[]{:S(2)}) collective-permute-start(bf16[128,512]{1,0:T(8,128)(2,1)S(1)} %add_convert_fusion.2.refs_0_), channel_id=1, source_target_pairs={{0,16},{1,17},{2,18},{3,19},{4,20},{5,21},{6,22},{7,23},{8,24},{9,... | collective-permute-start | bytes 393224 | tf_op jit(solution)/shard_map/ppermute | solution.py:233
  53.2 6.2 %collective-permute-start.12 = (bf16[128,512]{1,0:T(8,128)(2,1)S(1)}, bf16[128,512]{1,0:T(8,128)(2,1)S(1)}, u32[]{:S(2)}, u32[]{:S(2)}) collective-permute-start(bf16[128,512]{1,0:T(8,128)(2,1)S(1)} %add_convert_fusion.2.refs_0_), channel_id=1, source_target_pairs={{0,129},{1,128},{2,131},{3,130},{4,133},{5,132},{6,135},{7,134},{8... | collective-permute-start | bytes 393224 | tf_op jit(solution)/shard_map/ppermute | solution.py:233
  55.2 4.2 %collective-permute-start.15 = (bf16[128,512]{1,0:T(8,128)(2,1)S(1)}, bf16[128,512]{1,0:T(8,128)(2,1)S(1)}, u32[]{:S(2)}, u32[]{:S(2)}) collective-permute-start(bf16[128,512]{1,0:T(8,128)(2,1)S(1)} %add_convert_fusion.2.refs_0_), channel_id=1, source_target_pairs={{0,8},{1,9},{2,10},{3,11},{4,12},{5,13},{6,14},{7,15},{8,0},{9,1},... | collective-permute-start | bytes 393224 | tf_op jit(solution)/shard_map/ppermute | solution.py:233
  57.6 1.8 %collective-permute-start.18 = (bf16[128,512]{1,0:T(8,128)(2,1)S(1)}, bf16[128,512]{1,0:T(8,128)(2,1)S(1)}, u32[]{:S(2)}, u32[]{:S(2)}) collective-permute-start(bf16[128,512]{1,0:T(8,128)(2,1)S(1)} %collective-permute-done.14.refs_3_), channel_id=1, source_target_pairs={{0,8},{1,9},{2,10},{3,11},{4,12},{5,13},{6,14},{7,15},{8,0},{9,1},... | collective-permute-start | bytes 393224 | tf_op jit(solution)/shard_map/ppermute | solution.py:233
  57.6 1.8 %collective-permute-start.17 = (bf16[128,512]{1,0:T(8,128)(2,1)S(1)}, bf16[128,512]{1,0:T(8,128)(2,1)S(1)}, u32[]{:S(2)}, u32[]{:S(2)}) collective-permute-start(bf16[128,512]{1,0:T(8,128)(2,1)S(1)} %collective-permute-done.13.refs_2_), channel_id=1, source_target_pairs={{0,8},{1,9},{2,10},{3,11},{4,12},{5,13},{6,14},{7,15},{8,0},{9,1},... | collective-permute-start | bytes 393224 | tf_op jit(solution)/shard_map/ppermute | solution.py:233
  59.4 1.3 %collective-permute-start.16 = (bf16[128,512]{1,0:T(8,128)(2,1)S(1)}, bf16[128,512]{1,0:T(8,128)(2,1)S(1)}, u32[]{:S(2)}, u32[]{:S(2)}) collective-permute-start(bf16[128,512]{1,0:T(8,128)(2,1)S(1)} %collective-permute-done.12.refs_1_), channel_id=1, source_target_pairs={{0,8},{1,9},{2,10},{3,11},{4,12},{5,13},{6,14},{7,15},{8,0},{9,1},... | collective-permute-start | bytes 393224 | tf_op jit(solution)/shard_map/ppermute | solution.py:233
  62.2 14.3 %collective-permute-start.23 = (bf16[256,512]{1,0:T(8,128)(2,1)S(1)}, bf16[256,512]{1,0:T(8,128)(2,1)S(1)}, u32[]{:S(2)}, u32[]{:S(2)}) collective-permute-start(bf16[256,512]{1,0:T(8,128)(2,1)S(1)} %get-tuple-element.37), channel_id=1, source_target_pairs={{0,2},{1,3},{2,4},{3,5},{4,6},{5,7},{6,0},{7,1},{8,10},{9,11},{10,... | collective-permute-start | bytes 786440 | tf_op jit(solution)/shard_map/ppermute | solution.py:233
  62.5 14.0 %collective-permute-start.24 = (bf16[256,512]{1,0:T(8,128)(2,1)S(1)}, bf16[256,512]{1,0:T(8,128)(2,1)S(1)}, u32[]{:S(2)}, u32[]{:S(2)}) collective-permute-start(bf16[256,512]{1,0:T(8,128)(2,1)S(1)} %get-tuple-element.38), channel_id=1, source_target_pairs={{0,4},{1,5},{2,6},{3,7},{4,0},{5,1},{6,2},{7,3},{8,12},{9,13},{10,... | collective-permute-start | bytes 786440 | tf_op jit(solution)/shard_map/ppermute | solution.py:233
  65.4 12.4 %collective-permute-start.25 = (bf16[256,512]{1,0:T(8,128)(2,1)S(1)}, bf16[256,512]{1,0:T(8,128)(2,1)S(1)}, u32[]{:S(2)}, u32[]{:S(2)}) collective-permute-start(bf16[256,512]{1,0:T(8,128)(2,1)S(1)} %get-tuple-element.39), channel_id=1, source_target_pairs={{0,6},{1,7},{2,0},{3,1},{4,2},{5,3},{6,4},{7,5},{8,14},{9,15},{10,... | collective-permute-start | bytes 786440 | tf_op jit(solution)/shard_map/ppermute | solution.py:233
  76.5 26.7 %copy-start.3 = (f32[128,512]{1,0:T(8,128)S(1)}, f32[128,512]{1,0:T(8,128)}, u32[]{:S(2)}) copy-start(f32[128,512]{1,0:T(8,128)} %get-tuple-element.31) | copy-start | bytes 786436
  78.7 25.2 %all-to-all-start.1 = ((bf16[8,32,512]{2,1,0:T(8,128)(2,1)}), bf16[8,32,512]{2,1,0:T(8,128)(2,1)S(1)}, u32[]{:S(2)}, u32[]{:S(2)}) async-start(bf16[8,32,512]{2,1,0:T(8,128)(2,1)} %bitcast.8), calls=%async_computation.1 | async-start | bytes 524288 | tf_op jit(solution)/shard_map/all_to_all | solution.py:281
  87.2 7.4 %collective-permute-start.19 = (bf16[128,512]{1,0:T(8,128)(2,1)S(1)}, bf16[128,512]{1,0:T(8,128)(2,1)S(1)}, u32[]{:S(2)}, u32[]{:S(2)}) collective-permute-start(bf16[128,512]{1,0:T(8,128)(2,1)S(1)} %copy-done.17), channel_id=1, source_target_pairs={{0,7},{1,0},{2,1},{3,2},{4,3},{5,4},{6,5},{7,6},{8,15},{9,8},{10,9... | collective-permute-start | bytes 393224 | tf_op jit(solution)/shard_map/ppermute | solution.py:237
  89.1 14.1 %collective-permute-start.20 = (bf16[128,512]{1,0:T(8,128)(2,1)S(1)}, bf16[128,512]{1,0:T(8,128)(2,1)S(1)}, u32[]{:S(2)}, u32[]{:S(2)}) collective-permute-start(bf16[128,512]{1,0:T(8,128)(2,1)S(1)} %copy-done.16), channel_id=1, source_target_pairs={{0,6},{1,7},{2,0},{3,1},{4,2},{5,3},{6,4},{7,5},{8,14},{9,15},{10,... | collective-permute-start | bytes 393224 | tf_op jit(solution)/shard_map/ppermute | solution.py:237
  89.9 13.2 %collective-permute-start.21 = (bf16[128,512]{1,0:T(8,128)(2,1)S(1)}, bf16[128,512]{1,0:T(8,128)(2,1)S(1)}, u32[]{:S(2)}, u32[]{:S(2)}) collective-permute-start(bf16[128,512]{1,0:T(8,128)(2,1)S(1)} %copy-done.15), channel_id=1, source_target_pairs={{0,5},{1,6},{2,7},{3,0},{4,1},{5,2},{6,3},{7,4},{8,13},{9,14},{10,... | collective-permute-start | bytes 393224 | tf_op jit(solution)/shard_map/ppermute | solution.py:237
  91.3 11.9 %collective-permute-start.22 = (bf16[128,512]{1,0:T(8,128)(2,1)S(1)}, bf16[128,512]{1,0:T(8,128)(2,1)S(1)}, u32[]{:S(2)}, u32[]{:S(2)}) collective-permute-start(bf16[128,512]{1,0:T(8,128)(2,1)S(1)} %copy-done.14), channel_id=1, source_target_pairs={{0,4},{1,5},{2,6},{3,7},{4,0},{5,1},{6,2},{7,3},{8,12},{9,13},{10,... | collective-permute-start | bytes 393224 | tf_op jit(solution)/shard_map/ppermute | solution.py:237
  (14 other events, 123.0 us)

commit v3 on v2

--- a/solution.py
+++ b/solution.py
@@ -81,7 +81,8 @@
         ref[:, cols] = grad[n * ROWS : (n + 1) * ROWS].astype(ref.dtype)
 
 
-def value_kernel(lengths, q, do, k0, k1, k2, k3, k4, own, s1, s2, s3, s4, stats, bias, prob):
+def value_kernel(lengths, value, q, do, k0, k1, k2, k3, k4, passed, own, s1, s2, s3, s4, stats, bias, prob):
+    passed[...] = value[...]
     fill_bias(lengths, bias)
     mask = lower()
     for group in range(GROUPS):
@@ -134,17 +135,17 @@
 SCRATCH = [pltpu.VMEM((NEAR * ROWS, 2 * ROWS), F32), pltpu.VMEM((2, 5 * ROWS, GROUP * ROWS), BF16)]
 
 
-def value_call(lengths, q, do, keys):
+def value_call(lengths, value, q, do, keys):
     return pl.pallas_call(
         value_kernel,
-        in_specs=[SMEM] + [VMEM] * 7,
-        out_specs=[VMEM] * 6,
-        out_shape=TERMS + [STATS],
+        in_specs=[SMEM] + [VMEM] * 8,
+        out_specs=[VMEM] * 7,
+        out_shape=[sds(value.shape, BF16)] + TERMS + [STATS],
         scratch_shapes=SCRATCH,
-        compiler_params=params(58),
-        cost_estimate=pl.CostEstimate(flops=3 * 10**10, bytes_accessed=4 * 10**6, transcendentals=2 * 10**6),
+        compiler_params=params(24),
+        cost_estimate=pl.CostEstimate(flops=15 * 10**10, bytes_accessed=4 * 10**6, transcendentals=2 * 10**6),
         name="value_grad",
-    )(lengths, q, do, *keys)
+    )(lengths, value, q, do, *keys)
 
 
 def score_call(lengths, q, do, keys, values, stats):
@@ -154,7 +155,7 @@
         out_specs=[VMEM] * 6,
         out_shape=[sds((ROWS, GROUPS * GROUP * HD), BF16)] + TERMS,
         scratch_shapes=SCRATCH,
-        compiler_params=params(58),
+        compiler_params=params(24),
         cost_estimate=pl.CostEstimate(flops=4 * 10**10, bytes_accessed=4 * 10**6, transcendentals=2 * 10**6),
         name="score_grad",
     )(lengths, q, do, *keys, *values, stats)
@@ -191,28 +192,28 @@
     )(x)
 
 
-def weight_kernel(first, inputs, *refs):
-    grads, outs = refs[:8], refs[8:]
+def weight_kernel(inputs, *refs):
+    grads, outs = refs[:8], refs[-4:]
     dp, ctx = lax.axis_index("dp"), lax.axis_index("ctx")
     core, high, low, x = dp % 2, dp // 16, dp // 2 % 2, ctx // 2
     members = [(core ^ c) * 4 + (high ^ h) * 2 + (low ^ n) for c in range(2) for n in range(2) for h in range(2)]
     right = jnp.concatenate([ref[...] for ref in grads], axis=0)
     for n, out in enumerate(outs):
-        left = jnp.concatenate([inputs[member, (x + first + n) % 4] for member in members], axis=1)
+        left = jnp.concatenate([inputs[member, (x + n) % 4] for member in members], axis=1)
         out[...] = dot(left, right, (1, 0)).astype(out.dtype)
 
 
-def weight_call(first, count, inputs, grads, dtype):
-    width = grads[0].shape[1]
-    return pl.pallas_call(
-        functools.partial(weight_kernel, first),
-        in_specs=[VMEM] * 9,
-        out_specs=[VMEM] * count,
-        out_shape=[sds((256, width), dtype)] * count,
-        compiler_params=params(24),
-        cost_estimate=pl.CostEstimate(flops=3 * 10**8 * count, bytes_accessed=10**6 * count, transcendentals=0),
+def weight_call(inputs, grads, others):
+    shape = (256, grads[0].shape[1])
+    return pl.pallas_call(
+        weight_kernel,
+        in_specs=[VMEM] * (9 + len(others)),
+        out_specs=[VMEM] * 4,
+        out_shape=[sds(shape, F32)] + [sds(shape, BF16)] * 3,
+        compiler_params=params(24),
+        cost_estimate=pl.CostEstimate(flops=10**6, bytes_accessed=10**4, transcendentals=0),
         name="weight_grad",
-    )(inputs, *grads)
+    )(inputs, *grads, *others)
 
 
 def place(device):
@@ -246,7 +247,6 @@
     key, value = key_heads[0], value_heads[0]
     tokens = lax.axis_size("dp") * lax.axis_size("ctx") * q.shape[0]
     keys = [key] + [ring(key, d) for d in range(1, 5)]
-    values = [value] + [ring(value, d) for d in range(1, 5)]
     dealt = deal_call(layer_inputs[0])
     members = [
         [device(x, y, z, core) for core in range(2) for y in ys for z in (z0, z0 + 1)]
@@ -256,16 +256,16 @@
     ]
     inputs = lax.all_to_all(dealt, ("dp", "ctx"), 0, 0, axis_index_groups=members)
 
-    *value_terms, stats = value_call(doc_lengths, q, do, keys)
+    passed, *value_terms, stats = value_call(doc_lengths, value, q, do, keys)
+    values = [value] + [ring(passed, d) for d in range(1, 5)]
     arrived = [ring(term, -d) for d, term in enumerate(value_terms[1:], 1)]
-    value_grad = (after(value_terms[0], *values) + sum(term.astype(F32) for term in arrived)).astype(BF16)
+    value_grad = (value_terms[0] + sum(term.astype(F32) for term in arrived)).astype(BF16)
 
     flips = ((True, False), (False, True), (True, True))
     grads = [value_grad] + [move(value_grad, flip_y=y, flip_z=z) for y, z in flips]
     grads += [move(grad, flip_core=True) for grad in grads]
-    away = weight_call(1, 3, inputs, grads, BF16)
+    total, *away = weight_call(inputs, grads, values[1:])
     across = [move(term, dx=d) for d, term in enumerate(away, 1)]
-    (total,) = weight_call(0, 1, inputs, grads, F32)
 
     query_grad, *key_terms = score_call(doc_lengths, q, do, keys, values, after(stats, total))
     arrived = [ring(term, -d) for d, term in enumerate(key_terms[1:], 1)]

time: 105 us -> 98 us (0.933)
  the two profiles are of different devices: /device:TPU:6 before, /device:TPU:8 now
where the time goes in v3:
time: 98 us; the launch traced here: 97.7 us
  starting transfers between devices  51.9 us (53%)
  waiting for transfers between devices  20.9 us (21%)
  Pallas kernels  20.1 us (21%)
  other arithmetic  2.36 us (2%)
  local copies, waits for them, and re-layouts  1.62 us (2%)
    ppermute x16, starting transfers between devices, ring(): lax.ppermute(array, 'ctx', [(n, (n + distance) % 8) for n in range(8)])  28 us
    ppermute x16, waiting for transfers between devices, ring(): lax.ppermute(array, 'ctx', [(n, (n + distance) % 8) for n in range(8)])  12.5 us
    all_to_all x1, starting transfers between devices, shards(): lax.all_to_all(total.reshape(8, 32, -1), ('dp', 'ctx'), 0, 0, axis_index_...  10.3 us
    pallas_call x1, Pallas kernels, score_call(): pl.pallas_call(score_kernel, in_specs=[SMEM] + [VMEM] * 13, out_specs=[VM...  9.04 us
    ppermute x10, starting transfers between devices, move(): return lax.ppermute(array, ('dp', 'ctx'), pairs)  8.71 us
    ppermute x10, waiting for transfers between devices, move(): return lax.ppermute(array, ('dp', 'ctx'), pairs)  8.41 us
    all_to_all x1, starting transfers between devices, shards(): lax.all_to_all(dealt, ('dp', 'ctx'), 0, 0, axis_index_groups=members)  4.95 us
    pallas_call x1, Pallas kernels, value_call(): pl.pallas_call(value_kernel, in_specs=[SMEM] + [VMEM] * 8, out_specs=[VME...  4.13 us
  transfers between devices with their start and end apart: 28, of which 10 were waited for; matrix products, arithmetic and copies ran while one was open for 1% of the time, Pallas kernels for 18%

profile of v3, /device:TPU:8, one launch (start us, length us, event | category | flops | bytes accessed | tf_op | source)
XLA Modules:
  0.0 97.7 jit_solution(53607316260722585)
XLA Ops:
  0.6 1.5 %collective-permute-start = (bf16[128,512]{1,0:T(8,128)(2,1)}, bf16[128,512]{1,0:T(8,128)(2,1)S(1)}, u32[]{:S(2)}, u32[]{:S(2)}) collective-permute-start(bf16[128,512]{1,0:T(8,128)(2,1)} %bitcast.16), channel_id=1, source_target_pairs={{0,1},{1,2},{2,3},{3,4},{4,5},{5,6},{6,7},{7,0},{8,9},{9,10},{10,1... | collective-permute-start | bytes 393224 | tf_op jit(solution)/shard_map/ppermute | solution.py:238
  2.1 1.5 %collective-permute-start.1 = (bf16[128,512]{1,0:T(8,128)(2,1)}, bf16[128,512]{1,0:T(8,128)(2,1)S(1)}, u32[]{:S(2)}, u32[]{:S(2)}) collective-permute-start(bf16[128,512]{1,0:T(8,128)(2,1)} %bitcast.17), channel_id=1, source_target_pairs={{0,2},{1,3},{2,4},{3,5},{4,6},{5,7},{6,0},{7,1},{8,10},{9,11},{10,... | collective-permute-start | bytes 393224 | tf_op jit(solution)/shard_map/ppermute | solution.py:238
  3.6 2.8 %collective-permute-start.2 = (bf16[128,512]{1,0:T(8,128)(2,1)}, bf16[128,512]{1,0:T(8,128)(2,1)S(1)}, u32[]{:S(2)}, u32[]{:S(2)}) collective-permute-start(bf16[128,512]{1,0:T(8,128)(2,1)} %bitcast.18), channel_id=1, source_target_pairs={{0,3},{1,4},{2,5},{3,6},{4,7},{5,0},{6,1},{7,2},{8,11},{9,12},{10,... | collective-permute-start | bytes 393224 | tf_op jit(solution)/shard_map/ppermute | solution.py:238
  7.2 1.6 %copy-done.1 = bf16[1,128,8192]{2,1,0:T(8,128)(2,1)S(1)} copy-done((bf16[1,128,8192]{2,1,0:T(8,128)(2,1)S(1)}, bf16[1,128,8192]{2,1,0:T(8,128)(2,1)}, u32[]{:S(2)}) %copy-start.1) | copy-done | bytes 2097176
  8.8 4.1 %deal_inputs.1 = bf16[8,4,256,128]{3,2,1,0:T(8,128)(2,1)} custom-call(bf16[128,8192]{1,0:T(8,128)(2,1)S(1)} %bitcast.11), custom_call_target="tpu_custom_call" | custom-call | flops 2000000000 | bytes 4000000 | tf_op jit(solution)/shard_map/deal_inputs/pallas_call | solution.py:182
  12.9 5.0 %all-to-all-start = ((bf16[8,4,256,128]{3,2,1,0:T(8,128)(2,1)}), bf16[8,4,256,128]{3,2,1,0:T(8,128)(2,1)}, u32[]{:S(2)}, u32[]{:S(2)}) async-start(bf16[8,4,256,128]{3,2,1,0:T(8,128)(2,1)} %deal_inputs.1), calls=%async_computation | async-start | bytes 4194304 | tf_op jit(solution)/shard_map/all_to_all | solution.py:257
  17.9 4.1 %value_grad.1 = (bf16[128,512]{1,0:T(8,128)(2,1)S(1)}, f32[128,512]{1,0:T(8,128)S(1)}, bf16[128,512]{1,0:T(8,128)(2,1)S(1)}, bf16[128,512]{1,0:T(8,128)(2,1)S(1)...) custom-call(s32[1,8]{1,0:T(1,128)S(1)} %copy-done.7, ...), custom_call_target="tpu_custom_call" | custom-call | flops 149999992832 | bytes 4000000 | tf_op jit(solution)/shard_map/value_grad/pallas_call | solution.py:139
  22.0 2.4 %collective-permute-start.11 = (bf16[128,512]{1,0:T(8,128)(2,1)S(1)}, bf16[128,512]{1,0:T(8,128)(2,1)S(1)}, u32[]{:S(2)}, u32[]{:S(2)}) collective-permute-start(bf16[128,512]{1,0:T(8,128)(2,1)S(1)} %get-tuple-element.29), channel_id=1, source_target_pairs={{0,4},{1,5},{2,6},{3,7},{4,0},{5,1},{6,2},{7,3},{8,12},{9,13},{10,... | collective-permute-start | bytes 393224 | tf_op jit(solution)/shard_map/ppermute | solution.py:238
  24.4 2.6 %collective-permute-start.10 = (bf16[128,512]{1,0:T(8,128)(2,1)S(1)}, bf16[128,512]{1,0:T(8,128)(2,1)S(1)}, u32[]{:S(2)}, u32[]{:S(2)}) collective-permute-start(bf16[128,512]{1,0:T(8,128)(2,1)S(1)} %get-tuple-element.28), channel_id=1, source_target_pairs={{0,5},{1,6},{2,7},{3,0},{4,1},{5,2},{6,3},{7,4},{8,13},{9,14},{10,... | collective-permute-start | bytes 393224 | tf_op jit(solution)/shard_map/ppermute | solution.py:238
  27.0 1.7 %collective-permute-start.8 = (bf16[128,512]{1,0:T(8,128)(2,1)S(1)}, bf16[128,512]{1,0:T(8,128)(2,1)S(1)}, u32[]{:S(2)}, u32[]{:S(2)}) collective-permute-start(bf16[128,512]{1,0:T(8,128)(2,1)S(1)} %get-tuple-element.26), channel_id=1, source_target_pairs={{0,7},{1,0},{2,1},{3,2},{4,3},{5,4},{6,5},{7,6},{8,15},{9,8},{10,9... | collective-permute-start | bytes 393224 | tf_op jit(solution)/shard_map/ppermute | solution.py:238
  28.7 1.3 %collective-permute-start.4 = (bf16[128,512]{1,0:T(8,128)(2,1)S(1)}, bf16[128,512]{1,0:T(8,128)(2,1)S(1)}, u32[]{:S(2)}, u32[]{:S(2)}) collective-permute-start(bf16[128,512]{1,0:T(8,128)(2,1)S(1)} %get-tuple-element.23), channel_id=1, source_target_pairs={{0,1},{1,2},{2,3},{3,4},{4,5},{5,6},{6,7},{7,0},{8,9},{9,10},{10,1... | collective-permute-start | bytes 393224 | tf_op jit(solution)/shard_map/ppermute | solution.py:238
  29.9 2.0 %collective-permute-start.5 = (bf16[128,512]{1,0:T(8,128)(2,1)S(1)}, bf16[128,512]{1,0:T(8,128)(2,1)S(1)}, u32[]{:S(2)}, u32[]{:S(2)}) collective-permute-start(bf16[128,512]{1,0:T(8,128)(2,1)S(1)} %get-tuple-element.23), channel_id=1, source_target_pairs={{0,2},{1,3},{2,4},{3,5},{4,6},{5,7},{6,0},{7,1},{8,10},{9,11},{10,... | collective-permute-start | bytes 393224 | tf_op jit(solution)/shard_map/ppermute | solution.py:238
  31.9 1.2 %collective-permute-done.10 = bf16[128,512]{1,0:T(8,128)(2,1)S(1)} collective-permute-done((bf16[128,512]{1,0:T(8,128)(2,1)S(1)}, bf16[128,512]{1,0:T(8,128)(2,1)S(1)}, u32[]{:S(2)}, u32[]{:S(2)}) %collective-permute-start.10) | collective-permute-done | bytes 131104 | tf_op jit(solution)/shard_map/ppermute | solution.py:238
  33.1 2.5 %collective-permute-start.6 = (bf16[128,512]{1,0:T(8,128)(2,1)S(1)}, bf16[128,512]{1,0:T(8,128)(2,1)S(1)}, u32[]{:S(2)}, u32[]{:S(2)}) collective-permute-start(bf16[128,512]{1,0:T(8,128)(2,1)S(1)} %get-tuple-element.23), channel_id=1, source_target_pairs={{0,3},{1,4},{2,5},{3,6},{4,7},{5,0},{6,1},{7,2},{8,11},{9,12},{10,... | collective-permute-start | bytes 393224 | tf_op jit(solution)/shard_map/ppermute | solution.py:238
  35.6 3.3 %collective-permute-done.8 = bf16[128,512]{1,0:T(8,128)(2,1)S(1)} collective-permute-done((bf16[128,512]{1,0:T(8,128)(2,1)S(1)}, bf16[128,512]{1,0:T(8,128)(2,1)S(1)}, u32[]{:S(2)}, u32[]{:S(2)}) %collective-permute-start.8) | collective-permute-done | bytes 131104 | tf_op jit(solution)/shard_map/ppermute | solution.py:238
  39.0 2.4 %collective-permute-start.12 = (bf16[128,512]{1,0:T(8,128)(2,1)S(1)}, bf16[128,512]{1,0:T(8,128)(2,1)S(1)}, u32[]{:S(2)}, u32[]{:S(2)}) collective-permute-start(bf16[128,512]{1,0:T(8,128)(2,1)S(1)} %add_convert_fusion.2.refs_0_), channel_id=1, source_target_pairs={{0,129},{1,128},{2,131},{3,130},{4,133},{5,132},{6,135},{7,134},{8... | collective-permute-start | bytes 393224 | tf_op jit(solution)/shard_map/ppermute | solution.py:234
  41.4 1.5 %collective-permute-start.13 = (bf16[128,512]{1,0:T(8,128)(2,1)S(1)}, bf16[128,512]{1,0:T(8,128)(2,1)S(1)}, u32[]{:S(2)}, u32[]{:S(2)}) collective-permute-start(bf16[128,512]{1,0:T(8,128)(2,1)S(1)} %add_convert_fusion.2.refs_0_), channel_id=1, source_target_pairs={{0,16},{1,17},{2,18},{3,19},{4,20},{5,21},{6,22},{7,23},{8,24},{9,... | collective-permute-start | bytes 393224 | tf_op jit(solution)/shard_map/ppermute | solution.py:234
  43.3 3.5 %collective-permute-start.7 = (bf16[128,512]{1,0:T(8,128)(2,1)S(1)}, bf16[128,512]{1,0:T(8,128)(2,1)S(1)}, u32[]{:S(2)}, u32[]{:S(2)}) collective-permute-start(bf16[128,512]{1,0:T(8,128)(2,1)S(1)} %get-tuple-element.23), channel_id=1, source_target_pairs={{0,4},{1,5},{2,6},{3,7},{4,0},{5,1},{6,2},{7,3},{8,12},{9,13},{10,... | collective-permute-start | bytes 393224 | tf_op jit(solution)/shard_map/ppermute | solution.py:238
  46.7 1.0 collective-permute-done.12.refs_1_
  48.2 1.9 %collective-permute-done.14.refs_3_ = bf16[128,512]{1,0:T(8,128)(2,1)S(1)} collective-permute-done((bf16[128,512]{1,0:T(8,128)(2,1)S(1)}, bf16[128,512]{1,0:T(8,128)(2,1)S(1)}, u32[]{:S(2)}, u32[]{:S(2)}) %collective-permute-start.14) | collective-permute-done | bytes 131104 | tf_op jit(solution)/shard_map/ppermute | solution.py:234
  50.1 1.3 %collective-permute-done.18.refs_7_ = bf16[128,512]{1,0:T(8,128)(2,1)S(1)} collective-permute-done((bf16[128,512]{1,0:T(8,128)(2,1)S(1)}, bf16[128,512]{1,0:T(8,128)(2,1)S(1)}, u32[]{:S(2)}, u32[]{:S(2)}) %collective-permute-start.18) | collective-permute-done | bytes 131104 | tf_op jit(solution)/shard_map/ppermute | solution.py:234
  51.4 2.9 %weight_grad.1 = (f32[256,512]{1,0:T(8,128)S(1)}, bf16[256,512]{1,0:T(8,128)(2,1)S(1)}, bf16[256,512]{1,0:T(8,128)(2,1)S(1)}, bf16[256,512]{1,0:T(8,128)(2,1)S(1)}) custom-call(bf16[8,4,256,128]{3,2,1,0:T(8,128)(2,1)} %all-to-all-done.inputs, bf16[128,512]{1,0:T(8,128)(2,1)S(1)} %add_convert_fusion.2.refs_0_, ...), custom_call_target="tpu_custom_call" | custom-call | flops 1000000 | bytes 10000 | tf_op jit(solution)/shard_map/weight_grad/pallas_call | solution.py:208
  54.4 2.0 %collective-permute-start.25 = (bf16[256,512]{1,0:T(8,128)(2,1)S(1)}, bf16[256,512]{1,0:T(8,128)(2,1)S(1)}, u32[]{:S(2)}, u32[]{:S(2)}) collective-permute-start(bf16[256,512]{1,0:T(8,128)(2,1)S(1)} %get-tuple-element.41), channel_id=1, source_target_pairs={{0,6},{1,7},{2,0},{3,1},{4,2},{5,3},{6,4},{7,5},{8,14},{9,15},{10,... | collective-permute-start | bytes 786440 | tf_op jit(solution)/shard_map/ppermute | solution.py:234
  56.4 1.9 %collective-permute-start.24 = (bf16[256,512]{1,0:T(8,128)(2,1)S(1)}, bf16[256,512]{1,0:T(8,128)(2,1)S(1)}, u32[]{:S(2)}, u32[]{:S(2)}) collective-permute-start(bf16[256,512]{1,0:T(8,128)(2,1)S(1)} %get-tuple-element.40), channel_id=1, source_target_pairs={{0,4},{1,5},{2,6},{3,7},{4,0},{5,1},{6,2},{7,3},{8,12},{9,13},{10,... | collective-permute-start | bytes 786440 | tf_op jit(solution)/shard_map/ppermute | solution.py:234
  58.3 9.0 %score_grad.1 = (bf16[128,4096]{1,0:T(8,128)(2,1)}, f32[128,512]{1,0:T(8,128)S(1)}, bf16[128,512]{1,0:T(8,128)(2,1)S(1)}, bf16[128,512]{1,0:T(8,128)(2,1)S(1)}, ...) custom-call(s32[1,8]{1,0:T(1,128)S(1)} %copy-done.7, bf16[128,4096]{1,0:T(8,128)(2,1)S(1)} %bitcast.13, ...), custom_call_target="tpu_custom_call" | custom-call | flops 40000000000 | bytes 4000000 | tf_op jit(solution)/shard_map/score_grad/pallas_call | solution.py:152
  67.9 3.7 %collective-permute-done.23 = bf16[256,512]{1,0:T(8,128)(2,1)S(1)} collective-permute-done((bf16[256,512]{1,0:T(8,128)(2,1)S(1)}, bf16[256,512]{1,0:T(8,128)(2,1)S(1)}, u32[]{:S(2)}, u32[]{:S(2)}) %collective-permute-start.23) | collective-permute-done | bytes 262176 | tf_op jit(solution)/shard_map/ppermute | solution.py:234
  72.5 10.3 %all-to-all-start.1 = ((bf16[8,32,512]{2,1,0:T(8,128)(2,1)}), bf16[8,32,512]{2,1,0:T(8,128)(2,1)S(1)}, u32[]{:S(2)}, u32[]{:S(2)}) async-start(bf16[8,32,512]{2,1,0:T(8,128)(2,1)} %bitcast.8), calls=%async_computation.1 | async-start | bytes 524288 | tf_op jit(solution)/shard_map/all_to_all | solution.py:281
  82.7 1.7 %collective-permute-start.22 = (bf16[128,512]{1,0:T(8,128)(2,1)S(1)}, bf16[128,512]{1,0:T(8,128)(2,1)S(1)}, u32[]{:S(2)}, u32[]{:S(2)}) collective-permute-start(bf16[128,512]{1,0:T(8,128)(2,1)S(1)} %get-tuple-element.37), channel_id=1, source_target_pairs={{0,4},{1,5},{2,6},{3,7},{4,0},{5,1},{6,2},{7,3},{8,12},{9,13},{10,... | collective-permute-start | bytes 393224 | tf_op jit(solution)/shard_map/ppermute | solution.py:238
  84.5 1.0 %collective-permute-start.21 = (bf16[128,512]{1,0:T(8,128)(2,1)S(1)}, bf16[128,512]{1,0:T(8,128)(2,1)S(1)}, u32[]{:S(2)}, u32[]{:S(2)}) collective-permute-start(bf16[128,512]{1,0:T(8,128)(2,1)S(1)} %get-tuple-element.36), channel_id=1, source_target_pairs={{0,5},{1,6},{2,7},{3,0},{4,1},{5,2},{6,3},{7,4},{8,13},{9,14},{10,... | collective-permute-start | bytes 393224 | tf_op jit(solution)/shard_map/ppermute | solution.py:238
  86.3 2.1 %collective-permute-start.19 = (bf16[128,512]{1,0:T(8,128)(2,1)S(1)}, bf16[128,512]{1,0:T(8,128)(2,1)S(1)}, u32[]{:S(2)}, u32[]{:S(2)}) collective-permute-start(bf16[128,512]{1,0:T(8,128)(2,1)S(1)} %get-tuple-element.34), channel_id=1, source_target_pairs={{0,7},{1,0},{2,1},{3,2},{4,3},{5,4},{6,5},{7,6},{8,15},{9,8},{10,9... | collective-permute-start | bytes 393224 | tf_op jit(solution)/shard_map/ppermute | solution.py:238
  89.2 4.4 %collective-permute-done.21 = bf16[128,512]{1,0:T(8,128)(2,1)S(1)} collective-permute-done((bf16[128,512]{1,0:T(8,128)(2,1)S(1)}, bf16[128,512]{1,0:T(8,128)(2,1)S(1)}, u32[]{:S(2)}, u32[]{:S(2)}) %collective-permute-start.21) | collective-permute-done | bytes 131104 | tf_op jit(solution)/shard_map/ppermute | solution.py:238
  93.6 2.7 %collective-permute-done.19 = bf16[128,512]{1,0:T(8,128)(2,1)S(1)} collective-permute-done((bf16[128,512]{1,0:T(8,128)(2,1)S(1)}, bf16[128,512]{1,0:T(8,128)(2,1)S(1)}, u32[]{:S(2)}, u32[]{:S(2)}) %collective-permute-start.19) | collective-permute-done | bytes 131104 | tf_op jit(solution)/shard_map/ppermute | solution.py:238
  (49 shorter events, 6.4 us)
Async XLA Ops:
  0.6 17.2 %collective-permute-start = (bf16[128,512]{1,0:T(8,128)(2,1)}, bf16[128,512]{1,0:T(8,128)(2,1)S(1)}, u32[]{:S(2)}, u32[]{:S(2)}) collective-permute-start(bf16[128,512]{1,0:T(8,128)(2,1)} %bitcast.16), channel_id=1, source_target_pairs={{0,1},{1,2},{2,3},{3,4},{4,5},{5,6},{6,7},{7,0},{8,9},{9,10},{10,1... | collective-permute-start | bytes 393224 | tf_op jit(solution)/shard_map/ppermute | solution.py:238
  2.1 15.7 %collective-permute-start.1 = (bf16[128,512]{1,0:T(8,128)(2,1)}, bf16[128,512]{1,0:T(8,128)(2,1)S(1)}, u32[]{:S(2)}, u32[]{:S(2)}) collective-permute-start(bf16[128,512]{1,0:T(8,128)(2,1)} %bitcast.17), channel_id=1, source_target_pairs={{0,2},{1,3},{2,4},{3,5},{4,6},{5,7},{6,0},{7,1},{8,10},{9,11},{10,... | collective-permute-start | bytes 393224 | tf_op jit(solution)/shard_map/ppermute | solution.py:238
  3.6 14.3 %collective-permute-start.2 = (bf16[128,512]{1,0:T(8,128)(2,1)}, bf16[128,512]{1,0:T(8,128)(2,1)S(1)}, u32[]{:S(2)}, u32[]{:S(2)}) collective-permute-start(bf16[128,512]{1,0:T(8,128)(2,1)} %bitcast.18), channel_id=1, source_target_pairs={{0,3},{1,4},{2,5},{3,6},{4,7},{5,0},{6,1},{7,2},{8,11},{9,12},{10,... | collective-permute-start | bytes 393224 | tf_op jit(solution)/shard_map/ppermute | solution.py:238
  6.4 11.5 %collective-permute-start.3 = (bf16[128,512]{1,0:T(8,128)(2,1)}, bf16[128,512]{1,0:T(8,128)(2,1)S(1)}, u32[]{:S(2)}, u32[]{:S(2)}) collective-permute-start(bf16[128,512]{1,0:T(8,128)(2,1)} %bitcast.19), channel_id=1, source_target_pairs={{0,4},{1,5},{2,6},{3,7},{4,0},{5,1},{6,2},{7,3},{8,12},{9,13},{10,... | collective-permute-start | bytes 393224 | tf_op jit(solution)/shard_map/ppermute | solution.py:238
  12.8 5.0 %copy-start.6 = (bf16[1,128,512]{2,1,0:T(8,128)(2,1)S(1)}, bf16[1,128,512]{2,1,0:T(8,128)(2,1)}, u32[]{:S(2)}) copy-start(bf16[1,128,512]{2,1,0:T(8,128)(2,1)} %param.8) | copy-start | bytes 393220
  12.8 5.0 %copy-start.7 = (s32[1,8]{1,0:T(1,128)S(1)}, s32[1,8]{1,0:T(1,128)}, u32[]{:S(2)}) copy-start(s32[1,8]{1,0:T(1,128)} %lengths.3) | copy-start | bytes 100
  12.9 38.6 %all-to-all-start = ((bf16[8,4,256,128]{3,2,1,0:T(8,128)(2,1)}), bf16[8,4,256,128]{3,2,1,0:T(8,128)(2,1)}, u32[]{:S(2)}, u32[]{:S(2)}) async-start(bf16[8,4,256,128]{3,2,1,0:T(8,128)(2,1)} %deal_inputs.1), calls=%async_computation | async-start | bytes 4194304 | tf_op jit(solution)/shard_map/all_to_all | solution.py:257
  22.0 7.9 %collective-permute-start.11 = (bf16[128,512]{1,0:T(8,128)(2,1)S(1)}, bf16[128,512]{1,0:T(8,128)(2,1)S(1)}, u32[]{:S(2)}, u32[]{:S(2)}) collective-permute-start(bf16[128,512]{1,0:T(8,128)(2,1)S(1)} %get-tuple-element.29), channel_id=1, source_target_pairs={{0,4},{1,5},{2,6},{3,7},{4,0},{5,1},{6,2},{7,3},{8,12},{9,13},{10,... | collective-permute-start | bytes 393224 | tf_op jit(solution)/shard_map/ppermute | solution.py:238
  24.4 8.7 %collective-permute-start.10 = (bf16[128,512]{1,0:T(8,128)(2,1)S(1)}, bf16[128,512]{1,0:T(8,128)(2,1)S(1)}, u32[]{:S(2)}, u32[]{:S(2)}) collective-permute-start(bf16[128,512]{1,0:T(8,128)(2,1)S(1)} %get-tuple-element.28), channel_id=1, source_target_pairs={{0,5},{1,6},{2,7},{3,0},{4,1},{5,2},{6,3},{7,4},{8,13},{9,14},{10,... | collective-permute-start | bytes 393224 | tf_op jit(solution)/shard_map/ppermute | solution.py:238
  27.0 8.6 %collective-permute-start.9 = (bf16[128,512]{1,0:T(8,128)(2,1)S(1)}, bf16[128,512]{1,0:T(8,128)(2,1)S(1)}, u32[]{:S(2)}, u32[]{:S(2)}) collective-permute-start(bf16[128,512]{1,0:T(8,128)(2,1)S(1)} %get-tuple-element.27), channel_id=1, source_target_pairs={{0,6},{1,7},{2,0},{3,1},{4,2},{5,3},{6,4},{7,5},{8,14},{9,15},{10,... | collective-permute-start | bytes 393224 | tf_op jit(solution)/shard_map/ppermute | solution.py:238
  27.0 11.9 %collective-permute-start.8 = (bf16[128,512]{1,0:T(8,128)(2,1)S(1)}, bf16[128,512]{1,0:T(8,128)(2,1)S(1)}, u32[]{:S(2)}, u32[]{:S(2)}) collective-permute-start(bf16[128,512]{1,0:T(8,128)(2,1)S(1)} %get-tuple-element.26), channel_id=1, source_target_pairs={{0,7},{1,0},{2,1},{3,2},{4,3},{5,4},{6,5},{7,6},{8,15},{9,8},{10,9... | collective-permute-start | bytes 393224 | tf_op jit(solution)/shard_map/ppermute | solution.py:238
  28.7 14.2 %collective-permute-start.4 = (bf16[128,512]{1,0:T(8,128)(2,1)S(1)}, bf16[128,512]{1,0:T(8,128)(2,1)S(1)}, u32[]{:S(2)}, u32[]{:S(2)}) collective-permute-start(bf16[128,512]{1,0:T(8,128)(2,1)S(1)} %get-tuple-element.23), channel_id=1, source_target_pairs={{0,1},{1,2},{2,3},{3,4},{4,5},{5,6},{6,7},{7,0},{8,9},{9,10},{10,1... | collective-permute-start | bytes 393224 | tf_op jit(solution)/shard_map/ppermute | solution.py:238
  29.9 13.3 %collective-permute-start.5 = (bf16[128,512]{1,0:T(8,128)(2,1)S(1)}, bf16[128,512]{1,0:T(8,128)(2,1)S(1)}, u32[]{:S(2)}, u32[]{:S(2)}) collective-permute-start(bf16[128,512]{1,0:T(8,128)(2,1)S(1)} %get-tuple-element.23), channel_id=1, source_target_pairs={{0,2},{1,3},{2,4},{3,5},{4,6},{5,7},{6,0},{7,1},{8,10},{9,11},{10,... | collective-permute-start | bytes 393224 | tf_op jit(solution)/shard_map/ppermute | solution.py:238
  33.1 13.6 %collective-permute-start.6 = (bf16[128,512]{1,0:T(8,128)(2,1)S(1)}, bf16[128,512]{1,0:T(8,128)(2,1)S(1)}, u32[]{:S(2)}, u32[]{:S(2)}) collective-permute-start(bf16[128,512]{1,0:T(8,128)(2,1)S(1)} %get-tuple-element.23), channel_id=1, source_target_pairs={{0,3},{1,4},{2,5},{3,6},{4,7},{5,0},{6,1},{7,2},{8,11},{9,12},{10,... | collective-permute-start | bytes 393224 | tf_op jit(solution)/shard_map/ppermute | solution.py:238
  39.0 28.4 %copy-start = (bf16[128,512]{1,0:T(8,128)(2,1)}, bf16[128,512]{1,0:T(8,128)(2,1)S(1)}, u32[]{:S(2)}) copy-start(bf16[128,512]{1,0:T(8,128)(2,1)S(1)} %add_convert_fusion.2.refs_0_) | copy-start | bytes 393220
  39.0 8.7 %collective-permute-start.12 = (bf16[128,512]{1,0:T(8,128)(2,1)S(1)}, bf16[128,512]{1,0:T(8,128)(2,1)S(1)}, u32[]{:S(2)}, u32[]{:S(2)}) collective-permute-start(bf16[128,512]{1,0:T(8,128)(2,1)S(1)} %add_convert_fusion.2.refs_0_), channel_id=1, source_target_pairs={{0,129},{1,128},{2,131},{3,130},{4,133},{5,132},{6,135},{7,134},{8... | collective-permute-start | bytes 393224 | tf_op jit(solution)/shard_map/ppermute | solution.py:234
  41.4 6.3 %collective-permute-start.13 = (bf16[128,512]{1,0:T(8,128)(2,1)S(1)}, bf16[128,512]{1,0:T(8,128)(2,1)S(1)}, u32[]{:S(2)}, u32[]{:S(2)}) collective-permute-start(bf16[128,512]{1,0:T(8,128)(2,1)S(1)} %add_convert_fusion.2.refs_0_), channel_id=1, source_target_pairs={{0,16},{1,17},{2,18},{3,19},{4,20},{5,21},{6,22},{7,23},{8,24},{9,... | collective-permute-start | bytes 393224 | tf_op jit(solution)/shard_map/ppermute | solution.py:234
  42.8 7.2 %collective-permute-start.14 = (bf16[128,512]{1,0:T(8,128)(2,1)S(1)}, bf16[128,512]{1,0:T(8,128)(2,1)S(1)}, u32[]{:S(2)}, u32[]{:S(2)}) collective-permute-start(bf16[128,512]{1,0:T(8,128)(2,1)S(1)} %add_convert_fusion.2.refs_0_), channel_id=1, source_target_pairs={{0,145},{1,144},{2,147},{3,146},{4,149},{5,148},{6,151},{7,150},{8... | collective-permute-start | bytes 393224 | tf_op jit(solution)/shard_map/ppermute | solution.py:234
  43.3 6.8 %collective-permute-start.7 = (bf16[128,512]{1,0:T(8,128)(2,1)S(1)}, bf16[128,512]{1,0:T(8,128)(2,1)S(1)}, u32[]{:S(2)}, u32[]{:S(2)}) collective-permute-start(bf16[128,512]{1,0:T(8,128)(2,1)S(1)} %get-tuple-element.23), channel_id=1, source_target_pairs={{0,4},{1,5},{2,6},{3,7},{4,0},{5,1},{6,2},{7,3},{8,12},{9,13},{10,... | collective-permute-start | bytes 393224 | tf_op jit(solution)/shard_map/ppermute | solution.py:238
  46.7 3.4 %collective-permute-start.15 = (bf16[128,512]{1,0:T(8,128)(2,1)S(1)}, bf16[128,512]{1,0:T(8,128)(2,1)S(1)}, u32[]{:S(2)}, u32[]{:S(2)}) collective-permute-start(bf16[128,512]{1,0:T(8,128)(2,1)S(1)} %add_convert_fusion.2.refs_0_), channel_id=1, source_target_pairs={{0,8},{1,9},{2,10},{3,11},{4,12},{5,13},{6,14},{7,15},{8,0},{9,1},... | collective-permute-start | bytes 393224 | tf_op jit(solution)/shard_map/ppermute | solution.py:234
  47.7 2.4 %collective-permute-start.16 = (bf16[128,512]{1,0:T(8,128)(2,1)S(1)}, bf16[128,512]{1,0:T(8,128)(2,1)S(1)}, u32[]{:S(2)}, u32[]{:S(2)}) collective-permute-start(bf16[128,512]{1,0:T(8,128)(2,1)S(1)} %collective-permute-done.12.refs_1_), channel_id=1, source_target_pairs={{0,8},{1,9},{2,10},{3,11},{4,12},{5,13},{6,14},{7,15},{8,0},{9,1},... | collective-permute-start | bytes 393224 | tf_op jit(solution)/shard_map/ppermute | solution.py:234
  47.7 2.4 %collective-permute-start.17 = (bf16[128,512]{1,0:T(8,128)(2,1)S(1)}, bf16[128,512]{1,0:T(8,128)(2,1)S(1)}, u32[]{:S(2)}, u32[]{:S(2)}) collective-permute-start(bf16[128,512]{1,0:T(8,128)(2,1)S(1)} %collective-permute-done.13.refs_2_), channel_id=1, source_target_pairs={{0,8},{1,9},{2,10},{3,11},{4,12},{5,13},{6,14},{7,15},{8,0},{9,1},... | collective-permute-start | bytes 393224 | tf_op jit(solution)/shard_map/ppermute | solution.py:234
  50.1 1.3 %collective-permute-start.18 = (bf16[128,512]{1,0:T(8,128)(2,1)S(1)}, bf16[128,512]{1,0:T(8,128)(2,1)S(1)}, u32[]{:S(2)}, u32[]{:S(2)}) collective-permute-start(bf16[128,512]{1,0:T(8,128)(2,1)S(1)} %collective-permute-done.14.refs_3_), channel_id=1, source_target_pairs={{0,8},{1,9},{2,10},{3,11},{4,12},{5,13},{6,14},{7,15},{8,0},{9,1},... | collective-permute-start | bytes 393224 | tf_op jit(solution)/shard_map/ppermute | solution.py:234
  51.4 6.9 %copy-start.4 = (bf16[1,128,4096]{2,1,0:T(8,128)(2,1)S(1)}, bf16[1,128,4096]{2,1,0:T(8,128)(2,1)}, u32[]{:S(2)}) copy-start(bf16[1,128,4096]{2,1,0:T(8,128)(2,1)} %param.9) | copy-start | bytes 3145732
  54.4 13.6 %collective-permute-start.25 = (bf16[256,512]{1,0:T(8,128)(2,1)S(1)}, bf16[256,512]{1,0:T(8,128)(2,1)S(1)}, u32[]{:S(2)}, u32[]{:S(2)}) collective-permute-start(bf16[256,512]{1,0:T(8,128)(2,1)S(1)} %get-tuple-element.41), channel_id=1, source_target_pairs={{0,6},{1,7},{2,0},{3,1},{4,2},{5,3},{6,4},{7,5},{8,14},{9,15},{10,... | collective-permute-start | bytes 786440 | tf_op jit(solution)/shard_map/ppermute | solution.py:234
  56.4 11.5 %collective-permute-start.24 = (bf16[256,512]{1,0:T(8,128)(2,1)S(1)}, bf16[256,512]{1,0:T(8,128)(2,1)S(1)}, u32[]{:S(2)}, u32[]{:S(2)}) collective-permute-start(bf16[256,512]{1,0:T(8,128)(2,1)S(1)} %get-tuple-element.40), channel_id=1, source_target_pairs={{0,4},{1,5},{2,6},{3,7},{4,0},{5,1},{6,2},{7,3},{8,12},{9,13},{10,... | collective-permute-start | bytes 786440 | tf_op jit(solution)/shard_map/ppermute | solution.py:234
  58.3 13.3 %collective-permute-start.23 = (bf16[256,512]{1,0:T(8,128)(2,1)S(1)}, bf16[256,512]{1,0:T(8,128)(2,1)S(1)}, u32[]{:S(2)}, u32[]{:S(2)}) collective-permute-start(bf16[256,512]{1,0:T(8,128)(2,1)S(1)} %get-tuple-element.39), channel_id=1, source_target_pairs={{0,2},{1,3},{2,4},{3,5},{4,6},{5,7},{6,0},{7,1},{8,10},{9,11},{10,... | collective-permute-start | bytes 786440 | tf_op jit(solution)/shard_map/ppermute | solution.py:234
  72.5 24.6 %all-to-all-start.1 = ((bf16[8,32,512]{2,1,0:T(8,128)(2,1)}), bf16[8,32,512]{2,1,0:T(8,128)(2,1)S(1)}, u32[]{:S(2)}, u32[]{:S(2)}) async-start(bf16[8,32,512]{2,1,0:T(8,128)(2,1)} %bitcast.8), calls=%async_computation.1 | async-start | bytes 524288 | tf_op jit(solution)/shard_map/all_to_all | solution.py:281
  82.7 6.5 %collective-permute-start.22 = (bf16[128,512]{1,0:T(8,128)(2,1)S(1)}, bf16[128,512]{1,0:T(8,128)(2,1)S(1)}, u32[]{:S(2)}, u32[]{:S(2)}) collective-permute-start(bf16[128,512]{1,0:T(8,128)(2,1)S(1)} %get-tuple-element.37), channel_id=1, source_target_pairs={{0,4},{1,5},{2,6},{3,7},{4,0},{5,1},{6,2},{7,3},{8,12},{9,13},{10,... | collective-permute-start | bytes 393224 | tf_op jit(solution)/shard_map/ppermute | solution.py:238
  84.5 9.1 %collective-permute-start.21 = (bf16[128,512]{1,0:T(8,128)(2,1)S(1)}, bf16[128,512]{1,0:T(8,128)(2,1)S(1)}, u32[]{:S(2)}, u32[]{:S(2)}) collective-permute-start(bf16[128,512]{1,0:T(8,128)(2,1)S(1)} %get-tuple-element.36), channel_id=1, source_target_pairs={{0,5},{1,6},{2,7},{3,0},{4,1},{5,2},{6,3},{7,4},{8,13},{9,14},{10,... | collective-permute-start | bytes 393224 | tf_op jit(solution)/shard_map/ppermute | solution.py:238
  85.5 8.1 %collective-permute-start.20 = (bf16[128,512]{1,0:T(8,128)(2,1)S(1)}, bf16[128,512]{1,0:T(8,128)(2,1)S(1)}, u32[]{:S(2)}, u32[]{:S(2)}) collective-permute-start(bf16[128,512]{1,0:T(8,128)(2,1)S(1)} %get-tuple-element.35), channel_id=1, source_target_pairs={{0,6},{1,7},{2,0},{3,1},{4,2},{5,3},{6,4},{7,5},{8,14},{9,15},{10,... | collective-permute-start | bytes 393224 | tf_op jit(solution)/shard_map/ppermute | solution.py:238
  86.3 10.0 %collective-permute-start.19 = (bf16[128,512]{1,0:T(8,128)(2,1)S(1)}, bf16[128,512]{1,0:T(8,128)(2,1)S(1)}, u32[]{:S(2)}, u32[]{:S(2)}) collective-permute-start(bf16[128,512]{1,0:T(8,128)(2,1)S(1)} %get-tuple-element.34), channel_id=1, source_target_pairs={{0,7},{1,0},{2,1},{3,2},{4,3},{5,4},{6,5},{7,6},{8,15},{9,8},{10,9... | collective-permute-start | bytes 393224 | tf_op jit(solution)/shard_map/ppermute | solution.py:238
  (4 other events, 16.7 us)

commit v4 on v3

--- a/solution.py
+++ b/solution.py
@@ -155,7 +155,7 @@
         out_specs=[VMEM] * 6,
         out_shape=[sds((ROWS, GROUPS * GROUP * HD), BF16)] + TERMS,
         scratch_shapes=SCRATCH,
-        compiler_params=params(24),
+        compiler_params=params(58),
         cost_estimate=pl.CostEstimate(flops=4 * 10**10, bytes_accessed=4 * 10**6, transcendentals=2 * 10**6),
         name="score_grad",
     )(lengths, q, do, *keys, *values, stats)
@@ -193,29 +193,57 @@
 
 
 def weight_kernel(inputs, *refs):
-    grads, outs = refs[:8], refs[-4:]
+    grads, own, away = refs[:8], refs[-2], refs[-1]
     dp, ctx = lax.axis_index("dp"), lax.axis_index("ctx")
     core, high, low, x = dp % 2, dp // 16, dp // 2 % 2, ctx // 2
     members = [(core ^ c) * 4 + (high ^ h) * 2 + (low ^ n) for c in range(2) for n in range(2) for h in range(2)]
     right = jnp.concatenate([ref[...] for ref in grads], axis=0)
-    for n, out in enumerate(outs):
+    for n in range(4):
         left = jnp.concatenate([inputs[member, (x + n) % 4] for member in members], axis=1)
-        out[...] = dot(left, right, (1, 0)).astype(out.dtype)
+        term = dot(left, right, (1, 0))
+        for y in range(2):
+            away[(x + n) % 4 * 2 + y] = term[y * 128 : (y + 1) * 128].astype(BF16)
+        if n == 0:
+            own[...] = jnp.where(ctx % 2 == 0, term[:128], term[128:])
+    away[ctx] = jnp.zeros(away.shape[1:], BF16)
 
 
 def weight_call(inputs, grads, others):
-    shape = (256, grads[0].shape[1])
+    shape = (128, grads[0].shape[1])
     return pl.pallas_call(
         weight_kernel,
         in_specs=[VMEM] * (9 + len(others)),
-        out_specs=[VMEM] * 4,
-        out_shape=[sds(shape, F32)] + [sds(shape, BF16)] * 3,
+        out_specs=[VMEM] * 2,
+        out_shape=[sds(shape, F32), sds((8, *shape), BF16)],
         compiler_params=params(24),
         cost_estimate=pl.CostEstimate(flops=10**6, bytes_accessed=10**4, transcendentals=0),
         name="weight_grad",
     )(inputs, *grads, *others)
 
 
+def part_kernel(own, across, *outs):
+    total = own[...] + sum(across[n].astype(F32) for n in range(8))
+    near = lax.axis_index("dp") // 4 % 4
+    for n, out in enumerate(outs):
+        rows = total[:32]
+        for z in range(1, 4):
+            rows = jnp.where((near + n) % 4 == z, total[z * 32 : (z + 1) * 32], rows)
+        out[...] = rows.astype(out.dtype)
+
+
+def part_call(own, across):
+    shape = (32, own.shape[1])
+    return pl.pallas_call(
+        part_kernel,
+        in_specs=[VMEM] * 2,
+        out_specs=[VMEM] * 4,
+        out_shape=[sds(shape, F32)] + [sds(shape, BF16)] * 3,
+        compiler_params=params(16),
+        cost_estimate=pl.CostEstimate(flops=10**6, bytes_accessed=10**6, transcendentals=0),
+        name="add_terms",
+    )(own, across)
+
+
 def place(device):
     dp, ctx = divmod(device, 8)
     return ctx // 2, dp // 16 * 2 + ctx % 2, dp // 2 % 8, dp % 2
@@ -225,11 +253,11 @@
     return ((y // 2 * 8 + z) * 2 + core) * 8 + x * 2 + y % 2
 
 
-def move(array, dx=0, flip_y=False, flip_z=False, flip_core=False):
+def move(array, dz=0, flip_y=False, flip_z=False, flip_core=False):
     pairs = []
     for source in range(256):
         x, y, z, core = place(source)
-        target = device((x + dx) % 4, 3 - y if flip_y else y, z ^ flip_z, core ^ flip_core)
+        target = device(x, 3 - y if flip_y else y, (z ^ flip_z) + dz & 7, core ^ flip_core)
         pairs.append((source, target))
     return lax.ppermute(array, ("dp", "ctx"), pairs)
 
@@ -264,22 +292,15 @@
     flips = ((True, False), (False, True), (True, True))
     grads = [value_grad] + [move(value_grad, flip_y=y, flip_z=z) for y, z in flips]
     grads += [move(grad, flip_core=True) for grad in grads]
-    total, *away = weight_call(inputs, grads, values[1:])
-    across = [move(term, dx=d) for d, term in enumerate(away, 1)]
+    total, away = weight_call(inputs, grads, values[1:])
+    across = lax.all_to_all(away, "ctx", 0, 0)
 
     query_grad, *key_terms = score_call(doc_lengths, q, do, keys, values, after(stats, total))
     arrived = [ring(term, -d) for d, term in enumerate(key_terms[1:], 1)]
     key_grad = (key_terms[0] + sum(term.astype(F32) for term in arrived)).astype(BF16)
-    total = (after(total, query_grad) + sum(term.astype(F32) for term in across)).astype(BF16)
-    owners = [
-        [device(x, 2 * high + y, 2 * z + low, core) for y in range(2) for z in range(4)]
-        for x in range(4)
-        for high in range(2)
-        for low in range(2)
-        for core in range(2)
-    ]
-    parts = lax.all_to_all(total.reshape(8, 32, -1), ("dp", "ctx"), 0, 0, axis_index_groups=owners)
-    weight_grad = jnp.sum(parts.astype(F32), axis=0) * tokens**-0.5
+    total, *away = part_call(after(total, query_grad), across)
+    total = total + sum(move(term, dz=2 * d).astype(F32) for d, term in enumerate(away, 1))
+    weight_grad = total * tokens**-0.5
 
     return query_grad[None], key_grad[None], value_grad[None], weight_grad
 

time: 98 us -> 94.9 us (0.968)
  waiting for transfers between devices: 20.9 us -> 10.7 us
  starting transfers between devices: 51.9 us -> 55.5 us
  Pallas kernels: 20.1 us -> 22.8 us
    ppermute x16, waiting for transfers between devices: 12.5 us -> 4.87 us  [ring(): lax.ppermute(array, 'ctx', [(n, (n + distance) % 8) for n in range(8)])]
    ppermute x10, starting transfers between devices: 8.71 us -> 14.2 us  [move(): return lax.ppermute(array, ('dp', 'ctx'), pairs)]
    all_to_all x1, starting transfers between devices: 10.3 us -> 6.62 us  [shards(): across = lax.all_to_all(away, 'ctx', 0, 0)]
    ppermute x10, waiting for transfers between devices: 8.41 us -> 5.79 us  [move(): return lax.ppermute(array, ('dp', 'ctx'), pairs)]
    ppermute x16, starting transfers between devices: 28 us -> 29.8 us  [ring(): lax.ppermute(array, 'ctx', [(n, (n + distance) % 8) for n in range(8)])]
    pallas_call x1, Pallas kernels: 9.04 us -> 10.6 us  [score_call(): pl.pallas_call(score_kernel, in_specs=[SMEM] + [VMEM] * 13, out_specs=[VM...]
    unnamed x16 -> x32, local copies, waits for them, and re-layouts: 1.62 us -> 2.3 us
  transfers between devices with their start and end apart: 28 -> 28, of which waited for: 10 -> 8; matrix products, arithmetic and copies ran while one was open for 1% -> 2% of each run, Pallas kernels for 18% -> 20%
where the time goes in v4:
time: 94.9 us; the launch traced here: 94.6 us
  starting transfers between devices  55.5 us (58%)
  Pallas kernels  22.8 us (24%)
  waiting for transfers between devices  10.7 us (11%)
  other arithmetic  2.41 us (3%)
  local copies, waits for them, and re-layouts  2.3 us (2%)
    ppermute x16, starting transfers between devices, ring(): lax.ppermute(array, 'ctx', [(n, (n + distance) % 8) for n in range(8)])  29.8 us
    ppermute x10, starting transfers between devices, move(): return lax.ppermute(array, ('dp', 'ctx'), pairs)  14.2 us
    pallas_call x1, Pallas kernels, score_call(): pl.pallas_call(score_kernel, in_specs=[SMEM] + [VMEM] * 13, out_specs=[VM...  10.6 us
    all_to_all x1, starting transfers between devices, shards(): across = lax.all_to_all(away, 'ctx', 0, 0)  6.62 us
    ppermute x10, waiting for transfers between devices, move(): return lax.ppermute(array, ('dp', 'ctx'), pairs)  5.79 us
    all_to_all x1, starting transfers between devices, shards(): lax.all_to_all(dealt, ('dp', 'ctx'), 0, 0, axis_index_groups=members)  4.95 us
    ppermute x16, waiting for transfers between devices, ring(): lax.ppermute(array, 'ctx', [(n, (n + distance) % 8) for n in range(8)])  4.87 us
    pallas_call x1, Pallas kernels, value_call(): pl.pallas_call(value_kernel, in_specs=[SMEM] + [VMEM] * 8, out_specs=[VME...  4.13 us
  transfers between devices with their start and end apart: 28, of which 8 were waited for; matrix products, arithmetic and copies ran while one was open for 2% of the time, Pallas kernels for 20%

profile of v4, /device:TPU:8, one launch (start us, length us, event | category | flops | bytes accessed | tf_op | source)
XLA Modules:
  0.0 94.6 jit_solution(1506853983209348725)
XLA Ops:
  0.6 1.5 %collective-permute-start = (bf16[128,512]{1,0:T(8,128)(2,1)}, bf16[128,512]{1,0:T(8,128)(2,1)S(1)}, u32[]{:S(2)}, u32[]{:S(2)}) collective-permute-start(bf16[128,512]{1,0:T(8,128)(2,1)} %bitcast.15), channel_id=1, source_target_pairs={{0,1},{1,2},{2,3},{3,4},{4,5},{5,6},{6,7},{7,0},{8,9},{9,10},{10,1... | collective-permute-start | bytes 393224 | tf_op jit(solution)/shard_map/ppermute | solution.py:266
  2.1 1.5 %collective-permute-start.1 = (bf16[128,512]{1,0:T(8,128)(2,1)}, bf16[128,512]{1,0:T(8,128)(2,1)S(1)}, u32[]{:S(2)}, u32[]{:S(2)}) collective-permute-start(bf16[128,512]{1,0:T(8,128)(2,1)} %bitcast.16), channel_id=1, source_target_pairs={{0,2},{1,3},{2,4},{3,5},{4,6},{5,7},{6,0},{7,1},{8,10},{9,11},{10,... | collective-permute-start | bytes 393224 | tf_op jit(solution)/shard_map/ppermute | solution.py:266
  3.6 2.8 %collective-permute-start.2 = (bf16[128,512]{1,0:T(8,128)(2,1)}, bf16[128,512]{1,0:T(8,128)(2,1)S(1)}, u32[]{:S(2)}, u32[]{:S(2)}) collective-permute-start(bf16[128,512]{1,0:T(8,128)(2,1)} %bitcast.17), channel_id=1, source_target_pairs={{0,3},{1,4},{2,5},{3,6},{4,7},{5,0},{6,1},{7,2},{8,11},{9,12},{10,... | collective-permute-start | bytes 393224 | tf_op jit(solution)/shard_map/ppermute | solution.py:266
  6.4 0.8 collective-permute-start.3
  7.2 1.6 %copy-done.5 = bf16[1,128,8192]{2,1,0:T(8,128)(2,1)S(1)} copy-done((bf16[1,128,8192]{2,1,0:T(8,128)(2,1)S(1)}, bf16[1,128,8192]{2,1,0:T(8,128)(2,1)}, u32[]{:S(2)}) %copy-start.5) | copy-done | bytes 2097176
  8.8 4.1 %deal_inputs.1 = bf16[8,4,256,128]{3,2,1,0:T(8,128)(2,1)} custom-call(bf16[128,8192]{1,0:T(8,128)(2,1)S(1)} %bitcast.10), custom_call_target="tpu_custom_call" | custom-call | flops 2000000000 | bytes 4000000 | tf_op jit(solution)/shard_map/deal_inputs/pallas_call | solution.py:182
  12.9 5.0 %all-to-all-start = ((bf16[8,4,256,128]{3,2,1,0:T(8,128)(2,1)}), bf16[8,4,256,128]{3,2,1,0:T(8,128)(2,1)}, u32[]{:S(2)}, u32[]{:S(2)}) async-start(bf16[8,4,256,128]{3,2,1,0:T(8,128)(2,1)} %deal_inputs.1), calls=%async_computation | async-start | bytes 4194304 | tf_op jit(solution)/shard_map/all_to_all | solution.py:285
  17.9 4.1 %value_grad.1 = (bf16[128,512]{1,0:T(8,128)(2,1)S(1)}, f32[128,512]{1,0:T(8,128)S(1)}, bf16[128,512]{1,0:T(8,128)(2,1)S(1)}, bf16[128,512]{1,0:T(8,128)(2,1)S(1)...) custom-call(s32[1,8]{1,0:T(1,128)S(1)} %copy-done.14, ...), custom_call_target="tpu_custom_call" | custom-call | flops 149999992832 | bytes 4000000 | tf_op jit(solution)/shard_map/value_grad/pallas_call | solution.py:139
  22.8 2.3 %collective-permute-start.11 = (bf16[128,512]{1,0:T(8,128)(2,1)S(1)}, bf16[128,512]{1,0:T(8,128)(2,1)S(1)}, u32[]{:S(2)}, u32[]{:S(2)}) collective-permute-start(bf16[128,512]{1,0:T(8,128)(2,1)S(1)} %get-tuple-element.31), channel_id=1, source_target_pairs={{0,4},{1,5},{2,6},{3,7},{4,0},{5,1},{6,2},{7,3},{8,12},{9,13},{10,... | collective-permute-start | bytes 393224 | tf_op jit(solution)/shard_map/ppermute | solution.py:266
  25.0 2.6 %collective-permute-start.10 = (bf16[128,512]{1,0:T(8,128)(2,1)S(1)}, bf16[128,512]{1,0:T(8,128)(2,1)S(1)}, u32[]{:S(2)}, u32[]{:S(2)}) collective-permute-start(bf16[128,512]{1,0:T(8,128)(2,1)S(1)} %get-tuple-element.30), channel_id=1, source_target_pairs={{0,5},{1,6},{2,7},{3,0},{4,1},{5,2},{6,3},{7,4},{8,13},{9,14},{10,... | collective-permute-start | bytes 393224 | tf_op jit(solution)/shard_map/ppermute | solution.py:266
  27.6 1.7 %collective-permute-start.8 = (bf16[128,512]{1,0:T(8,128)(2,1)S(1)}, bf16[128,512]{1,0:T(8,128)(2,1)S(1)}, u32[]{:S(2)}, u32[]{:S(2)}) collective-permute-start(bf16[128,512]{1,0:T(8,128)(2,1)S(1)} %get-tuple-element.28), channel_id=1, source_target_pairs={{0,7},{1,0},{2,1},{3,2},{4,3},{5,4},{6,5},{7,6},{8,15},{9,8},{10,9... | collective-permute-start | bytes 393224 | tf_op jit(solution)/shard_map/ppermute | solution.py:266
  29.3 1.3 %collective-permute-start.4 = (bf16[128,512]{1,0:T(8,128)(2,1)S(1)}, bf16[128,512]{1,0:T(8,128)(2,1)S(1)}, u32[]{:S(2)}, u32[]{:S(2)}) collective-permute-start(bf16[128,512]{1,0:T(8,128)(2,1)S(1)} %get-tuple-element.25), channel_id=1, source_target_pairs={{0,1},{1,2},{2,3},{3,4},{4,5},{5,6},{6,7},{7,0},{8,9},{9,10},{10,1... | collective-permute-start | bytes 393224 | tf_op jit(solution)/shard_map/ppermute | solution.py:266
  30.6 2.0 %collective-permute-start.5 = (bf16[128,512]{1,0:T(8,128)(2,1)S(1)}, bf16[128,512]{1,0:T(8,128)(2,1)S(1)}, u32[]{:S(2)}, u32[]{:S(2)}) collective-permute-start(bf16[128,512]{1,0:T(8,128)(2,1)S(1)} %get-tuple-element.25), channel_id=1, source_target_pairs={{0,2},{1,3},{2,4},{3,5},{4,6},{5,7},{6,0},{7,1},{8,10},{9,11},{10,... | collective-permute-start | bytes 393224 | tf_op jit(solution)/shard_map/ppermute | solution.py:266
  32.6 1.2 %collective-permute-done.10 = bf16[128,512]{1,0:T(8,128)(2,1)S(1)} collective-permute-done((bf16[128,512]{1,0:T(8,128)(2,1)S(1)}, bf16[128,512]{1,0:T(8,128)(2,1)S(1)}, u32[]{:S(2)}, u32[]{:S(2)}) %collective-permute-start.10) | collective-permute-done | bytes 131104 | tf_op jit(solution)/shard_map/ppermute | solution.py:266
  33.8 2.5 %collective-permute-start.6 = (bf16[128,512]{1,0:T(8,128)(2,1)S(1)}, bf16[128,512]{1,0:T(8,128)(2,1)S(1)}, u32[]{:S(2)}, u32[]{:S(2)}) collective-permute-start(bf16[128,512]{1,0:T(8,128)(2,1)S(1)} %get-tuple-element.25), channel_id=1, source_target_pairs={{0,3},{1,4},{2,5},{3,6},{4,7},{5,0},{6,1},{7,2},{8,11},{9,12},{10,... | collective-permute-start | bytes 393224 | tf_op jit(solution)/shard_map/ppermute | solution.py:266
  36.2 3.3 %collective-permute-done.8 = bf16[128,512]{1,0:T(8,128)(2,1)S(1)} collective-permute-done((bf16[128,512]{1,0:T(8,128)(2,1)S(1)}, bf16[128,512]{1,0:T(8,128)(2,1)S(1)}, u32[]{:S(2)}, u32[]{:S(2)}) %collective-permute-start.8) | collective-permute-done | bytes 131104 | tf_op jit(solution)/shard_map/ppermute | solution.py:266
  39.6 2.2 %collective-permute-start.12 = (bf16[128,512]{1,0:T(8,128)(2,1)S(1)}, bf16[128,512]{1,0:T(8,128)(2,1)S(1)}, u32[]{:S(2)}, u32[]{:S(2)}) collective-permute-start(bf16[128,512]{1,0:T(8,128)(2,1)S(1)} %add_convert_fusion.1.refs_0_), channel_id=1, source_target_pairs={{0,129},{1,128},{2,131},{3,130},{4,133},{5,132},{6,135},{7,134},{8... | collective-permute-start | bytes 393224 | tf_op jit(solution)/shard_map/ppermute | solution.py:262
  41.8 1.5 %collective-permute-start.13 = (bf16[128,512]{1,0:T(8,128)(2,1)S(1)}, bf16[128,512]{1,0:T(8,128)(2,1)S(1)}, u32[]{:S(2)}, u32[]{:S(2)}) collective-permute-start(bf16[128,512]{1,0:T(8,128)(2,1)S(1)} %add_convert_fusion.1.refs_0_), channel_id=1, source_target_pairs={{0,16},{1,17},{2,18},{3,19},{4,20},{5,21},{6,22},{7,23},{8,24},{9,... | collective-permute-start | bytes 393224 | tf_op jit(solution)/shard_map/ppermute | solution.py:262
  43.9 3.3 %collective-permute-start.7 = (bf16[128,512]{1,0:T(8,128)(2,1)S(1)}, bf16[128,512]{1,0:T(8,128)(2,1)S(1)}, u32[]{:S(2)}, u32[]{:S(2)}) collective-permute-start(bf16[128,512]{1,0:T(8,128)(2,1)S(1)} %get-tuple-element.25), channel_id=1, source_target_pairs={{0,4},{1,5},{2,6},{3,7},{4,0},{5,1},{6,2},{7,3},{8,12},{9,13},{10,... | collective-permute-start | bytes 393224 | tf_op jit(solution)/shard_map/ppermute | solution.py:266
  48.3 1.8 %collective-permute-done.14.refs_3_ = bf16[128,512]{1,0:T(8,128)(2,1)S(1)} collective-permute-done((bf16[128,512]{1,0:T(8,128)(2,1)S(1)}, bf16[128,512]{1,0:T(8,128)(2,1)S(1)}, u32[]{:S(2)}, u32[]{:S(2)}) %collective-permute-start.14) | collective-permute-done | bytes 131104 | tf_op jit(solution)/shard_map/ppermute | solution.py:262
  50.4 1.0 %collective-permute-done.18.refs_7_ = bf16[128,512]{1,0:T(8,128)(2,1)S(1)} collective-permute-done((bf16[128,512]{1,0:T(8,128)(2,1)S(1)}, bf16[128,512]{1,0:T(8,128)(2,1)S(1)}, u32[]{:S(2)}, u32[]{:S(2)}) %collective-permute-start.18) | collective-permute-done | bytes 131104 | tf_op jit(solution)/shard_map/ppermute | solution.py:262
  51.4 3.8 %weight_grad.1 = (f32[128,512]{1,0:T(8,128)S(1)}, bf16[8,128,512]{2,1,0:T(8,128)(2,1)}) custom-call(bf16[8,4,256,128]{3,2,1,0:T(8,128)(2,1)} %all-to-all-done.inputs, bf16[128,512]{1,0:T(8,128)(2,1)S(1)} %add_convert_fusion.1.refs_0_, bf16[128,512]{1,0:T(8,128)(2,1)S(1)} %collective-permute-done.12.refs_1_, ...), custom_call_target="tpu_custom_call" | custom-call | flops 1000000 | bytes 10000 | tf_op jit(solution)/shard_map/weight_grad/pallas_call | solution.py:213
  55.3 6.6 %all-to-all-start.1 = ((bf16[8,128,512]{2,1,0:T(8,128)(2,1)}), bf16[8,128,512]{2,1,0:T(8,128)(2,1)S(1)}, u32[]{:S(2)}, u32[]{:S(2)}) async-start(bf16[8,128,512]{2,1,0:T(8,128)(2,1)} %get-tuple-element.41), calls=%async_computation.1 | async-start | bytes 2097152 | tf_op jit(solution)/shard_map/all_to_all | solution.py:296
  61.9 10.6 %score_grad.1 = (bf16[128,4096]{1,0:T(8,128)(2,1)}, f32[128,512]{1,0:T(8,128)}, bf16[128,512]{1,0:T(8,128)(2,1)}, bf16[128,512]{1,0:T(8,128)(2,1)}, bf16[128,512]{1,0:T(8,128)(2,1)}, /*index=5*/bf16[128,512]{1,0:T(8,128)(2,1)}) custom-call(s32[1,8]{1,0:T(1,128)} %lengths.3, bf16[128,4096]{1,0:T(8,128)(2,1)} %bitcast.11, bf16[128,4096]{1,0:T(8,128)(2,1)} %bitcast.13, ...), custom_call_target="tpu_custom_call" | custom-call | flops 40000000000 | bytes 4000000 | tf_op jit(solution)/shard_map/score_grad/pallas_call | solution.py:152
  72.5 3.0 %collective-permute-start.22 = (bf16[128,512]{1,0:T(8,128)(2,1)}, bf16[128,512]{1,0:T(8,128)(2,1)S(1)}, u32[]{:S(2)}, u32[]{:S(2)}) collective-permute-start(bf16[128,512]{1,0:T(8,128)(2,1)} %get-tuple-element.39), channel_id=1, source_target_pairs={{0,4},{1,5},{2,6},{3,7},{4,0},{5,1},{6,2},{7,3},{8,12},{9,13},{10,... | collective-permute-start | bytes 393224 | tf_op jit(solution)/shard_map/ppermute | solution.py:266
  75.5 1.2 %collective-permute-start.21 = (bf16[128,512]{1,0:T(8,128)(2,1)}, bf16[128,512]{1,0:T(8,128)(2,1)S(1)}, u32[]{:S(2)}, u32[]{:S(2)}) collective-permute-start(bf16[128,512]{1,0:T(8,128)(2,1)} %get-tuple-element.38), channel_id=1, source_target_pairs={{0,5},{1,6},{2,7},{3,0},{4,1},{5,2},{6,3},{7,4},{8,13},{9,14},{10,... | collective-permute-start | bytes 393224 | tf_op jit(solution)/shard_map/ppermute | solution.py:266
  76.7 3.5 %collective-permute-start.19 = (bf16[128,512]{1,0:T(8,128)(2,1)}, bf16[128,512]{1,0:T(8,128)(2,1)S(1)}, u32[]{:S(2)}, u32[]{:S(2)}) collective-permute-start(bf16[128,512]{1,0:T(8,128)(2,1)} %get-tuple-element.36), channel_id=1, source_target_pairs={{0,7},{1,0},{2,1},{3,2},{4,3},{5,4},{6,5},{7,6},{8,15},{9,8},{10,9... | collective-permute-start | bytes 393224 | tf_op jit(solution)/shard_map/ppermute | solution.py:266
  80.4 5.7 %collective-permute-start.25 = (bf16[32,512]{1,0:T(8,128)(2,1)S(1)}, bf16[32,512]{1,0:T(8,128)(2,1)S(1)}, u32[]{:S(2)}, u32[]{:S(2)}) collective-permute-start(bf16[32,512]{1,0:T(8,128)(2,1)S(1)} %get-tuple-element.45), channel_id=1, source_target_pairs={{0,96},{1,97},{2,98},{3,99},{4,100},{5,101},{6,102},{7,103},{8,104... | collective-permute-start | bytes 98312 | tf_op jit(solution)/shard_map/ppermute | solution.py:262
  86.1 1.3 %collective-permute-start.24 = (bf16[32,512]{1,0:T(8,128)(2,1)S(1)}, bf16[32,512]{1,0:T(8,128)(2,1)S(1)}, u32[]{:S(2)}, u32[]{:S(2)}) collective-permute-start(bf16[32,512]{1,0:T(8,128)(2,1)S(1)} %get-tuple-element.44), channel_id=1, source_target_pairs={{0,64},{1,65},{2,66},{3,67},{4,68},{5,69},{6,70},{7,71},{8,72},{9,... | collective-permute-start | bytes 98312 | tf_op jit(solution)/shard_map/ppermute | solution.py:262
  87.4 2.5 %collective-permute-start.23 = (bf16[32,512]{1,0:T(8,128)(2,1)S(1)}, bf16[32,512]{1,0:T(8,128)(2,1)S(1)}, u32[]{:S(2)}, u32[]{:S(2)}) collective-permute-start(bf16[32,512]{1,0:T(8,128)(2,1)S(1)} %get-tuple-element.43), channel_id=1, source_target_pairs={{0,32},{1,33},{2,34},{3,35},{4,36},{5,37},{6,38},{7,39},{8,40},{9,... | collective-permute-start | bytes 98312 | tf_op jit(solution)/shard_map/ppermute | solution.py:262
  89.9 1.7 %fusion = bf16[1,128,512]{2,1,0:T(8,128)(2,1)} fusion(f32[128,512]{1,0:T(8,128)} %get-tuple-element.35, bf16[128,512]{1,0:T(8,128)(2,1)S(1)} %collective-permute-done.22, bf16[128,512]{1,0:T(8,128)(2,1)S(1)} %collective-permute-done.21, bf16[128,512]{1,0:T(8,128)(2,1)S(1)} %collective-permute-done.20, bf16[128,512]{1,0:T(8,128)(2,1)S(1)} %collective-permute-done.19), kind=kLoop, calls=%fused_computation.2 | loop fusion | flops 589824 | bytes 917504 | tf_op jit(solution)/shard_map/broadcast_in_dim | solution.py:305
  91.6 2.3 %collective-permute-done.24 = bf16[32,512]{1,0:T(8,128)(2,1)S(1)} collective-permute-done((bf16[32,512]{1,0:T(8,128)(2,1)S(1)}, bf16[32,512]{1,0:T(8,128)(2,1)S(1)}, u32[]{:S(2)}, u32[]{:S(2)}) %collective-permute-start.24) | collective-permute-done | bytes 32800 | tf_op jit(solution)/shard_map/ppermute | solution.py:262
  (64 shorter events, 3.7 us)
Async XLA Ops:
  0.6 17.2 %collective-permute-start = (bf16[128,512]{1,0:T(8,128)(2,1)}, bf16[128,512]{1,0:T(8,128)(2,1)S(1)}, u32[]{:S(2)}, u32[]{:S(2)}) collective-permute-start(bf16[128,512]{1,0:T(8,128)(2,1)} %bitcast.15), channel_id=1, source_target_pairs={{0,1},{1,2},{2,3},{3,4},{4,5},{5,6},{6,7},{7,0},{8,9},{9,10},{10,1... | collective-permute-start | bytes 393224 | tf_op jit(solution)/shard_map/ppermute | solution.py:266
  2.1 15.8 %collective-permute-start.1 = (bf16[128,512]{1,0:T(8,128)(2,1)}, bf16[128,512]{1,0:T(8,128)(2,1)S(1)}, u32[]{:S(2)}, u32[]{:S(2)}) collective-permute-start(bf16[128,512]{1,0:T(8,128)(2,1)} %bitcast.16), channel_id=1, source_target_pairs={{0,2},{1,3},{2,4},{3,5},{4,6},{5,7},{6,0},{7,1},{8,10},{9,11},{10,... | collective-permute-start | bytes 393224 | tf_op jit(solution)/shard_map/ppermute | solution.py:266
  3.6 14.3 %collective-permute-start.2 = (bf16[128,512]{1,0:T(8,128)(2,1)}, bf16[128,512]{1,0:T(8,128)(2,1)S(1)}, u32[]{:S(2)}, u32[]{:S(2)}) collective-permute-start(bf16[128,512]{1,0:T(8,128)(2,1)} %bitcast.17), channel_id=1, source_target_pairs={{0,3},{1,4},{2,5},{3,6},{4,7},{5,0},{6,1},{7,2},{8,11},{9,12},{10,... | collective-permute-start | bytes 393224 | tf_op jit(solution)/shard_map/ppermute | solution.py:266
  6.4 11.5 %collective-permute-start.3 = (bf16[128,512]{1,0:T(8,128)(2,1)}, bf16[128,512]{1,0:T(8,128)(2,1)S(1)}, u32[]{:S(2)}, u32[]{:S(2)}) collective-permute-start(bf16[128,512]{1,0:T(8,128)(2,1)} %bitcast.18), channel_id=1, source_target_pairs={{0,4},{1,5},{2,6},{3,7},{4,0},{5,1},{6,2},{7,3},{8,12},{9,13},{10,... | collective-permute-start | bytes 393224 | tf_op jit(solution)/shard_map/ppermute | solution.py:266
  12.9 38.5 %all-to-all-start = ((bf16[8,4,256,128]{3,2,1,0:T(8,128)(2,1)}), bf16[8,4,256,128]{3,2,1,0:T(8,128)(2,1)}, u32[]{:S(2)}, u32[]{:S(2)}) async-start(bf16[8,4,256,128]{3,2,1,0:T(8,128)(2,1)} %deal_inputs.1), calls=%async_computation | async-start | bytes 4194304 | tf_op jit(solution)/shard_map/all_to_all | solution.py:285
  22.8 7.8 %collective-permute-start.11 = (bf16[128,512]{1,0:T(8,128)(2,1)S(1)}, bf16[128,512]{1,0:T(8,128)(2,1)S(1)}, u32[]{:S(2)}, u32[]{:S(2)}) collective-permute-start(bf16[128,512]{1,0:T(8,128)(2,1)S(1)} %get-tuple-element.31), channel_id=1, source_target_pairs={{0,4},{1,5},{2,6},{3,7},{4,0},{5,1},{6,2},{7,3},{8,12},{9,13},{10,... | collective-permute-start | bytes 393224 | tf_op jit(solution)/shard_map/ppermute | solution.py:266
  25.0 8.7 %collective-permute-start.10 = (bf16[128,512]{1,0:T(8,128)(2,1)S(1)}, bf16[128,512]{1,0:T(8,128)(2,1)S(1)}, u32[]{:S(2)}, u32[]{:S(2)}) collective-permute-start(bf16[128,512]{1,0:T(8,128)(2,1)S(1)} %get-tuple-element.30), channel_id=1, source_target_pairs={{0,5},{1,6},{2,7},{3,0},{4,1},{5,2},{6,3},{7,4},{8,13},{9,14},{10,... | collective-permute-start | bytes 393224 | tf_op jit(solution)/shard_map/ppermute | solution.py:266
  27.6 8.6 %collective-permute-start.9 = (bf16[128,512]{1,0:T(8,128)(2,1)S(1)}, bf16[128,512]{1,0:T(8,128)(2,1)S(1)}, u32[]{:S(2)}, u32[]{:S(2)}) collective-permute-start(bf16[128,512]{1,0:T(8,128)(2,1)S(1)} %get-tuple-element.29), channel_id=1, source_target_pairs={{0,6},{1,7},{2,0},{3,1},{4,2},{5,3},{6,4},{7,5},{8,14},{9,15},{10,... | collective-permute-start | bytes 393224 | tf_op jit(solution)/shard_map/ppermute | solution.py:266
  27.6 11.9 %collective-permute-start.8 = (bf16[128,512]{1,0:T(8,128)(2,1)S(1)}, bf16[128,512]{1,0:T(8,128)(2,1)S(1)}, u32[]{:S(2)}, u32[]{:S(2)}) collective-permute-start(bf16[128,512]{1,0:T(8,128)(2,1)S(1)} %get-tuple-element.28), channel_id=1, source_target_pairs={{0,7},{1,0},{2,1},{3,2},{4,3},{5,4},{6,5},{7,6},{8,15},{9,8},{10,9... | collective-permute-start | bytes 393224 | tf_op jit(solution)/shard_map/ppermute | solution.py:266
  29.3 14.0 %collective-permute-start.4 = (bf16[128,512]{1,0:T(8,128)(2,1)S(1)}, bf16[128,512]{1,0:T(8,128)(2,1)S(1)}, u32[]{:S(2)}, u32[]{:S(2)}) collective-permute-start(bf16[128,512]{1,0:T(8,128)(2,1)S(1)} %get-tuple-element.25), channel_id=1, source_target_pairs={{0,1},{1,2},{2,3},{3,4},{4,5},{5,6},{6,7},{7,0},{8,9},{9,10},{10,1... | collective-permute-start | bytes 393224 | tf_op jit(solution)/shard_map/ppermute | solution.py:266
  30.6 13.3 %collective-permute-start.5 = (bf16[128,512]{1,0:T(8,128)(2,1)S(1)}, bf16[128,512]{1,0:T(8,128)(2,1)S(1)}, u32[]{:S(2)}, u32[]{:S(2)}) collective-permute-start(bf16[128,512]{1,0:T(8,128)(2,1)S(1)} %get-tuple-element.25), channel_id=1, source_target_pairs={{0,2},{1,3},{2,4},{3,5},{4,6},{5,7},{6,0},{7,1},{8,10},{9,11},{10,... | collective-permute-start | bytes 393224 | tf_op jit(solution)/shard_map/ppermute | solution.py:266
  33.8 13.4 %collective-permute-start.6 = (bf16[128,512]{1,0:T(8,128)(2,1)S(1)}, bf16[128,512]{1,0:T(8,128)(2,1)S(1)}, u32[]{:S(2)}, u32[]{:S(2)}) collective-permute-start(bf16[128,512]{1,0:T(8,128)(2,1)S(1)} %get-tuple-element.25), channel_id=1, source_target_pairs={{0,3},{1,4},{2,5},{3,6},{4,7},{5,0},{6,1},{7,2},{8,11},{9,12},{10,... | collective-permute-start | bytes 393224 | tf_op jit(solution)/shard_map/ppermute | solution.py:266
  39.6 15.6 %copy-start = (bf16[128,512]{1,0:T(8,128)(2,1)}, bf16[128,512]{1,0:T(8,128)(2,1)S(1)}, u32[]{:S(2)}) copy-start(bf16[128,512]{1,0:T(8,128)(2,1)S(1)} %add_convert_fusion.1.refs_0_) | copy-start | bytes 393220
  39.6 8.1 %collective-permute-start.12 = (bf16[128,512]{1,0:T(8,128)(2,1)S(1)}, bf16[128,512]{1,0:T(8,128)(2,1)S(1)}, u32[]{:S(2)}, u32[]{:S(2)}) collective-permute-start(bf16[128,512]{1,0:T(8,128)(2,1)S(1)} %add_convert_fusion.1.refs_0_), channel_id=1, source_target_pairs={{0,129},{1,128},{2,131},{3,130},{4,133},{5,132},{6,135},{7,134},{8... | collective-permute-start | bytes 393224 | tf_op jit(solution)/shard_map/ppermute | solution.py:262
  41.8 6.1 %collective-permute-start.13 = (bf16[128,512]{1,0:T(8,128)(2,1)S(1)}, bf16[128,512]{1,0:T(8,128)(2,1)S(1)}, u32[]{:S(2)}, u32[]{:S(2)}) collective-permute-start(bf16[128,512]{1,0:T(8,128)(2,1)S(1)} %add_convert_fusion.1.refs_0_), channel_id=1, source_target_pairs={{0,16},{1,17},{2,18},{3,19},{4,20},{5,21},{6,22},{7,23},{8,24},{9,... | collective-permute-start | bytes 393224 | tf_op jit(solution)/shard_map/ppermute | solution.py:262
  43.3 11.9 %copy-start.1 = (bf16[128,512]{1,0:T(8,128)(2,1)}, bf16[128,512]{1,0:T(8,128)(2,1)S(1)}, u32[]{:S(2)}) copy-start(bf16[128,512]{1,0:T(8,128)(2,1)S(1)} %collective-permute-done.4.refs_8_.v1) | copy-start | bytes 393220
  43.3 6.7 %collective-permute-start.14 = (bf16[128,512]{1,0:T(8,128)(2,1)S(1)}, bf16[128,512]{1,0:T(8,128)(2,1)S(1)}, u32[]{:S(2)}, u32[]{:S(2)}) collective-permute-start(bf16[128,512]{1,0:T(8,128)(2,1)S(1)} %add_convert_fusion.1.refs_0_), channel_id=1, source_target_pairs={{0,145},{1,144},{2,147},{3,146},{4,149},{5,148},{6,151},{7,150},{8... | collective-permute-start | bytes 393224 | tf_op jit(solution)/shard_map/ppermute | solution.py:262
  43.9 11.3 %copy-start.2 = (bf16[128,512]{1,0:T(8,128)(2,1)}, bf16[128,512]{1,0:T(8,128)(2,1)S(1)}, u32[]{:S(2)}) copy-start(bf16[128,512]{1,0:T(8,128)(2,1)S(1)} %collective-permute-done.5.refs_9_.v2) | copy-start | bytes 393220
  43.9 6.5 %collective-permute-start.7 = (bf16[128,512]{1,0:T(8,128)(2,1)S(1)}, bf16[128,512]{1,0:T(8,128)(2,1)S(1)}, u32[]{:S(2)}, u32[]{:S(2)}) collective-permute-start(bf16[128,512]{1,0:T(8,128)(2,1)S(1)} %get-tuple-element.25), channel_id=1, source_target_pairs={{0,4},{1,5},{2,6},{3,7},{4,0},{5,1},{6,2},{7,3},{8,12},{9,13},{10,... | collective-permute-start | bytes 393224 | tf_op jit(solution)/shard_map/ppermute | solution.py:266
  47.2 8.0 %copy-start.3 = (bf16[128,512]{1,0:T(8,128)(2,1)}, bf16[128,512]{1,0:T(8,128)(2,1)S(1)}, u32[]{:S(2)}) copy-start(bf16[128,512]{1,0:T(8,128)(2,1)S(1)} %collective-permute-done.6.refs_10_.v3) | copy-start | bytes 393220
  47.2 3.2 %collective-permute-start.15 = (bf16[128,512]{1,0:T(8,128)(2,1)S(1)}, bf16[128,512]{1,0:T(8,128)(2,1)S(1)}, u32[]{:S(2)}, u32[]{:S(2)}) collective-permute-start(bf16[128,512]{1,0:T(8,128)(2,1)S(1)} %add_convert_fusion.1.refs_0_), channel_id=1, source_target_pairs={{0,8},{1,9},{2,10},{3,11},{4,12},{5,13},{6,14},{7,15},{8,0},{9,1},... | collective-permute-start | bytes 393224 | tf_op jit(solution)/shard_map/ppermute | solution.py:262
  47.8 2.6 %collective-permute-start.16 = (bf16[128,512]{1,0:T(8,128)(2,1)S(1)}, bf16[128,512]{1,0:T(8,128)(2,1)S(1)}, u32[]{:S(2)}, u32[]{:S(2)}) collective-permute-start(bf16[128,512]{1,0:T(8,128)(2,1)S(1)} %collective-permute-done.12.refs_1_), channel_id=1, source_target_pairs={{0,8},{1,9},{2,10},{3,11},{4,12},{5,13},{6,14},{7,15},{8,0},{9,1},... | collective-permute-start | bytes 393224 | tf_op jit(solution)/shard_map/ppermute | solution.py:262
  47.9 2.5 %collective-permute-start.17 = (bf16[128,512]{1,0:T(8,128)(2,1)S(1)}, bf16[128,512]{1,0:T(8,128)(2,1)S(1)}, u32[]{:S(2)}, u32[]{:S(2)}) collective-permute-start(bf16[128,512]{1,0:T(8,128)(2,1)S(1)} %collective-permute-done.13.refs_2_), channel_id=1, source_target_pairs={{0,8},{1,9},{2,10},{3,11},{4,12},{5,13},{6,14},{7,15},{8,0},{9,1},... | collective-permute-start | bytes 393224 | tf_op jit(solution)/shard_map/ppermute | solution.py:262
  50.0 1.3 %collective-permute-start.18 = (bf16[128,512]{1,0:T(8,128)(2,1)S(1)}, bf16[128,512]{1,0:T(8,128)(2,1)S(1)}, u32[]{:S(2)}, u32[]{:S(2)}) collective-permute-start(bf16[128,512]{1,0:T(8,128)(2,1)S(1)} %collective-permute-done.14.refs_3_), channel_id=1, source_target_pairs={{0,8},{1,9},{2,10},{3,11},{4,12},{5,13},{6,14},{7,15},{8,0},{9,1},... | collective-permute-start | bytes 393224 | tf_op jit(solution)/shard_map/ppermute | solution.py:262
  55.3 24.9 %all-to-all-start.1 = ((bf16[8,128,512]{2,1,0:T(8,128)(2,1)}), bf16[8,128,512]{2,1,0:T(8,128)(2,1)S(1)}, u32[]{:S(2)}, u32[]{:S(2)}) async-start(bf16[8,128,512]{2,1,0:T(8,128)(2,1)} %get-tuple-element.41), calls=%async_computation.1 | async-start | bytes 2097152 | tf_op jit(solution)/shard_map/all_to_all | solution.py:296
  72.5 13.6 %collective-permute-start.22 = (bf16[128,512]{1,0:T(8,128)(2,1)}, bf16[128,512]{1,0:T(8,128)(2,1)S(1)}, u32[]{:S(2)}, u32[]{:S(2)}) collective-permute-start(bf16[128,512]{1,0:T(8,128)(2,1)} %get-tuple-element.39), channel_id=1, source_target_pairs={{0,4},{1,5},{2,6},{3,7},{4,0},{5,1},{6,2},{7,3},{8,12},{9,13},{10,... | collective-permute-start | bytes 393224 | tf_op jit(solution)/shard_map/ppermute | solution.py:266
  75.5 11.9 %collective-permute-start.21 = (bf16[128,512]{1,0:T(8,128)(2,1)}, bf16[128,512]{1,0:T(8,128)(2,1)S(1)}, u32[]{:S(2)}, u32[]{:S(2)}) collective-permute-start(bf16[128,512]{1,0:T(8,128)(2,1)} %get-tuple-element.38), channel_id=1, source_target_pairs={{0,5},{1,6},{2,7},{3,0},{4,1},{5,2},{6,3},{7,4},{8,13},{9,14},{10,... | collective-permute-start | bytes 393224 | tf_op jit(solution)/shard_map/ppermute | solution.py:266
  76.7 13.3 %collective-permute-start.20 = (bf16[128,512]{1,0:T(8,128)(2,1)}, bf16[128,512]{1,0:T(8,128)(2,1)S(1)}, u32[]{:S(2)}, u32[]{:S(2)}) collective-permute-start(bf16[128,512]{1,0:T(8,128)(2,1)} %get-tuple-element.37), channel_id=1, source_target_pairs={{0,6},{1,7},{2,0},{3,1},{4,2},{5,3},{6,4},{7,5},{8,14},{9,15},{10,... | collective-permute-start | bytes 393224 | tf_op jit(solution)/shard_map/ppermute | solution.py:266
  76.7 13.3 %collective-permute-start.19 = (bf16[128,512]{1,0:T(8,128)(2,1)}, bf16[128,512]{1,0:T(8,128)(2,1)S(1)}, u32[]{:S(2)}, u32[]{:S(2)}) collective-permute-start(bf16[128,512]{1,0:T(8,128)(2,1)} %get-tuple-element.36), channel_id=1, source_target_pairs={{0,7},{1,0},{2,1},{3,2},{4,3},{5,4},{6,5},{7,6},{8,15},{9,8},{10,9... | collective-permute-start | bytes 393224 | tf_op jit(solution)/shard_map/ppermute | solution.py:266
  80.4 11.2 %collective-permute-start.25 = (bf16[32,512]{1,0:T(8,128)(2,1)S(1)}, bf16[32,512]{1,0:T(8,128)(2,1)S(1)}, u32[]{:S(2)}, u32[]{:S(2)}) collective-permute-start(bf16[32,512]{1,0:T(8,128)(2,1)S(1)} %get-tuple-element.45), channel_id=1, source_target_pairs={{0,96},{1,97},{2,98},{3,99},{4,100},{5,101},{6,102},{7,103},{8,104... | collective-permute-start | bytes 98312 | tf_op jit(solution)/shard_map/ppermute | solution.py:262
  86.1 7.8 %collective-permute-start.24 = (bf16[32,512]{1,0:T(8,128)(2,1)S(1)}, bf16[32,512]{1,0:T(8,128)(2,1)S(1)}, u32[]{:S(2)}, u32[]{:S(2)}) collective-permute-start(bf16[32,512]{1,0:T(8,128)(2,1)S(1)} %get-tuple-element.44), channel_id=1, source_target_pairs={{0,64},{1,65},{2,66},{3,67},{4,68},{5,69},{6,70},{7,71},{8,72},{9,... | collective-permute-start | bytes 98312 | tf_op jit(solution)/shard_map/ppermute | solution.py:262
  87.4 6.5 %collective-permute-start.23 = (bf16[32,512]{1,0:T(8,128)(2,1)S(1)}, bf16[32,512]{1,0:T(8,128)(2,1)S(1)}, u32[]{:S(2)}, u32[]{:S(2)}) collective-permute-start(bf16[32,512]{1,0:T(8,128)(2,1)S(1)} %get-tuple-element.43), channel_id=1, source_target_pairs={{0,32},{1,33},{2,34},{3,35},{4,36},{5,37},{6,38},{7,39},{8,40},{9,... | collective-permute-start | bytes 98312 | tf_op jit(solution)/shard_map/ppermute | solution.py:262
  (12 other events, 49.4 us)

commit v5 on v4

--- a/solution.py
+++ b/solution.py
@@ -103,9 +103,12 @@
 def score_kernel(
     lengths, q, do, k0, k1, k2, k3, k4, v0, v1, v2, v3, v4, stats, dq, own, s1, s2, s3, s4, bias, dsc
 ):
-    fill_bias(lengths, bias)
+    @pl.when(pl.program_id(0) == 0)
+    def _():
+        fill_bias(lengths, bias)
+
     mask = lower()
-    for group in range(GROUPS):
+    for group in range(GROUPS // 2):
         keys, values = blocks((k0, k1, k2, k3, k4), group), blocks((v0, v1, v2, v3, v4), group)
         for pair in range(GROUP // 2):
             lanes = slice(pair * 256, (pair + 1) * 256)
@@ -149,10 +152,17 @@
 
 
 def score_call(lengths, q, do, keys, values, stats):
+    def half(width):
+        return pl.BlockSpec((ROWS, width), lambda n: (0, n))
+
+    wide, narrow = half(GROUPS // 2 * GROUP * HD), half(GROUPS // 2 * HD)
     return pl.pallas_call(
         score_kernel,
-        in_specs=[SMEM] + [VMEM] * 13,
-        out_specs=[VMEM] * 6,
+        grid=(2,),
+        in_specs=[SMEM, wide, wide]
+        + [narrow] * 10
+        + [pl.BlockSpec((GROUPS // 2, 8, GROUP * ROWS), lambda n: (n, 0, 0))],
+        out_specs=[wide] + [narrow] * 5,
         out_shape=[sds((ROWS, GROUPS * GROUP * HD), BF16)] + TERMS,
         scratch_shapes=SCRATCH,
         compiler_params=params(58),

time: 94.9 us -> 94.6 us (level)
  no operation moved by 1% of the time
where the time goes in v5:
time: 94.6 us; the launch traced here: 94.2 us
  starting transfers between devices  55.6 us (59%)
  Pallas kernels  22.3 us (24%)
  waiting for transfers between devices  10.7 us (11%)
  other arithmetic  2.41 us (3%)
  local copies, waits for them, and re-layouts  2.3 us (2%)
    ppermute x16, starting transfers between devices, ring(): lax.ppermute(array, 'ctx', [(n, (n + distance) % 8) for n in range(8)])  29.9 us
    ppermute x10, starting transfers between devices, move(): return lax.ppermute(array, ('dp', 'ctx'), pairs)  14.2 us
    pallas_call x1, Pallas kernels, score_call(): pl.pallas_call(score_kernel, grid=(2,), in_specs=[SMEM, wide, wide] + [na...  10.1 us
    all_to_all x1, starting transfers between devices, shards(): across = lax.all_to_all(away, 'ctx', 0, 0)  6.62 us
    ppermute x10, waiting for transfers between devices, move(): return lax.ppermute(array, ('dp', 'ctx'), pairs)  5.79 us
    all_to_all x1, starting transfers between devices, shards(): lax.all_to_all(dealt, ('dp', 'ctx'), 0, 0, axis_index_groups=members)  4.95 us
    ppermute x16, waiting for transfers between devices, ring(): lax.ppermute(array, 'ctx', [(n, (n + distance) % 8) for n in range(8)])  4.87 us
    pallas_call x1, Pallas kernels, value_call(): pl.pallas_call(value_kernel, in_specs=[SMEM] + [VMEM] * 8, out_specs=[VME...  4.13 us
  transfers between devices with their start and end apart: 28, of which 8 were waited for; matrix products, arithmetic and copies ran while one was open for 2% of the time, Pallas kernels for 20%

profile of v5, /device:TPU:8, one launch (start us, length us, event | category | flops | bytes accessed | tf_op | source)
XLA Modules:
  0.0 94.2 jit_solution(2624985018603628292)
XLA Ops:
  0.6 1.5 %collective-permute-start = (bf16[128,512]{1,0:T(8,128)(2,1)}, bf16[128,512]{1,0:T(8,128)(2,1)S(1)}, u32[]{:S(2)}, u32[]{:S(2)}) collective-permute-start(bf16[128,512]{1,0:T(8,128)(2,1)} %bitcast.15), channel_id=1, source_target_pairs={{0,1},{1,2},{2,3},{3,4},{4,5},{5,6},{6,7},{7,0},{8,9},{9,10},{10,1... | collective-permute-start | bytes 393224 | tf_op jit(solution)/shard_map/ppermute | solution.py:276
  2.1 1.5 %collective-permute-start.1 = (bf16[128,512]{1,0:T(8,128)(2,1)}, bf16[128,512]{1,0:T(8,128)(2,1)S(1)}, u32[]{:S(2)}, u32[]{:S(2)}) collective-permute-start(bf16[128,512]{1,0:T(8,128)(2,1)} %bitcast.16), channel_id=1, source_target_pairs={{0,2},{1,3},{2,4},{3,5},{4,6},{5,7},{6,0},{7,1},{8,10},{9,11},{10,... | collective-permute-start | bytes 393224 | tf_op jit(solution)/shard_map/ppermute | solution.py:276
  3.6 2.8 %collective-permute-start.2 = (bf16[128,512]{1,0:T(8,128)(2,1)}, bf16[128,512]{1,0:T(8,128)(2,1)S(1)}, u32[]{:S(2)}, u32[]{:S(2)}) collective-permute-start(bf16[128,512]{1,0:T(8,128)(2,1)} %bitcast.17), channel_id=1, source_target_pairs={{0,3},{1,4},{2,5},{3,6},{4,7},{5,0},{6,1},{7,2},{8,11},{9,12},{10,... | collective-permute-start | bytes 393224 | tf_op jit(solution)/shard_map/ppermute | solution.py:276
  6.4 0.8 collective-permute-start.3
  7.2 1.6 %copy-done.5 = bf16[1,128,8192]{2,1,0:T(8,128)(2,1)S(1)} copy-done((bf16[1,128,8192]{2,1,0:T(8,128)(2,1)S(1)}, bf16[1,128,8192]{2,1,0:T(8,128)(2,1)}, u32[]{:S(2)}) %copy-start.5) | copy-done | bytes 2097176
  8.8 4.1 %deal_inputs.1 = bf16[8,4,256,128]{3,2,1,0:T(8,128)(2,1)} custom-call(bf16[128,8192]{1,0:T(8,128)(2,1)S(1)} %bitcast.10), custom_call_target="tpu_custom_call" | custom-call | flops 2000000000 | bytes 4000000 | tf_op jit(solution)/shard_map/deal_inputs/pallas_call | solution.py:192
  12.9 5.0 %all-to-all-start = ((bf16[8,4,256,128]{3,2,1,0:T(8,128)(2,1)}), bf16[8,4,256,128]{3,2,1,0:T(8,128)(2,1)}, u32[]{:S(2)}, u32[]{:S(2)}) async-start(bf16[8,4,256,128]{3,2,1,0:T(8,128)(2,1)} %deal_inputs.1), calls=%async_computation | async-start | bytes 4194304 | tf_op jit(solution)/shard_map/all_to_all | solution.py:295
  17.9 4.1 %value_grad.1 = (bf16[128,512]{1,0:T(8,128)(2,1)S(1)}, f32[128,512]{1,0:T(8,128)S(1)}, bf16[128,512]{1,0:T(8,128)(2,1)S(1)}, bf16[128,512]{1,0:T(8,128)(2,1)S(1)...) custom-call(s32[1,8]{1,0:T(1,128)S(1)} %copy-done.14, ...), custom_call_target="tpu_custom_call" | custom-call | flops 149999992832 | bytes 4000000 | tf_op jit(solution)/shard_map/value_grad/pallas_call | solution.py:142
  22.8 2.3 %collective-permute-start.11 = (bf16[128,512]{1,0:T(8,128)(2,1)S(1)}, bf16[128,512]{1,0:T(8,128)(2,1)S(1)}, u32[]{:S(2)}, u32[]{:S(2)}) collective-permute-start(bf16[128,512]{1,0:T(8,128)(2,1)S(1)} %get-tuple-element.31), channel_id=1, source_target_pairs={{0,4},{1,5},{2,6},{3,7},{4,0},{5,1},{6,2},{7,3},{8,12},{9,13},{10,... | collective-permute-start | bytes 393224 | tf_op jit(solution)/shard_map/ppermute | solution.py:276
  25.0 2.6 %collective-permute-start.10 = (bf16[128,512]{1,0:T(8,128)(2,1)S(1)}, bf16[128,512]{1,0:T(8,128)(2,1)S(1)}, u32[]{:S(2)}, u32[]{:S(2)}) collective-permute-start(bf16[128,512]{1,0:T(8,128)(2,1)S(1)} %get-tuple-element.30), channel_id=1, source_target_pairs={{0,5},{1,6},{2,7},{3,0},{4,1},{5,2},{6,3},{7,4},{8,13},{9,14},{10,... | collective-permute-start | bytes 393224 | tf_op jit(solution)/shard_map/ppermute | solution.py:276
  27.6 1.7 %collective-permute-start.8 = (bf16[128,512]{1,0:T(8,128)(2,1)S(1)}, bf16[128,512]{1,0:T(8,128)(2,1)S(1)}, u32[]{:S(2)}, u32[]{:S(2)}) collective-permute-start(bf16[128,512]{1,0:T(8,128)(2,1)S(1)} %get-tuple-element.28), channel_id=1, source_target_pairs={{0,7},{1,0},{2,1},{3,2},{4,3},{5,4},{6,5},{7,6},{8,15},{9,8},{10,9... | collective-permute-start | bytes 393224 | tf_op jit(solution)/shard_map/ppermute | solution.py:276
  29.3 1.3 %collective-permute-start.4 = (bf16[128,512]{1,0:T(8,128)(2,1)S(1)}, bf16[128,512]{1,0:T(8,128)(2,1)S(1)}, u32[]{:S(2)}, u32[]{:S(2)}) collective-permute-start(bf16[128,512]{1,0:T(8,128)(2,1)S(1)} %get-tuple-element.25), channel_id=1, source_target_pairs={{0,1},{1,2},{2,3},{3,4},{4,5},{5,6},{6,7},{7,0},{8,9},{9,10},{10,1... | collective-permute-start | bytes 393224 | tf_op jit(solution)/shard_map/ppermute | solution.py:276
  30.6 2.0 %collective-permute-start.5 = (bf16[128,512]{1,0:T(8,128)(2,1)S(1)}, bf16[128,512]{1,0:T(8,128)(2,1)S(1)}, u32[]{:S(2)}, u32[]{:S(2)}) collective-permute-start(bf16[128,512]{1,0:T(8,128)(2,1)S(1)} %get-tuple-element.25), channel_id=1, source_target_pairs={{0,2},{1,3},{2,4},{3,5},{4,6},{5,7},{6,0},{7,1},{8,10},{9,11},{10,... | collective-permute-start | bytes 393224 | tf_op jit(solution)/shard_map/ppermute | solution.py:276
  32.6 1.2 %collective-permute-done.10 = bf16[128,512]{1,0:T(8,128)(2,1)S(1)} collective-permute-done((bf16[128,512]{1,0:T(8,128)(2,1)S(1)}, bf16[128,512]{1,0:T(8,128)(2,1)S(1)}, u32[]{:S(2)}, u32[]{:S(2)}) %collective-permute-start.10) | collective-permute-done | bytes 131104 | tf_op jit(solution)/shard_map/ppermute | solution.py:276
  33.8 2.5 %collective-permute-start.6 = (bf16[128,512]{1,0:T(8,128)(2,1)S(1)}, bf16[128,512]{1,0:T(8,128)(2,1)S(1)}, u32[]{:S(2)}, u32[]{:S(2)}) collective-permute-start(bf16[128,512]{1,0:T(8,128)(2,1)S(1)} %get-tuple-element.25), channel_id=1, source_target_pairs={{0,3},{1,4},{2,5},{3,6},{4,7},{5,0},{6,1},{7,2},{8,11},{9,12},{10,... | collective-permute-start | bytes 393224 | tf_op jit(solution)/shard_map/ppermute | solution.py:276
  36.2 3.3 %collective-permute-done.8 = bf16[128,512]{1,0:T(8,128)(2,1)S(1)} collective-permute-done((bf16[128,512]{1,0:T(8,128)(2,1)S(1)}, bf16[128,512]{1,0:T(8,128)(2,1)S(1)}, u32[]{:S(2)}, u32[]{:S(2)}) %collective-permute-start.8) | collective-permute-done | bytes 131104 | tf_op jit(solution)/shard_map/ppermute | solution.py:276
  39.6 2.2 %collective-permute-start.12 = (bf16[128,512]{1,0:T(8,128)(2,1)S(1)}, bf16[128,512]{1,0:T(8,128)(2,1)S(1)}, u32[]{:S(2)}, u32[]{:S(2)}) collective-permute-start(bf16[128,512]{1,0:T(8,128)(2,1)S(1)} %add_convert_fusion.1.refs_0_), channel_id=1, source_target_pairs={{0,129},{1,128},{2,131},{3,130},{4,133},{5,132},{6,135},{7,134},{8... | collective-permute-start | bytes 393224 | tf_op jit(solution)/shard_map/ppermute | solution.py:272
  41.8 1.5 %collective-permute-start.13 = (bf16[128,512]{1,0:T(8,128)(2,1)S(1)}, bf16[128,512]{1,0:T(8,128)(2,1)S(1)}, u32[]{:S(2)}, u32[]{:S(2)}) collective-permute-start(bf16[128,512]{1,0:T(8,128)(2,1)S(1)} %add_convert_fusion.1.refs_0_), channel_id=1, source_target_pairs={{0,16},{1,17},{2,18},{3,19},{4,20},{5,21},{6,22},{7,23},{8,24},{9,... | collective-permute-start | bytes 393224 | tf_op jit(solution)/shard_map/ppermute | solution.py:272
  43.9 3.3 %collective-permute-start.7 = (bf16[128,512]{1,0:T(8,128)(2,1)S(1)}, bf16[128,512]{1,0:T(8,128)(2,1)S(1)}, u32[]{:S(2)}, u32[]{:S(2)}) collective-permute-start(bf16[128,512]{1,0:T(8,128)(2,1)S(1)} %get-tuple-element.25), channel_id=1, source_target_pairs={{0,4},{1,5},{2,6},{3,7},{4,0},{5,1},{6,2},{7,3},{8,12},{9,13},{10,... | collective-permute-start | bytes 393224 | tf_op jit(solution)/shard_map/ppermute | solution.py:276
  48.3 1.8 %collective-permute-done.14.refs_3_ = bf16[128,512]{1,0:T(8,128)(2,1)S(1)} collective-permute-done((bf16[128,512]{1,0:T(8,128)(2,1)S(1)}, bf16[128,512]{1,0:T(8,128)(2,1)S(1)}, u32[]{:S(2)}, u32[]{:S(2)}) %collective-permute-start.14) | collective-permute-done | bytes 131104 | tf_op jit(solution)/shard_map/ppermute | solution.py:272
  50.4 1.0 %collective-permute-done.18.refs_7_ = bf16[128,512]{1,0:T(8,128)(2,1)S(1)} collective-permute-done((bf16[128,512]{1,0:T(8,128)(2,1)S(1)}, bf16[128,512]{1,0:T(8,128)(2,1)S(1)}, u32[]{:S(2)}, u32[]{:S(2)}) %collective-permute-start.18) | collective-permute-done | bytes 131104 | tf_op jit(solution)/shard_map/ppermute | solution.py:272
  51.4 3.8 %weight_grad.1 = (f32[128,512]{1,0:T(8,128)S(1)}, bf16[8,128,512]{2,1,0:T(8,128)(2,1)}) custom-call(bf16[8,4,256,128]{3,2,1,0:T(8,128)(2,1)} %all-to-all-done.inputs, bf16[128,512]{1,0:T(8,128)(2,1)S(1)} %add_convert_fusion.1.refs_0_, bf16[128,512]{1,0:T(8,128)(2,1)S(1)} %collective-permute-done.12.refs_1_, ...), custom_call_target="tpu_custom_call" | custom-call | flops 1000000 | bytes 10000 | tf_op jit(solution)/shard_map/weight_grad/pallas_call | solution.py:223
  55.3 6.6 %all-to-all-start.1 = ((bf16[8,128,512]{2,1,0:T(8,128)(2,1)}), bf16[8,128,512]{2,1,0:T(8,128)(2,1)S(1)}, u32[]{:S(2)}, u32[]{:S(2)}) async-start(bf16[8,128,512]{2,1,0:T(8,128)(2,1)} %get-tuple-element.41), calls=%async_computation.1 | async-start | bytes 2097152 | tf_op jit(solution)/shard_map/all_to_all | solution.py:306
  61.9 10.1 %score_grad.1 = (bf16[128,4096]{1,0:T(8,128)(2,1)}, f32[128,512]{1,0:T(8,128)}, bf16[128,512]{1,0:T(8,128)(2,1)}, bf16[128,512]{1,0:T(8,128)(2,1)}, bf16[128,512]{1,0:T(8,128)(2,1)}, /*index=5*/bf16[128,512]{1,0:T(8,128)(2,1)}) custom-call(s32[1,8]{1,0:T(1,128)} %lengths.3, bf16[128,4096]{1,0:T(8,128)(2,1)} %bitcast.11, bf16[128,4096]{1,0:T(8,128)(2,1)} %bitcast.13, ...), custom_call_target="tpu_custom_call" | custom-call | flops 40000000000 | bytes 4000000 | tf_op jit(solution)/shard_map/score_grad/pallas_call | solution.py:159
  72.0 3.1 %collective-permute-start.22 = (bf16[128,512]{1,0:T(8,128)(2,1)}, bf16[128,512]{1,0:T(8,128)(2,1)S(1)}, u32[]{:S(2)}, u32[]{:S(2)}) collective-permute-start(bf16[128,512]{1,0:T(8,128)(2,1)} %get-tuple-element.39), channel_id=1, source_target_pairs={{0,4},{1,5},{2,6},{3,7},{4,0},{5,1},{6,2},{7,3},{8,12},{9,13},{10,... | collective-permute-start | bytes 393224 | tf_op jit(solution)/shard_map/ppermute | solution.py:276
  75.1 1.2 %collective-permute-start.21 = (bf16[128,512]{1,0:T(8,128)(2,1)}, bf16[128,512]{1,0:T(8,128)(2,1)S(1)}, u32[]{:S(2)}, u32[]{:S(2)}) collective-permute-start(bf16[128,512]{1,0:T(8,128)(2,1)} %get-tuple-element.38), channel_id=1, source_target_pairs={{0,5},{1,6},{2,7},{3,0},{4,1},{5,2},{6,3},{7,4},{8,13},{9,14},{10,... | collective-permute-start | bytes 393224 | tf_op jit(solution)/shard_map/ppermute | solution.py:276
  76.2 3.5 %collective-permute-start.19 = (bf16[128,512]{1,0:T(8,128)(2,1)}, bf16[128,512]{1,0:T(8,128)(2,1)S(1)}, u32[]{:S(2)}, u32[]{:S(2)}) collective-permute-start(bf16[128,512]{1,0:T(8,128)(2,1)} %get-tuple-element.36), channel_id=1, source_target_pairs={{0,7},{1,0},{2,1},{3,2},{4,3},{5,4},{6,5},{7,6},{8,15},{9,8},{10,9... | collective-permute-start | bytes 393224 | tf_op jit(solution)/shard_map/ppermute | solution.py:276
  80.0 5.7 %collective-permute-start.25 = (bf16[32,512]{1,0:T(8,128)(2,1)S(1)}, bf16[32,512]{1,0:T(8,128)(2,1)S(1)}, u32[]{:S(2)}, u32[]{:S(2)}) collective-permute-start(bf16[32,512]{1,0:T(8,128)(2,1)S(1)} %get-tuple-element.45), channel_id=1, source_target_pairs={{0,96},{1,97},{2,98},{3,99},{4,100},{5,101},{6,102},{7,103},{8,104... | collective-permute-start | bytes 98312 | tf_op jit(solution)/shard_map/ppermute | solution.py:272
  85.7 1.3 %collective-permute-start.24 = (bf16[32,512]{1,0:T(8,128)(2,1)S(1)}, bf16[32,512]{1,0:T(8,128)(2,1)S(1)}, u32[]{:S(2)}, u32[]{:S(2)}) collective-permute-start(bf16[32,512]{1,0:T(8,128)(2,1)S(1)} %get-tuple-element.44), channel_id=1, source_target_pairs={{0,64},{1,65},{2,66},{3,67},{4,68},{5,69},{6,70},{7,71},{8,72},{9,... | collective-permute-start | bytes 98312 | tf_op jit(solution)/shard_map/ppermute | solution.py:272
  87.0 2.5 %collective-permute-start.23 = (bf16[32,512]{1,0:T(8,128)(2,1)S(1)}, bf16[32,512]{1,0:T(8,128)(2,1)S(1)}, u32[]{:S(2)}, u32[]{:S(2)}) collective-permute-start(bf16[32,512]{1,0:T(8,128)(2,1)S(1)} %get-tuple-element.43), channel_id=1, source_target_pairs={{0,32},{1,33},{2,34},{3,35},{4,36},{5,37},{6,38},{7,39},{8,40},{9,... | collective-permute-start | bytes 98312 | tf_op jit(solution)/shard_map/ppermute | solution.py:272
  89.5 1.7 %fusion = bf16[1,128,512]{2,1,0:T(8,128)(2,1)} fusion(f32[128,512]{1,0:T(8,128)} %get-tuple-element.35, bf16[128,512]{1,0:T(8,128)(2,1)S(1)} %collective-permute-done.22, bf16[128,512]{1,0:T(8,128)(2,1)S(1)} %collective-permute-done.21, bf16[128,512]{1,0:T(8,128)(2,1)S(1)} %collective-permute-done.20, bf16[128,512]{1,0:T(8,128)(2,1)S(1)} %collective-permute-done.19), kind=kLoop, calls=%fused_computation.2 | loop fusion | flops 589824 | bytes 917504 | tf_op jit(solution)/shard_map/broadcast_in_dim | solution.py:315
  91.2 2.3 %collective-permute-done.24 = bf16[32,512]{1,0:T(8,128)(2,1)S(1)} collective-permute-done((bf16[32,512]{1,0:T(8,128)(2,1)S(1)}, bf16[32,512]{1,0:T(8,128)(2,1)S(1)}, u32[]{:S(2)}, u32[]{:S(2)}) %collective-permute-start.24) | collective-permute-done | bytes 32800 | tf_op jit(solution)/shard_map/ppermute | solution.py:272
  (64 shorter events, 3.7 us)
Async XLA Ops:
  0.6 17.2 %collective-permute-start = (bf16[128,512]{1,0:T(8,128)(2,1)}, bf16[128,512]{1,0:T(8,128)(2,1)S(1)}, u32[]{:S(2)}, u32[]{:S(2)}) collective-permute-start(bf16[128,512]{1,0:T(8,128)(2,1)} %bitcast.15), channel_id=1, source_target_pairs={{0,1},{1,2},{2,3},{3,4},{4,5},{5,6},{6,7},{7,0},{8,9},{9,10},{10,1... | collective-permute-start | bytes 393224 | tf_op jit(solution)/shard_map/ppermute | solution.py:276
  2.1 15.8 %collective-permute-start.1 = (bf16[128,512]{1,0:T(8,128)(2,1)}, bf16[128,512]{1,0:T(8,128)(2,1)S(1)}, u32[]{:S(2)}, u32[]{:S(2)}) collective-permute-start(bf16[128,512]{1,0:T(8,128)(2,1)} %bitcast.16), channel_id=1, source_target_pairs={{0,2},{1,3},{2,4},{3,5},{4,6},{5,7},{6,0},{7,1},{8,10},{9,11},{10,... | collective-permute-start | bytes 393224 | tf_op jit(solution)/shard_map/ppermute | solution.py:276
  3.6 14.3 %collective-permute-start.2 = (bf16[128,512]{1,0:T(8,128)(2,1)}, bf16[128,512]{1,0:T(8,128)(2,1)S(1)}, u32[]{:S(2)}, u32[]{:S(2)}) collective-permute-start(bf16[128,512]{1,0:T(8,128)(2,1)} %bitcast.17), channel_id=1, source_target_pairs={{0,3},{1,4},{2,5},{3,6},{4,7},{5,0},{6,1},{7,2},{8,11},{9,12},{10,... | collective-permute-start | bytes 393224 | tf_op jit(solution)/shard_map/ppermute | solution.py:276
  6.4 11.5 %collective-permute-start.3 = (bf16[128,512]{1,0:T(8,128)(2,1)}, bf16[128,512]{1,0:T(8,128)(2,1)S(1)}, u32[]{:S(2)}, u32[]{:S(2)}) collective-permute-start(bf16[128,512]{1,0:T(8,128)(2,1)} %bitcast.18), channel_id=1, source_target_pairs={{0,4},{1,5},{2,6},{3,7},{4,0},{5,1},{6,2},{7,3},{8,12},{9,13},{10,... | collective-permute-start | bytes 393224 | tf_op jit(solution)/shard_map/ppermute | solution.py:276
  12.9 38.5 %all-to-all-start = ((bf16[8,4,256,128]{3,2,1,0:T(8,128)(2,1)}), bf16[8,4,256,128]{3,2,1,0:T(8,128)(2,1)}, u32[]{:S(2)}, u32[]{:S(2)}) async-start(bf16[8,4,256,128]{3,2,1,0:T(8,128)(2,1)} %deal_inputs.1), calls=%async_computation | async-start | bytes 4194304 | tf_op jit(solution)/shard_map/all_to_all | solution.py:295
  22.8 7.8 %collective-permute-start.11 = (bf16[128,512]{1,0:T(8,128)(2,1)S(1)}, bf16[128,512]{1,0:T(8,128)(2,1)S(1)}, u32[]{:S(2)}, u32[]{:S(2)}) collective-permute-start(bf16[128,512]{1,0:T(8,128)(2,1)S(1)} %get-tuple-element.31), channel_id=1, source_target_pairs={{0,4},{1,5},{2,6},{3,7},{4,0},{5,1},{6,2},{7,3},{8,12},{9,13},{10,... | collective-permute-start | bytes 393224 | tf_op jit(solution)/shard_map/ppermute | solution.py:276
  25.0 8.7 %collective-permute-start.10 = (bf16[128,512]{1,0:T(8,128)(2,1)S(1)}, bf16[128,512]{1,0:T(8,128)(2,1)S(1)}, u32[]{:S(2)}, u32[]{:S(2)}) collective-permute-start(bf16[128,512]{1,0:T(8,128)(2,1)S(1)} %get-tuple-element.30), channel_id=1, source_target_pairs={{0,5},{1,6},{2,7},{3,0},{4,1},{5,2},{6,3},{7,4},{8,13},{9,14},{10,... | collective-permute-start | bytes 393224 | tf_op jit(solution)/shard_map/ppermute | solution.py:276
  27.6 8.6 %collective-permute-start.9 = (bf16[128,512]{1,0:T(8,128)(2,1)S(1)}, bf16[128,512]{1,0:T(8,128)(2,1)S(1)}, u32[]{:S(2)}, u32[]{:S(2)}) collective-permute-start(bf16[128,512]{1,0:T(8,128)(2,1)S(1)} %get-tuple-element.29), channel_id=1, source_target_pairs={{0,6},{1,7},{2,0},{3,1},{4,2},{5,3},{6,4},{7,5},{8,14},{9,15},{10,... | collective-permute-start | bytes 393224 | tf_op jit(solution)/shard_map/ppermute | solution.py:276
  27.6 11.9 %collective-permute-start.8 = (bf16[128,512]{1,0:T(8,128)(2,1)S(1)}, bf16[128,512]{1,0:T(8,128)(2,1)S(1)}, u32[]{:S(2)}, u32[]{:S(2)}) collective-permute-start(bf16[128,512]{1,0:T(8,128)(2,1)S(1)} %get-tuple-element.28), channel_id=1, source_target_pairs={{0,7},{1,0},{2,1},{3,2},{4,3},{5,4},{6,5},{7,6},{8,15},{9,8},{10,9... | collective-permute-start | bytes 393224 | tf_op jit(solution)/shard_map/ppermute | solution.py:276
  29.3 14.0 %collective-permute-start.4 = (bf16[128,512]{1,0:T(8,128)(2,1)S(1)}, bf16[128,512]{1,0:T(8,128)(2,1)S(1)}, u32[]{:S(2)}, u32[]{:S(2)}) collective-permute-start(bf16[128,512]{1,0:T(8,128)(2,1)S(1)} %get-tuple-element.25), channel_id=1, source_target_pairs={{0,1},{1,2},{2,3},{3,4},{4,5},{5,6},{6,7},{7,0},{8,9},{9,10},{10,1... | collective-permute-start | bytes 393224 | tf_op jit(solution)/shard_map/ppermute | solution.py:276
  30.6 13.3 %collective-permute-start.5 = (bf16[128,512]{1,0:T(8,128)(2,1)S(1)}, bf16[128,512]{1,0:T(8,128)(2,1)S(1)}, u32[]{:S(2)}, u32[]{:S(2)}) collective-permute-start(bf16[128,512]{1,0:T(8,128)(2,1)S(1)} %get-tuple-element.25), channel_id=1, source_target_pairs={{0,2},{1,3},{2,4},{3,5},{4,6},{5,7},{6,0},{7,1},{8,10},{9,11},{10,... | collective-permute-start | bytes 393224 | tf_op jit(solution)/shard_map/ppermute | solution.py:276
  33.8 13.4 %collective-permute-start.6 = (bf16[128,512]{1,0:T(8,128)(2,1)S(1)}, bf16[128,512]{1,0:T(8,128)(2,1)S(1)}, u32[]{:S(2)}, u32[]{:S(2)}) collective-permute-start(bf16[128,512]{1,0:T(8,128)(2,1)S(1)} %get-tuple-element.25), channel_id=1, source_target_pairs={{0,3},{1,4},{2,5},{3,6},{4,7},{5,0},{6,1},{7,2},{8,11},{9,12},{10,... | collective-permute-start | bytes 393224 | tf_op jit(solution)/shard_map/ppermute | solution.py:276
  39.6 15.6 %copy-start = (bf16[128,512]{1,0:T(8,128)(2,1)}, bf16[128,512]{1,0:T(8,128)(2,1)S(1)}, u32[]{:S(2)}) copy-start(bf16[128,512]{1,0:T(8,128)(2,1)S(1)} %add_convert_fusion.1.refs_0_) | copy-start | bytes 393220
  39.6 8.1 %collective-permute-start.12 = (bf16[128,512]{1,0:T(8,128)(2,1)S(1)}, bf16[128,512]{1,0:T(8,128)(2,1)S(1)}, u32[]{:S(2)}, u32[]{:S(2)}) collective-permute-start(bf16[128,512]{1,0:T(8,128)(2,1)S(1)} %add_convert_fusion.1.refs_0_), channel_id=1, source_target_pairs={{0,129},{1,128},{2,131},{3,130},{4,133},{5,132},{6,135},{7,134},{8... | collective-permute-start | bytes 393224 | tf_op jit(solution)/shard_map/ppermute | solution.py:272
  41.8 6.1 %collective-permute-start.13 = (bf16[128,512]{1,0:T(8,128)(2,1)S(1)}, bf16[128,512]{1,0:T(8,128)(2,1)S(1)}, u32[]{:S(2)}, u32[]{:S(2)}) collective-permute-start(bf16[128,512]{1,0:T(8,128)(2,1)S(1)} %add_convert_fusion.1.refs_0_), channel_id=1, source_target_pairs={{0,16},{1,17},{2,18},{3,19},{4,20},{5,21},{6,22},{7,23},{8,24},{9,... | collective-permute-start | bytes 393224 | tf_op jit(solution)/shard_map/ppermute | solution.py:272
  43.3 11.9 %copy-start.1 = (bf16[128,512]{1,0:T(8,128)(2,1)}, bf16[128,512]{1,0:T(8,128)(2,1)S(1)}, u32[]{:S(2)}) copy-start(bf16[128,512]{1,0:T(8,128)(2,1)S(1)} %collective-permute-done.4.refs_8_.v1) | copy-start | bytes 393220
  43.3 6.7 %collective-permute-start.14 = (bf16[128,512]{1,0:T(8,128)(2,1)S(1)}, bf16[128,512]{1,0:T(8,128)(2,1)S(1)}, u32[]{:S(2)}, u32[]{:S(2)}) collective-permute-start(bf16[128,512]{1,0:T(8,128)(2,1)S(1)} %add_convert_fusion.1.refs_0_), channel_id=1, source_target_pairs={{0,145},{1,144},{2,147},{3,146},{4,149},{5,148},{6,151},{7,150},{8... | collective-permute-start | bytes 393224 | tf_op jit(solution)/shard_map/ppermute | solution.py:272
  43.9 11.3 %copy-start.2 = (bf16[128,512]{1,0:T(8,128)(2,1)}, bf16[128,512]{1,0:T(8,128)(2,1)S(1)}, u32[]{:S(2)}) copy-start(bf16[128,512]{1,0:T(8,128)(2,1)S(1)} %collective-permute-done.5.refs_9_.v2) | copy-start | bytes 393220
  43.9 6.5 %collective-permute-start.7 = (bf16[128,512]{1,0:T(8,128)(2,1)S(1)}, bf16[128,512]{1,0:T(8,128)(2,1)S(1)}, u32[]{:S(2)}, u32[]{:S(2)}) collective-permute-start(bf16[128,512]{1,0:T(8,128)(2,1)S(1)} %get-tuple-element.25), channel_id=1, source_target_pairs={{0,4},{1,5},{2,6},{3,7},{4,0},{5,1},{6,2},{7,3},{8,12},{9,13},{10,... | collective-permute-start | bytes 393224 | tf_op jit(solution)/shard_map/ppermute | solution.py:276
  47.2 8.0 %copy-start.3 = (bf16[128,512]{1,0:T(8,128)(2,1)}, bf16[128,512]{1,0:T(8,128)(2,1)S(1)}, u32[]{:S(2)}) copy-start(bf16[128,512]{1,0:T(8,128)(2,1)S(1)} %collective-permute-done.6.refs_10_.v3) | copy-start | bytes 393220
  47.2 3.2 %collective-permute-start.15 = (bf16[128,512]{1,0:T(8,128)(2,1)S(1)}, bf16[128,512]{1,0:T(8,128)(2,1)S(1)}, u32[]{:S(2)}, u32[]{:S(2)}) collective-permute-start(bf16[128,512]{1,0:T(8,128)(2,1)S(1)} %add_convert_fusion.1.refs_0_), channel_id=1, source_target_pairs={{0,8},{1,9},{2,10},{3,11},{4,12},{5,13},{6,14},{7,15},{8,0},{9,1},... | collective-permute-start | bytes 393224 | tf_op jit(solution)/shard_map/ppermute | solution.py:272
  47.8 2.6 %collective-permute-start.16 = (bf16[128,512]{1,0:T(8,128)(2,1)S(1)}, bf16[128,512]{1,0:T(8,128)(2,1)S(1)}, u32[]{:S(2)}, u32[]{:S(2)}) collective-permute-start(bf16[128,512]{1,0:T(8,128)(2,1)S(1)} %collective-permute-done.12.refs_1_), channel_id=1, source_target_pairs={{0,8},{1,9},{2,10},{3,11},{4,12},{5,13},{6,14},{7,15},{8,0},{9,1},... | collective-permute-start | bytes 393224 | tf_op jit(solution)/shard_map/ppermute | solution.py:272
  47.9 2.5 %collective-permute-start.17 = (bf16[128,512]{1,0:T(8,128)(2,1)S(1)}, bf16[128,512]{1,0:T(8,128)(2,1)S(1)}, u32[]{:S(2)}, u32[]{:S(2)}) collective-permute-start(bf16[128,512]{1,0:T(8,128)(2,1)S(1)} %collective-permute-done.13.refs_2_), channel_id=1, source_target_pairs={{0,8},{1,9},{2,10},{3,11},{4,12},{5,13},{6,14},{7,15},{8,0},{9,1},... | collective-permute-start | bytes 393224 | tf_op jit(solution)/shard_map/ppermute | solution.py:272
  50.0 1.3 %collective-permute-start.18 = (bf16[128,512]{1,0:T(8,128)(2,1)S(1)}, bf16[128,512]{1,0:T(8,128)(2,1)S(1)}, u32[]{:S(2)}, u32[]{:S(2)}) collective-permute-start(bf16[128,512]{1,0:T(8,128)(2,1)S(1)} %collective-permute-done.14.refs_3_), channel_id=1, source_target_pairs={{0,8},{1,9},{2,10},{3,11},{4,12},{5,13},{6,14},{7,15},{8,0},{9,1},... | collective-permute-start | bytes 393224 | tf_op jit(solution)/shard_map/ppermute | solution.py:272
  55.3 24.5 %all-to-all-start.1 = ((bf16[8,128,512]{2,1,0:T(8,128)(2,1)}), bf16[8,128,512]{2,1,0:T(8,128)(2,1)S(1)}, u32[]{:S(2)}, u32[]{:S(2)}) async-start(bf16[8,128,512]{2,1,0:T(8,128)(2,1)} %get-tuple-element.41), calls=%async_computation.1 | async-start | bytes 2097152 | tf_op jit(solution)/shard_map/all_to_all | solution.py:306
  72.0 13.7 %collective-permute-start.22 = (bf16[128,512]{1,0:T(8,128)(2,1)}, bf16[128,512]{1,0:T(8,128)(2,1)S(1)}, u32[]{:S(2)}, u32[]{:S(2)}) collective-permute-start(bf16[128,512]{1,0:T(8,128)(2,1)} %get-tuple-element.39), channel_id=1, source_target_pairs={{0,4},{1,5},{2,6},{3,7},{4,0},{5,1},{6,2},{7,3},{8,12},{9,13},{10,... | collective-permute-start | bytes 393224 | tf_op jit(solution)/shard_map/ppermute | solution.py:276
  75.1 11.9 %collective-permute-start.21 = (bf16[128,512]{1,0:T(8,128)(2,1)}, bf16[128,512]{1,0:T(8,128)(2,1)S(1)}, u32[]{:S(2)}, u32[]{:S(2)}) collective-permute-start(bf16[128,512]{1,0:T(8,128)(2,1)} %get-tuple-element.38), channel_id=1, source_target_pairs={{0,5},{1,6},{2,7},{3,0},{4,1},{5,2},{6,3},{7,4},{8,13},{9,14},{10,... | collective-permute-start | bytes 393224 | tf_op jit(solution)/shard_map/ppermute | solution.py:276
  76.2 13.3 %collective-permute-start.20 = (bf16[128,512]{1,0:T(8,128)(2,1)}, bf16[128,512]{1,0:T(8,128)(2,1)S(1)}, u32[]{:S(2)}, u32[]{:S(2)}) collective-permute-start(bf16[128,512]{1,0:T(8,128)(2,1)} %get-tuple-element.37), channel_id=1, source_target_pairs={{0,6},{1,7},{2,0},{3,1},{4,2},{5,3},{6,4},{7,5},{8,14},{9,15},{10,... | collective-permute-start | bytes 393224 | tf_op jit(solution)/shard_map/ppermute | solution.py:276
  76.2 13.3 %collective-permute-start.19 = (bf16[128,512]{1,0:T(8,128)(2,1)}, bf16[128,512]{1,0:T(8,128)(2,1)S(1)}, u32[]{:S(2)}, u32[]{:S(2)}) collective-permute-start(bf16[128,512]{1,0:T(8,128)(2,1)} %get-tuple-element.36), channel_id=1, source_target_pairs={{0,7},{1,0},{2,1},{3,2},{4,3},{5,4},{6,5},{7,6},{8,15},{9,8},{10,9... | collective-permute-start | bytes 393224 | tf_op jit(solution)/shard_map/ppermute | solution.py:276
  80.0 11.2 %collective-permute-start.25 = (bf16[32,512]{1,0:T(8,128)(2,1)S(1)}, bf16[32,512]{1,0:T(8,128)(2,1)S(1)}, u32[]{:S(2)}, u32[]{:S(2)}) collective-permute-start(bf16[32,512]{1,0:T(8,128)(2,1)S(1)} %get-tuple-element.45), channel_id=1, source_target_pairs={{0,96},{1,97},{2,98},{3,99},{4,100},{5,101},{6,102},{7,103},{8,104... | collective-permute-start | bytes 98312 | tf_op jit(solution)/shard_map/ppermute | solution.py:272
  85.7 7.8 %collective-permute-start.24 = (bf16[32,512]{1,0:T(8,128)(2,1)S(1)}, bf16[32,512]{1,0:T(8,128)(2,1)S(1)}, u32[]{:S(2)}, u32[]{:S(2)}) collective-permute-start(bf16[32,512]{1,0:T(8,128)(2,1)S(1)} %get-tuple-element.44), channel_id=1, source_target_pairs={{0,64},{1,65},{2,66},{3,67},{4,68},{5,69},{6,70},{7,71},{8,72},{9,... | collective-permute-start | bytes 98312 | tf_op jit(solution)/shard_map/ppermute | solution.py:272
  87.0 6.6 %collective-permute-start.23 = (bf16[32,512]{1,0:T(8,128)(2,1)S(1)}, bf16[32,512]{1,0:T(8,128)(2,1)S(1)}, u32[]{:S(2)}, u32[]{:S(2)}) collective-permute-start(bf16[32,512]{1,0:T(8,128)(2,1)S(1)} %get-tuple-element.43), channel_id=1, source_target_pairs={{0,32},{1,33},{2,34},{3,35},{4,36},{5,37},{6,38},{7,39},{8,40},{9,... | collective-permute-start | bytes 98312 | tf_op jit(solution)/shard_map/ppermute | solution.py:272
  (12 other events, 49.4 us)
